TPU v7x, 256 devices: a whole 4x4x8 slice. The times are simulated.
256 devices in a mesh: tile: 64 (over z_hi, y, x), lev: 4 (over z_lo, core).
Axes of the slice: x: 4, y: 4, z: 8 (z_hi: 4, z_lo: 2; z = z_hi * 2 + z_lo), core: 2. Of those that a mesh axis runs over, the one named last changes fastest.
Arguments:
- control: float32 [20, 128, 768, 128], P(None, 'lev', 'tile'), may hold values from -6 to 6
- ensemble: bfloat16 [20, 128, 768, 128], P(None, 'lev', 'tile'), may hold values from -6 to 6
- coupling_x: float32 [768, 128], P('tile'), may hold values from 0.16 to 0.245
- coupling_y: float32 [128], replicated, may hold values from 0.16 to 0.245
- vertical_loc: bfloat16 [128, 128], replicated
- obs_cells: int32 [4096, 32], P('tile'), may hold values from 0 to 1535, as said below
- obs_counts: int32 [4096], P('tile'), may hold values from 8 to 32, as said below
- obs_values: float32 [4096, 32, 128], P('tile', None, 'lev'), may hold values from -6 to 6
Outputs:
- increment: float32 [128, 768, 128], P('lev', 'tile')
- gradient: float32 [20, 128, 768, 128], P(None, 'lev', 'tile')
Inputs may be any that keep to these rules, and one draw needn't show every extreme that they name: `obs_cells`: each row holds owner-local cells of one owner, in rising order. The live slots of a row are its first obs_counts entries; in every draw some owners receive 32 live slots from every device.
All inputs are finite; a program needn't handle non-finite values.
Results may differ from a plain program's by a relative error of at most 0.0029.
Values may be sent and summed in bfloat16 or wider, within the bound.
No kernel may reach another device: no remote copies, remote signals or barrier semaphores. Data moves between devices by JAX's collectives and lax.ppermute only.
A program may use at most 64 MiB of HBM per device.

v0:
```python
import jax
import jax.numpy as jnp
from jax import lax
from jax.sharding import PartitionSpec as P

STEPS = 4


def with_halo(shard, sides, width):
    for axis, dim in sides:
        size, length = (lax.axis_size(axis), shard.shape[dim])
        up = [(i, (i + 1) % size) for i in range(size)]
        down = [(j, i) for i, j in up]
        last = lax.slice_in_dim(shard, length - width, length, axis=dim)
        first = lax.slice_in_dim(shard, 0, width, axis=dim)
        before = lax.ppermute(last, axis, up)
        after = lax.ppermute(first, axis, down)
        shard = jnp.concatenate([before, shard, after], axis=dim)
    return shard


def shifted(block, axis, distance):
    devices = range(lax.axis_size(axis))
    route = [((i - distance) % len(devices), i) for i in devices]
    return lax.ppermute(block, axis, route)


def sweep_across(middle, coupling_y):
    differ = middle[..., 1:] - middle[..., :-1]
    fluxes = coupling_y[:-1] * differ
    zeros_col = jnp.zeros_like(middle[..., :1])
    return jnp.concatenate([fluxes, zeros_col], -1) - jnp.concatenate([zeros_col, fluxes], -1)


def diffuse_step(padded, window, coupling_y):
    middle = padded[..., 1:-1, :]
    along = window[1:-1] * (padded[..., 2:, :] - middle) - window[:-2] * (
        middle - padded[..., :-2, :]
    )
    return middle + along + sweep_across(middle, coupling_y)


def diffuse(field, coupling_ext, coupling_y):
    for step in range(STEPS):
        padded = with_halo(field, (("tile", 2),), 1)
        field = diffuse_step(padded, coupling_ext, coupling_y)
    return field


def localize(field, vertical_loc, transposed):
    if transposed:
        form = "lk,mlxy->mkxy"
    else:
        form = "kl,mlxy->mkxy"
    mixed = jnp.einsum(
        form,
        vertical_loc,
        lax.all_to_all(field, "lev", split_axis=0, concat_axis=1, tiled=True),
        preferred_element_type=jnp.float32,
    )
    return lax.all_to_all(mixed, "lev", split_axis=1, concat_axis=0, tiled=True)


def local(
    control, ensemble, coupling_x, coupling_y, vertical_loc, obs_cells, obs_counts, obs_values
):
    block = control.shape[1]
    columns = control.shape[2]
    across = control.shape[3]
    before_row = shifted(coupling_x[-1:], "tile", 1)
    coupling_ext = jnp.concatenate([before_row, coupling_x, jnp.zeros_like(before_row)], 0)
    slot_index = lax.broadcasted_iota(jnp.int32, obs_cells.shape, 1)
    live = slot_index < obs_counts[:, None]
    masked = jnp.where(live[..., None], obs_values, jnp.float32(0.0))
    got_cells, got_values = (
        lax.all_to_all(obs_cells, "tile", split_axis=0, concat_axis=0, tiled=True),
        lax.all_to_all(masked, "tile", split_axis=0, concat_axis=0, tiled=True),
    )
    smooth = diffuse(control, coupling_ext, coupling_y).astype(jnp.bfloat16)
    localized = localize(smooth, vertical_loc, False)
    increment = jnp.sum(ensemble.astype(jnp.float32) * localized, axis=0)
    summed = jax.ops.segment_sum(
        got_values.reshape(-1, block), got_cells.reshape(-1), num_segments=columns * across
    )
    obs_grad = summed.T.reshape(block, columns, across)
    weighted = (ensemble.astype(jnp.float32) * obs_grad[None]).astype(jnp.bfloat16)
    returned = localize(weighted, vertical_loc, True)
    gradient = control + diffuse(returned, coupling_ext, coupling_y)
    return (increment, gradient)


def solution(mesh):
    placed = (
        P(None, "lev", "tile", None),
        P(None, "lev", "tile", None),
        P("tile", None),
        P(),
        P(),
        P("tile", None),
        P("tile"),
        P("tile", None, "lev"),
    )
    return jax.shard_map(
        local,
        mesh=mesh,
        in_specs=placed,
        out_specs=(P("lev", "tile", None), P(None, "lev", "tile", None)),
        check_vma=False,
    )
```

profile of v0, /device:TPU:1, one launch (start us, length us, event | category | flops | bytes accessed | tf_op | source)
XLA Modules:
  0.0 461.3 jit_solution(1625512377437936179)
XLA Ops:
  2.1 15.1 %all-to-all-start.2 = ((s32[64,1,32]{2,1,0:T(1,128)}), s32[64,1,32]{2,1,0:T(1,128)S(1)}, u32[]{:S(2)}, u32[]{:S(2)}) async-start(s32[64,1,32]{2,1,0:T(1,128)} %bitcast.10), calls=%async_computation.2 | async-start | bytes 65536 | tf_op jit(solution)/shard_map/all_to_all | solution.py:76
  27.8 8.0 %all-to-all-start.3 = ((f32[64,1,1024]{2,1,0:T(1,128)}), f32[64,1,1024]{2,1,0:T(1,128)S(1)}, u32[]{:S(2)}, u32[]{:S(2)}) async-start(f32[64,1,1024]{2,1,0:T(1,128)} %reshape.55), calls=%async_computation.3 | async-start | bytes 524288 | tf_op jit(solution)/shard_map/all_to_all | solution.py:77
  37.1 11.4 %all-to-all-done.3 = f32[64,1,1024]{2,1,0:T(1,128)S(1)} async-done(((f32[64,1,1024]{2,1,0:T(1,128)}), f32[64,1,1024]{2,1,0:T(1,128)S(1)}, u32[]{:S(2)}, u32[]{:S(2)}) %all-to-all-start.3) | async-done | bytes 262176 | tf_op jit(solution)/shard_map/all_to_all | solution.py:77
  51.6 12.0 %scatter_custom_fusion = f32[1536,32]{1,0:T(8,128)S(1)} fusion(s32[2048]{0:T(1024)S(1)} %reshape.36, f32[2048,32]{1,0:T(8,128)} %bitcast.45, f32[]{:T(128)} %constant.1.clone.1), kind=kCustom, calls=%fused_computation.97 | custom fusion | flops 65536 | bytes 197120 | tf_op jit(solution)/shard_map/scatter-add | solution.py:82
  64.4 28.8 %all_to_all.86 = bf16[20,32,12,128]{3,1,2,0:T(8,128)(2,1)S(1)} all-to-all(bf16[20,32,12,128]{3,1,2,0:T(8,128)(2,1)S(1)} %fusion.1), channel_id=1, replica_groups=mesh['tile'=64,'lev'=4] {'lev'}, dimensions={0} | all-to-all | bytes 3932160 | tf_op jit(solution)/shard_map/all_to_all | solution.py:58
  96.4 6.1 %copy.47 = f32[5,128,12,128]{3,2,0,1:T(8,128)} copy(f32[5,128,12,128]{1,3,2,0:T(8,128)} %convolution_bitcast_fusion) | data formatting | bytes 7864320 | tf_op jit(solution)/shard_map/lk,mlxy->mkxy/transpose | solution.py:55
  102.5 6.2 %all-to-all-start.5 = ((f32[5,128,12,128]{3,2,0,1:T(8,128)}), f32[5,128,12,128]{3,2,0,1:T(8,128)}, u32[]{:S(2)}, u32[]{:S(2)}) async-start(f32[5,128,12,128]{3,2,0,1:T(8,128)} %copy.47), calls=%async_computation.5 | async-start | bytes 10485760 | tf_op jit(solution)/shard_map/all_to_all | solution.py:61
  110.7 7.6 %collective-permute-start = (f32[20,32,1,128]{3,1,2,0:T(8,128)}, f32[20,32,1,128]{3,1,2,0:T(8,128)}, u32[]{:S(2)}, u32[]{:S(2)}) collective-permute-start(f32[20,32,1,128]{3,1,2,0:T(8,128)} %get-tuple-element.18), channel_id=1, source_target_pairs={{4,0},{8,4},{12,8},{16,12},{20,16},{24,20},{28,24},{32,28},{36,32}... | collective-permute-start | bytes 983048 | tf_op jit(solution)/shard_map/ppermute | solution.py:17
  118.5 56.2 %collective-permute-done.1 = f32[1,128]{1,0:T(1,128)S(1)} collective-permute-done((f32[1,128]{1,0:T(1,128)S(1)}, f32[1,128]{1,0:T(1,128)S(1)}, u32[]{:S(2)}, u32[]{:S(2)}) %collective-permute-start.1) | collective-permute-done | bytes 544 | tf_op jit(solution)/shard_map/ppermute | solution.py:25
  181.3 10.1 %collective-permute-done.9 = f32[20,32,1,128]{3,1,2,0:T(8,128)S(1)} collective-permute-done((f32[20,32,1,128]{3,1,2,0:T(8,128)S(1)}, f32[20,32,1,128]{3,1,2,0:T(8,128)S(1)}, u32[]{:S(2)}, u32[]{:S(2)}) %collective-permute-start.9) | collective-permute-done | bytes 327712 | tf_op jit(solution)/shard_map/ppermute | solution.py:17
  196.0 6.7 %collective-permute-start.11 = (f32[20,32,1,128]{3,1,2,0:T(8,128)S(1)}, f32[20,32,1,128]{3,1,2,0:T(8,128)S(1)}, u32[]{:S(2)}, u32[]{:S(2)}) collective-permute-start(f32[20,32,1,128]{3,1,2,0:T(8,128)S(1)} %get-tuple-element.8), channel_id=1, source_target_pairs={{4,0},{8,4},{12,8},{16,12},{20,16},{24,20},{28,24},{32,28},{36,32}... | collective-permute-start | bytes 983048 | tf_op jit(solution)/shard_map/ppermute | solution.py:17
  203.7 10.8 %collective-permute-done.11 = f32[20,32,1,128]{3,1,2,0:T(8,128)S(1)} collective-permute-done((f32[20,32,1,128]{3,1,2,0:T(8,128)S(1)}, f32[20,32,1,128]{3,1,2,0:T(8,128)S(1)}, u32[]{:S(2)}, u32[]{:S(2)}) %collective-permute-start.11) | collective-permute-done | bytes 327712 | tf_op jit(solution)/shard_map/ppermute | solution.py:17
  219.6 6.2 %collective-permute-start.13 = (f32[20,32,1,128]{3,1,2,0:T(8,128)S(1)}, f32[20,32,1,128]{3,1,2,0:T(8,128)S(1)}, u32[]{:S(2)}, u32[]{:S(2)}) collective-permute-start(f32[20,32,1,128]{3,1,2,0:T(8,128)S(1)} %get-tuple-element.6), channel_id=1, source_target_pairs={{4,0},{8,4},{12,8},{16,12},{20,16},{24,20},{28,24},{32,28},{36,32}... | collective-permute-start | bytes 983048 | tf_op jit(solution)/shard_map/ppermute | solution.py:17
  229.8 15.2 %collective-permute-done.14 = f32[20,32,1,128]{3,1,2,0:T(8,128)S(1)} collective-permute-done((f32[20,32,1,128]{3,1,2,0:T(8,128)S(1)}, f32[20,32,1,128]{3,1,2,0:T(8,128)S(1)}, u32[]{:S(2)}, u32[]{:S(2)}) %collective-permute-start.14) | collective-permute-done | bytes 327712 | tf_op jit(solution)/shard_map/ppermute | solution.py:16
  254.3 6.5 %collective-permute-done.16 = f32[20,32,1,128]{3,1,2,0:T(8,128)S(1)} collective-permute-done((f32[20,32,1,128]{3,1,2,0:T(8,128)S(1)}, f32[20,32,1,128]{3,1,2,0:T(8,128)S(1)}, u32[]{:S(2)}, u32[]{:S(2)}) %collective-permute-start.16) | collective-permute-done | bytes 327712 | tf_op jit(solution)/shard_map/ppermute | solution.py:16
  261.6 15.2 %fusion.8 = (f32[20,32,12,128]{3,1,2,0:T(8,128)}, f32[20,32,12,128]{3,1,2,0:T(8,128)S(1)}) fusion(f32[20,32,12,128]{3,1,2,0:T(8,128)} %param.8, f32[20,32,12,128]{3,1,2,0:T(8,128)S(1)} %fusion.16, f32[20,32,1,128]{3,1,2,0:T(8,128)} %copy-done.6, f32[20,32,1,128]{3,1,2,0:T(8,128)} %copy-done.5, f32[20,32,12,127]{3,1,2,0:T(8,128)} %get-tuple-element.20, ...), kind=kLoop, calls=%fused_computation.13 | loop fusion | flops 20643840 | bytes 24854528 | tf_op jit(solution)/shard_map/add | solution.py:88
  282.9 6.7 %collective-permute-done.4 = f32[20,32,1,128]{3,1,2,0:T(8,128)S(1)} collective-permute-done((f32[20,32,1,128]{3,1,2,0:T(8,128)S(1)}, f32[20,32,1,128]{3,1,2,0:T(8,128)S(1)}, u32[]{:S(2)}, u32[]{:S(2)}) %collective-permute-start.4) | collective-permute-done | bytes 327712 | tf_op jit(solution)/shard_map/ppermute | solution.py:16
  294.7 5.6 %collective-permute-done.5 = f32[20,32,1,128]{3,1,2,0:T(8,128)S(1)} collective-permute-done((f32[20,32,1,128]{3,1,2,0:T(8,128)S(1)}, f32[20,32,1,128]{3,1,2,0:T(8,128)S(1)}, u32[]{:S(2)}, u32[]{:S(2)}) %collective-permute-start.5) | collective-permute-done | bytes 327712 | tf_op jit(solution)/shard_map/ppermute | solution.py:17
  300.2 12.0 %collective-permute-done.6 = f32[20,32,1,128]{3,1,2,0:T(8,128)S(1)} collective-permute-done((f32[20,32,1,128]{3,1,2,0:T(8,128)S(1)}, f32[20,32,1,128]{3,1,2,0:T(8,128)S(1)}, u32[]{:S(2)}, u32[]{:S(2)}) %collective-permute-start.6) | collective-permute-done | bytes 327712 | tf_op jit(solution)/shard_map/ppermute | solution.py:16
  317.4 11.7 %collective-permute-done.7 = f32[20,32,1,128]{3,1,2,0:T(8,128)S(1)} collective-permute-done((f32[20,32,1,128]{3,1,2,0:T(8,128)S(1)}, f32[20,32,1,128]{3,1,2,0:T(8,128)S(1)}, u32[]{:S(2)}, u32[]{:S(2)}) %collective-permute-start.7) | collective-permute-done | bytes 327712 | tf_op jit(solution)/shard_map/ppermute | solution.py:17
  329.0 5.9 %collective-permute-done.8 = f32[20,32,1,128]{3,1,2,0:T(8,128)S(1)} collective-permute-done((f32[20,32,1,128]{3,1,2,0:T(8,128)S(1)}, f32[20,32,1,128]{3,1,2,0:T(8,128)S(1)}, u32[]{:S(2)}, u32[]{:S(2)}) %collective-permute-start.8) | collective-permute-done | bytes 327712 | tf_op jit(solution)/shard_map/ppermute | solution.py:16
  337.4 48.1 %all_to_all.87 = bf16[20,32,12,128]{3,1,2,0:T(8,128)(2,1)S(1)} all-to-all(bf16[20,32,12,128]{3,1,2,0:T(8,128)(2,1)S(1)} %fusion.41), channel_id=1, replica_groups=mesh['tile'=64,'lev'=4] {'lev'}, dimensions={0} | all-to-all | bytes 3932160 | tf_op jit(solution)/shard_map/all_to_all | solution.py:58
  388.8 6.0 %copy.36 = f32[5,128,12,128]{3,2,0,1:T(8,128)} copy(f32[5,128,12,128]{1,3,2,0:T(8,128)} %convolution_bitcast_fusion.1) | data formatting | bytes 7864320 | tf_op jit(solution)/shard_map/kl,mlxy->mkxy/transpose | solution.py:55
  394.7 63.3 %all_to_all.88 = f32[5,128,12,128]{3,2,0,1:T(8,128)S(1)} all-to-all(f32[5,128,12,128]{3,2,0,1:T(8,128)} %copy.36), channel_id=1, replica_groups=mesh['tile'=64,'lev'=4] {'lev'}, dimensions={1} | all-to-all | bytes 7864320 | tf_op jit(solution)/shard_map/all_to_all | solution.py:61
  (82 shorter events, 78.7 us)
Async XLA Ops:
  0.6 93.2 %copy-start = (bf16[128,128]{1,0:T(8,128)(2,1)S(1)}, bf16[128,128]{1,0:T(8,128)(2,1)}, u32[]{:S(2)}) copy-start(bf16[128,128]{1,0:T(8,128)(2,1)} %param.12) | copy-start | bytes 98308
  2.1 25.8 %all-to-all-start.2 = ((s32[64,1,32]{2,1,0:T(1,128)}), s32[64,1,32]{2,1,0:T(1,128)S(1)}, u32[]{:S(2)}, u32[]{:S(2)}) async-start(s32[64,1,32]{2,1,0:T(1,128)} %bitcast.10), calls=%async_computation.2 | async-start | bytes 65536 | tf_op jit(solution)/shard_map/all_to_all | solution.py:76
  20.7 43.1 %copy-start.2 = (bf16[20,32,12,128]{3,1,2,0:T(8,128)(2,1)S(1)}, bf16[20,32,12,128]{3,1,2,0:T(8,128)(2,1)}, u32[]{:S(2)}) copy-start(bf16[20,32,12,128]{3,1,2,0:T(8,128)(2,1)} %param.9) | copy-start | bytes 5898244
  27.8 20.7 %all-to-all-start.3 = ((f32[64,1,1024]{2,1,0:T(1,128)}), f32[64,1,1024]{2,1,0:T(1,128)S(1)}, u32[]{:S(2)}, u32[]{:S(2)}) async-start(f32[64,1,1024]{2,1,0:T(1,128)} %reshape.55), calls=%async_computation.3 | async-start | bytes 524288 | tf_op jit(solution)/shard_map/all_to_all | solution.py:77
  102.5 72.2 %all-to-all-start.5 = ((f32[5,128,12,128]{3,2,0,1:T(8,128)}), f32[5,128,12,128]{3,2,0,1:T(8,128)}, u32[]{:S(2)}, u32[]{:S(2)}) async-start(f32[5,128,12,128]{3,2,0,1:T(8,128)} %copy.47), calls=%async_computation.5 | async-start | bytes 10485760 | tf_op jit(solution)/shard_map/all_to_all | solution.py:61
  108.7 66.0 %collective-permute-start.1 = (f32[1,128]{1,0:T(1,128)S(1)}, f32[1,128]{1,0:T(1,128)S(1)}, u32[]{:S(2)}, u32[]{:S(2)}) collective-permute-start(f32[1,128]{1,0:T(1,128)S(1)} %slice.186), channel_id=1, source_target_pairs={{252,0},{0,4},{4,8},{8,12},{12,16},{16,20},{20,24},{24,28},{28,32}... | collective-permute-start | bytes 1544 | tf_op jit(solution)/shard_map/ppermute | solution.py:25
  110.7 143.5 %collective-permute-start = (f32[20,32,1,128]{3,1,2,0:T(8,128)}, f32[20,32,1,128]{3,1,2,0:T(8,128)}, u32[]{:S(2)}, u32[]{:S(2)}) collective-permute-start(f32[20,32,1,128]{3,1,2,0:T(8,128)} %get-tuple-element.18), channel_id=1, source_target_pairs={{4,0},{8,4},{12,8},{16,12},{20,16},{24,20},{28,24},{32,28},{36,32}... | collective-permute-start | bytes 983048 | tf_op jit(solution)/shard_map/ppermute | solution.py:17
  118.3 136.0 %collective-permute-start.2 = (f32[20,32,1,128]{3,1,2,0:T(8,128)S(1)}, f32[20,32,1,128]{3,1,2,0:T(8,128)}, u32[]{:S(2)}, u32[]{:S(2)}) collective-permute-start(f32[20,32,1,128]{3,1,2,0:T(8,128)S(1)} %get-tuple-element.19), channel_id=1, source_target_pairs={{0,4},{4,8},{8,12},{12,16},{16,20},{20,24},{24,28},{28,32},{32,36}... | collective-permute-start | bytes 983048 | tf_op jit(solution)/shard_map/ppermute | solution.py:16
  178.7 12.7 %collective-permute-start.9 = (f32[20,32,1,128]{3,1,2,0:T(8,128)S(1)}, f32[20,32,1,128]{3,1,2,0:T(8,128)S(1)}, u32[]{:S(2)}, u32[]{:S(2)}) collective-permute-start(f32[20,32,1,128]{3,1,2,0:T(8,128)S(1)} %get-tuple-element.10), channel_id=1, source_target_pairs={{4,0},{8,4},{12,8},{16,12},{20,16},{24,20},{28,24},{32,28},{36,32}... | collective-permute-start | bytes 983048 | tf_op jit(solution)/shard_map/ppermute | solution.py:17
  178.8 14.7 %collective-permute-start.10 = (f32[20,32,1,128]{3,1,2,0:T(8,128)S(1)}, f32[20,32,1,128]{3,1,2,0:T(8,128)S(1)}, u32[]{:S(2)}, u32[]{:S(2)}) collective-permute-start(f32[20,32,1,128]{3,1,2,0:T(8,128)S(1)} %get-tuple-element.11), channel_id=1, source_target_pairs={{0,4},{4,8},{8,12},{12,16},{16,20},{20,24},{24,28},{28,32},{32,36}... | collective-permute-start | bytes 983048 | tf_op jit(solution)/shard_map/ppermute | solution.py:16
  196.0 18.6 %collective-permute-start.11 = (f32[20,32,1,128]{3,1,2,0:T(8,128)S(1)}, f32[20,32,1,128]{3,1,2,0:T(8,128)S(1)}, u32[]{:S(2)}, u32[]{:S(2)}) collective-permute-start(f32[20,32,1,128]{3,1,2,0:T(8,128)S(1)} %get-tuple-element.8), channel_id=1, source_target_pairs={{4,0},{8,4},{12,8},{16,12},{20,16},{24,20},{28,24},{32,28},{36,32}... | collective-permute-start | bytes 983048 | tf_op jit(solution)/shard_map/ppermute | solution.py:17
  202.6 14.5 %collective-permute-start.12 = (f32[20,32,1,128]{3,1,2,0:T(8,128)S(1)}, f32[20,32,1,128]{3,1,2,0:T(8,128)S(1)}, u32[]{:S(2)}, u32[]{:S(2)}) collective-permute-start(f32[20,32,1,128]{3,1,2,0:T(8,128)S(1)} %get-tuple-element.9), channel_id=1, source_target_pairs={{0,4},{4,8},{8,12},{12,16},{16,20},{20,24},{24,28},{28,32},{32,36}... | collective-permute-start | bytes 983048 | tf_op jit(solution)/shard_map/ppermute | solution.py:16
  219.6 10.3 %collective-permute-start.13 = (f32[20,32,1,128]{3,1,2,0:T(8,128)S(1)}, f32[20,32,1,128]{3,1,2,0:T(8,128)S(1)}, u32[]{:S(2)}, u32[]{:S(2)}) collective-permute-start(f32[20,32,1,128]{3,1,2,0:T(8,128)S(1)} %get-tuple-element.6), channel_id=1, source_target_pairs={{4,0},{8,4},{12,8},{16,12},{20,16},{24,20},{28,24},{32,28},{36,32}... | collective-permute-start | bytes 983048 | tf_op jit(solution)/shard_map/ppermute | solution.py:17
  225.8 19.3 %collective-permute-start.14 = (f32[20,32,1,128]{3,1,2,0:T(8,128)S(1)}, f32[20,32,1,128]{3,1,2,0:T(8,128)S(1)}, u32[]{:S(2)}, u32[]{:S(2)}) collective-permute-start(f32[20,32,1,128]{3,1,2,0:T(8,128)S(1)} %get-tuple-element.7), channel_id=1, source_target_pairs={{0,4},{4,8},{8,12},{12,16},{16,20},{20,24},{24,28},{28,32},{32,36}... | collective-permute-start | bytes 983048 | tf_op jit(solution)/shard_map/ppermute | solution.py:16
  227.1 22.0 %copy-start.1 = (f32[20,32,12,128]{3,1,2,0:T(8,128)S(1)}, f32[20,32,12,128]{3,1,2,0:T(8,128)}, u32[]{:S(2)}) copy-start(f32[20,32,12,128]{3,1,2,0:T(8,128)} %param.8) | copy-start | bytes 11796484
  247.5 6.7 %collective-permute-start.15 = (f32[20,32,1,128]{3,1,2,0:T(8,128)S(1)}, f32[20,32,1,128]{3,1,2,0:T(8,128)S(1)}, u32[]{:S(2)}, u32[]{:S(2)}) collective-permute-start(f32[20,32,1,128]{3,1,2,0:T(8,128)S(1)} %get-tuple-element.4), channel_id=1, source_target_pairs={{4,0},{8,4},{12,8},{16,12},{20,16},{24,20},{28,24},{32,28},{36,32}... | collective-permute-start | bytes 983048 | tf_op jit(solution)/shard_map/ppermute | solution.py:17
  247.6 13.2 %collective-permute-start.16 = (f32[20,32,1,128]{3,1,2,0:T(8,128)S(1)}, f32[20,32,1,128]{3,1,2,0:T(8,128)S(1)}, u32[]{:S(2)}, u32[]{:S(2)}) collective-permute-start(f32[20,32,1,128]{3,1,2,0:T(8,128)S(1)} %get-tuple-element.5), channel_id=1, source_target_pairs={{0,4},{4,8},{8,12},{12,16},{16,20},{20,24},{24,28},{28,32},{32,36}... | collective-permute-start | bytes 983048 | tf_op jit(solution)/shard_map/ppermute | solution.py:16
  254.3 6.5 %copy-start.5 = (f32[20,32,1,128]{3,1,2,0:T(8,128)}, f32[20,32,1,128]{3,1,2,0:T(8,128)S(1)}, u32[]{:S(2)}) copy-start(f32[20,32,1,128]{3,1,2,0:T(8,128)S(1)} %collective-permute-done.15) | copy-start | bytes 983044
  276.9 6.0 %collective-permute-start.3 = (f32[20,32,1,128]{3,1,2,0:T(8,128)S(1)}, f32[20,32,1,128]{3,1,2,0:T(8,128)S(1)}, u32[]{:S(2)}, u32[]{:S(2)}) collective-permute-start(f32[20,32,1,128]{3,1,2,0:T(8,128)S(1)} %get-tuple-element.16), channel_id=1, source_target_pairs={{4,0},{8,4},{12,8},{16,12},{20,16},{24,20},{28,24},{32,28},{36,32}... | collective-permute-start | bytes 983048 | tf_op jit(solution)/shard_map/ppermute | solution.py:17
  277.0 12.6 %collective-permute-start.4 = (f32[20,32,1,128]{3,1,2,0:T(8,128)S(1)}, f32[20,32,1,128]{3,1,2,0:T(8,128)S(1)}, u32[]{:S(2)}, u32[]{:S(2)}) collective-permute-start(f32[20,32,1,128]{3,1,2,0:T(8,128)S(1)} %get-tuple-element.17), channel_id=1, source_target_pairs={{0,4},{4,8},{8,12},{12,16},{16,20},{20,24},{24,28},{28,32},{32,36}... | collective-permute-start | bytes 983048 | tf_op jit(solution)/shard_map/ppermute | solution.py:16
  292.0 8.2 %collective-permute-start.5 = (f32[20,32,1,128]{3,1,2,0:T(8,128)S(1)}, f32[20,32,1,128]{3,1,2,0:T(8,128)S(1)}, u32[]{:S(2)}, u32[]{:S(2)}) collective-permute-start(f32[20,32,1,128]{3,1,2,0:T(8,128)S(1)} %get-tuple-element.14), channel_id=1, source_target_pairs={{4,0},{8,4},{12,8},{16,12},{20,16},{24,20},{28,24},{32,28},{36,32}... | collective-permute-start | bytes 983048 | tf_op jit(solution)/shard_map/ppermute | solution.py:17
  292.1 20.1 %collective-permute-start.6 = (f32[20,32,1,128]{3,1,2,0:T(8,128)S(1)}, f32[20,32,1,128]{3,1,2,0:T(8,128)S(1)}, u32[]{:S(2)}, u32[]{:S(2)}) collective-permute-start(f32[20,32,1,128]{3,1,2,0:T(8,128)S(1)} %get-tuple-element.15), channel_id=1, source_target_pairs={{0,4},{4,8},{8,12},{12,16},{16,20},{20,24},{24,28},{28,32},{32,36}... | collective-permute-start | bytes 983048 | tf_op jit(solution)/shard_map/ppermute | solution.py:16
  314.7 14.3 %collective-permute-start.7 = (f32[20,32,1,128]{3,1,2,0:T(8,128)S(1)}, f32[20,32,1,128]{3,1,2,0:T(8,128)S(1)}, u32[]{:S(2)}, u32[]{:S(2)}) collective-permute-start(f32[20,32,1,128]{3,1,2,0:T(8,128)S(1)} %get-tuple-element.12), channel_id=1, source_target_pairs={{4,0},{8,4},{12,8},{16,12},{20,16},{24,20},{28,24},{32,28},{36,32}... | collective-permute-start | bytes 983048 | tf_op jit(solution)/shard_map/ppermute | solution.py:17
  314.8 20.1 %collective-permute-start.8 = (f32[20,32,1,128]{3,1,2,0:T(8,128)S(1)}, f32[20,32,1,128]{3,1,2,0:T(8,128)S(1)}, u32[]{:S(2)}, u32[]{:S(2)}) collective-permute-start(f32[20,32,1,128]{3,1,2,0:T(8,128)S(1)} %get-tuple-element.13), channel_id=1, source_target_pairs={{0,4},{4,8},{8,12},{12,16},{16,20},{20,24},{24,28},{28,32},{32,36}... | collective-permute-start | bytes 983048 | tf_op jit(solution)/shard_map/ppermute | solution.py:16
  (4 other events, 14.0 us)
where the time goes:
time: 470 us; the launch traced here: 461 us
  waiting for transfers between devices  167 us (36%)
  blocking collectives  140 us (30%)
  other arithmetic  59.9 us (13%)
  starting transfers between devices  58.2 us (12%)
  local copies, waits for them, and re-layouts  29.5 us (6%)
  matrix products  5.31 us (1%)
    all_to_all x2, blocking collectives, localize(): lax.all_to_all(field, 'lev', split_axis=0, concat_axis=1, tiled=True)  76.9 us
    all_to_all x1, blocking collectives, localize(): return lax.all_to_all(mixed, 'lev', split_axis=1, concat_axis=0, tiled=True)  63.3 us
    ppermute x1, waiting for transfers between devices, shifted(): return lax.ppermute(block, axis, route)  56.2 us
    ppermute x8, waiting for transfers between devices, with_halo(): before = lax.ppermute(last, axis, up)  50.9 us
    ppermute x8, waiting for transfers between devices, with_halo(): after = lax.ppermute(first, axis, down)  44 us
    ppermute x8, starting transfers between devices, with_halo(): after = lax.ppermute(first, axis, down)  20.9 us
    add x1, other arithmetic, local(): gradient = control + diffuse(returned, coupling_ext, coupling_y)  15.2 us
    all_to_all x1, starting transfers between devices, local(): lax.all_to_all(obs_cells, 'tile', split_axis=0, concat_axis=0, tiled=True)  15.1 us
  transfers between devices with their start and end apart: 20, of which 16 were waited for; matrix products, arithmetic and copies ran while one was open for 7% of the time, Pallas kernels for 0%

commit v1 on v0

v1 whole, which is shorter than its diff:
```python
import functools

import jax
import jax.numpy as jnp
from jax import lax
from jax.experimental import pallas as pl
from jax.experimental.pallas import tpu as pltpu
from jax.sharding import PartitionSpec as P

STEPS = 4
W = STEPS
PLANE = 16


def chunks_of(half):
    sizes = [half - half // 2, half // 2]
    out, at = [], 0
    for s in sizes:
        if s:
            out.append((at, s))
            at += s
    return out


def permute(x, route):
    tiles, levs = lax.axis_size("tile"), lax.axis_size("lev")
    pairs = []
    for t in range(tiles):
        for j in range(levs):
            to = route(t, j)
            if to is not None:
                pairs.append((t * levs + j, (to[0] % tiles) * levs + to[1]))
    return lax.ppermute(x, ("tile", "lev"), pairs)


def flip_core(x):
    return permute(x, lambda t, j: (t, j ^ 1))


def flip_chip(x):
    return permute(x, lambda t, j: (t, j ^ 2))


def up(x):
    return permute(x, lambda t, j: (t + 1, j))


def down(x):
    return permute(x, lambda t, j: (t - 1, j))


def up_near(x):
    def route(t, j):
        if t % PLANE != PLANE - 1:
            return (t + 1, j)
        return (t + 1, j ^ 2) if j >= 2 else None

    return permute(x, route)


def down_near(x):
    def route(t, j):
        if t % PLANE != 0:
            return (t - 1, j)
        return (t - 1, j ^ 2) if j < 2 else None

    return permute(x, route)


def relay(x):
    def route(t, j):
        if t % PLANE == 0 and j < 2:
            return (t, j ^ 2)
        if t % PLANE == PLANE - 1 and j >= 2:
            return (t, j ^ 2)
        return None

    return permute(x, route)


def across(u, cy):
    n = u.shape[-1]
    f = cy * (pltpu.roll(u, n - 1, u.ndim - 1) - u)
    return f - pltpu.roll(f, 1, u.ndim - 1)


def sweep(u_ref, lo, hi, cx_ref, cy, emit):
    count = u_ref.shape[0]
    cur = u_ref[lo]
    before = cx_ref[lo - 1 : lo, :] * (cur - u_ref[lo - 1]) if lo > 0 else None
    for x in range(lo, hi + 1):
        nxt = u_ref[x + 1] if x + 1 < count else None
        flux = cx_ref[x : x + 1, :] * (nxt - cur) if nxt is not None else None
        new = cur + across(cur, cy)
        if flux is not None:
            new = new + flux
        if before is not None:
            new = new - before
        emit(x, new)
        cur, before = nxt, flux


def smooth_kernel(c_ref, ctl_ref, cx_ref, cy_ref, out_ref, u_ref):
    cols = ctl_ref.shape[1]
    cy = cy_ref[...]
    zero = jnp.zeros(u_ref.shape[1:], u_ref.dtype)
    for x in range(W):
        u_ref[x] = zero
        u_ref[W + cols + x] = zero
    for x in range(cols):
        u_ref[W + x] = ctl_ref[0, x]

    def keep(x, v):
        u_ref[x] = v

    def give(x, v):
        out_ref[0, x] = v.astype(out_ref.dtype)

    for step in range(1, STEPS + 1):
        sweep(u_ref, W - step, W + cols - 1 + step, cx_ref, cy, keep if step < STEPS else give)


def smooth_call(core, control, cxe, cyz):
    m, cols, lev, cy = control.shape
    half = m // 2
    ext = cols + 2 * W
    return pl.pallas_call(
        smooth_kernel,
        grid_spec=pltpu.PrefetchScalarGridSpec(
            num_scalar_prefetch=1,
            grid=(m,),
            in_specs=[
                pl.BlockSpec((1, cols, lev, cy), lambda i, c: (lax.rem(i + half * c[0], m), 0, 0, 0)),
                pl.BlockSpec((ext, cy), lambda i, c: (0, 0)),
                pl.BlockSpec((1, cy), lambda i, c: (0, 0)),
            ],
            out_specs=pl.BlockSpec((1, ext, lev, cy), lambda i, c: (i, 0, 0, 0)),
            scratch_shapes=[pltpu.VMEM((ext, lev, cy), jnp.float32)],
        ),
        out_shape=jax.ShapeDtypeStruct((m, ext, lev, cy), jnp.bfloat16),
        compiler_params=pltpu.CompilerParams(vmem_limit_bytes=32 * 2**20),
        cost_estimate=pl.CostEstimate(flops=80 * control.size, bytes_accessed=8 * control.size, transcendentals=0),
        name="smooth",
    )(core, control, cxe, cyz)


def scatter_kernel(vals_ref, cells_ref, out_ref):
    cols, lev, cy = out_ref.shape
    groups = vals_ref.shape[1] // lev
    rows = vals_ref.shape[0]
    vt = vals_ref[...].T
    high = vt.astype(jnp.bfloat16)
    low = (vt - high.astype(jnp.float32)).astype(jnp.bfloat16)
    lane = lax.broadcasted_iota(jnp.int32, (rows, cy), 1)
    total = [jnp.zeros((2 * lev, cy), jnp.float32) for _ in range(cols)]
    for a in range(groups):
        part = slice(a * lev, (a + 1) * lev)
        both = jnp.concatenate([high[part], low[part]], 0)
        cell = jnp.broadcast_to(cells_ref[:, a : a + 1], (rows, cy)).astype(jnp.int32) - lane
        for x in range(cols):
            hot = jnp.where(cell == x * cy, jnp.float32(1), jnp.float32(0)).astype(jnp.bfloat16)
            total[x] = total[x] + jnp.dot(both, hot, preferred_element_type=jnp.float32)
    for x in range(cols):
        out_ref[x] = total[x][:lev] + total[x][lev:]


def scatter_call(vals, cells, cols, lev, cy):
    return pl.pallas_call(
        scatter_kernel,
        out_shape=jax.ShapeDtypeStruct((cols, lev, cy), jnp.float32),
        in_specs=[pl.BlockSpec(memory_space=pltpu.VMEM)] * 2,
        out_specs=pl.BlockSpec(memory_space=pltpu.VMEM),
        compiler_params=pltpu.CompilerParams(vmem_limit_bytes=32 * 2**20),
        cost_estimate=pl.CostEstimate(flops=2**30, bytes_accessed=2**20, transcendentals=0),
        name="scatter",
    )(vals, cells)


def member_kernel(
    core_ref, own_ref, far_ref, left_ref, right_ref, s0_ref, s1_ref, g_ref, vf_ref, vt_ref, cx_ref, cy_ref,
    ctl_ref, part_ref, _grad, grad_ref, other_ref, inc_ref, u_ref,
):
    cols, lev, _ = grad_ref.shape[1:]
    ext = cols + 2 * W
    cy = cy_ref[...]

    @pl.when(pl.program_id(0) == 0)
    def _():
        inc_ref[...] = part_ref[...]

    def block(b, x):
        if x < W:
            return left_ref[b, 0, x]
        if x >= W + cols:
            return right_ref[b, 0, x - W - cols]
        return own_ref[b, 0, x - W] if b < 2 else far_ref[b - 2, 0, x - W]

    for x in range(0, ext, 2):
        weighted, smooth = [], []
        for y in (x, x + 1):
            weighted.append(
                jnp.concatenate([(block(b, y).astype(jnp.float32) * g_ref[b, y]).astype(jnp.bfloat16) for b in range(4)], 0)
            )
            smooth.append(jnp.concatenate([s0_ref[0, y], s1_ref[0, y]], 0))
        back = jnp.dot(vt_ref[...], jnp.concatenate(weighted, 1), preferred_element_type=jnp.float32)
        local = jnp.dot(vf_ref[...], jnp.concatenate(smooth, 1), preferred_element_type=jnp.float32)
        width = back.shape[1] // 2
        for i, y in enumerate((x, x + 1)):
            u_ref[y] = back[:, i * width : (i + 1) * width]
            for b in range(4):
                inc_ref[b, y] += block(b, y).astype(jnp.float32) * local[b * lev : (b + 1) * lev, i * width : (i + 1) * width]

    def keep(x, v):
        u_ref[x] = v

    def give(x, v):
        grad_ref[0, x - W] = ctl_ref[0, x - W] + v[:lev]
        other_ref[0, x - W] = v[lev:]

    for step in range(1, STEPS + 1):
        sweep(u_ref, step, ext - 1 - step, cx_ref, cy, keep if step < STEPS else give)


def member_call(core, at, own, far, left, right, s0, s1, g, vf, vt, cxe, cyz, control, part, grad):
    _, c, cols, lev, cy = own.shape
    m = control.shape[0]
    half = m // 2
    ext = cols + 2 * W
    first = grad is None
    whole = pl.BlockSpec((4, ext, lev, cy), lambda i, k: (0, 0, 0, 0))
    pair = pl.BlockSpec((2, 1, cols, lev, cy), lambda i, k: (0, i, 0, 0, 0))
    halo = pl.BlockSpec((4, 1, W, lev, cy), lambda i, k: (0, i, 0, 0, 0))
    spread = pl.BlockSpec((1, ext, lev, cy), lambda i, k: (at + i, 0, 0, 0))
    moved = pl.BlockSpec((1, ext, lev, cy), lambda i, k: (at + i, 0, 0, 0))
    mine = pl.BlockSpec((1, cols, lev, cy), lambda i, k: (k[0] * half + at + i, 0, 0, 0))

    def flat(shape):
        return pl.BlockSpec(shape, lambda i, k: (0,) * len(shape))

    in_specs = [pair, pair, halo, halo, spread, moved, whole, flat(vf.shape), flat(vt.shape), flat(cxe.shape), flat(cyz.shape), mine, whole]
    args = [own, far, left, right, s0, s1, g, vf, vt, cxe, cyz, control, part]
    body = member_kernel
    aliases = {}
    if first:
        body = functools.partial(_no_grad, member_kernel)
    else:
        in_specs.append(pl.BlockSpec(memory_space=pl.ANY))
        args.append(grad)
        aliases = {len(args): 0}
    return pl.pallas_call(
        body,
        grid_spec=pltpu.PrefetchScalarGridSpec(
            num_scalar_prefetch=1,
            grid=(c,),
            in_specs=in_specs,
            out_specs=[mine, pl.BlockSpec((1, cols, lev, cy), lambda i, k: (i, 0, 0, 0)), whole],
            scratch_shapes=[pltpu.VMEM((ext, 2 * lev, cy), jnp.float32)],
        ),
        out_shape=[
            jax.ShapeDtypeStruct(control.shape, jnp.float32),
            jax.ShapeDtypeStruct((c, cols, lev, cy), jnp.float32),
            jax.ShapeDtypeStruct(part.shape, jnp.float32),
        ],
        input_output_aliases=aliases,
        compiler_params=pltpu.CompilerParams(vmem_limit_bytes=40 * 2**20),
        cost_estimate=pl.CostEstimate(flops=c * 2**28, bytes_accessed=c * 2**20, transcendentals=0),
        name="members",
    )(core, *args)


def _no_grad(body, *refs):
    body(*refs[:14], None, *refs[14:])


def finish_kernel(_core, r_ref, ctl_ref, _grad, out_ref):
    out_ref[...] = ctl_ref[...] + r_ref[...]


def finish_call(core, at, r, control, grad):
    c, cols, lev, cy = r.shape
    half = control.shape[0] // 2
    theirs = pl.BlockSpec((1, cols, lev, cy), lambda i, k: ((1 - k[0]) * half + at + i, 0, 0, 0))
    return pl.pallas_call(
        finish_kernel,
        grid_spec=pltpu.PrefetchScalarGridSpec(
            num_scalar_prefetch=1,
            grid=(c,),
            in_specs=[pl.BlockSpec((1, cols, lev, cy), lambda i, k: (i, 0, 0, 0)), theirs, pl.BlockSpec(memory_space=pl.ANY)],
            out_specs=theirs,
        ),
        out_shape=jax.ShapeDtypeStruct(control.shape, jnp.float32),
        input_output_aliases={3: 0},
        compiler_params=pltpu.CompilerParams(vmem_limit_bytes=16 * 2**20),
        cost_estimate=pl.CostEstimate(flops=r.size, bytes_accessed=12 * r.size, transcendentals=0),
        name="finish",
    )(core, r, control, grad)


def local(control, ensemble, coupling_x, coupling_y, vertical_loc, obs_cells, obs_counts, obs_values):
    m, lev, cols, cy = control.shape
    half = m // 2
    tile, j = lax.axis_index("tile"), lax.axis_index("lev")
    core, chip = j % 2, j // 2
    core_arg = core.astype(jnp.int32).reshape(1)
    control = jnp.transpose(control, (0, 2, 1, 3))
    ens = jnp.transpose(ensemble, (0, 2, 1, 3))

    slot = lax.broadcasted_iota(jnp.int32, obs_cells.shape, 1)
    live = slot < obs_counts[:, None]
    masked = jnp.where(live[..., None], obs_values, jnp.float32(0.0))
    rows, cap = obs_cells.shape
    flat = masked.reshape(rows, cap * lev)
    message = jnp.concatenate(
        [flat, obs_cells.astype(jnp.float32), jnp.zeros((rows, (-cap * (lev + 1)) % 128), jnp.float32)], 1
    )

    mine = jnp.where(core == 0, ens[:half], ens[half:])
    other = jnp.where(core == 0, ens[half:], ens[:half])
    beside = flip_core(other)
    plan = chunks_of(half)
    owns = [jnp.stack([mine[a : a + c], beside[a : a + c]]) for a, c in plan]
    fars = [flip_chip(o) for o in owns]

    got = lax.all_to_all(message, "tile", split_axis=0, concat_axis=0, tiled=True)

    before = up(coupling_x[cols - W :])
    after = down(coupling_x[:W])
    cxe = jnp.concatenate([before, coupling_x, after], 0)
    cyz = jnp.where(lax.broadcasted_iota(jnp.int32, (1, cy), 1) < cy - 1, coupling_y[None], jnp.float32(0.0))

    v = vertical_loc
    v = jnp.where(chip == 0, v, jnp.roll(v, (2 * lev, 2 * lev), (0, 1)))
    v6 = v.reshape(2, 2, lev, 2, 2, lev)
    v = jnp.where(core == 0, v6, v6[:, ::-1, :, :, ::-1, :]).reshape(4 * lev, 4 * lev)
    vf = v[:, : 2 * lev]
    vt = v[:, : 2 * lev].T

    smooth = smooth_call(core_arg, control, cxe, cyz)
    smooth_beside = flip_core(smooth[half:])

    vals = got[:, : cap * lev].reshape(rows * cap * lev // 128, 128)
    cells = got[:, cap * lev : cap * (lev + 1)].reshape(vals.shape[0], -1)
    g_own = scatter_call(vals, cells, cols, lev, cy)
    g_own = jnp.concatenate([up(g_own[cols - W :]), g_own, down(g_own[:W])], 0)
    g_far = flip_chip(g_own)
    g_pair = jnp.stack([g_own, g_far])
    g_beside = flip_core(g_pair)
    g = jnp.stack([g_own, g_beside[0], g_far, g_beside[1]])

    low_edge, high_edge = tile % PLANE == 0, tile % PLANE == PLANE - 1
    part = jnp.zeros((4, cols + 2 * W, lev, cy), jnp.float32)
    grad = None
    returned = []
    for (at, c), own, far in zip(plan, owns, fars):
        last = (own[:, :, cols - W :], far[:, :, cols - W :])
        head = (own[:, :, :W], far[:, :, :W])

        def ordered(swap, pair):
            return jnp.concatenate([jnp.where(swap, pair[1], pair[0]), jnp.where(swap, pair[0], pair[1])], 0)

        left = up_near(ordered(high_edge, last))
        right = down_near(ordered(low_edge, head))
        edge = jnp.where(low_edge, left, right)
        again = relay(jnp.concatenate([edge[2:], edge[:2]], 0))
        left = jnp.where(low_edge & (chip == 1), again, left)
        right = jnp.where(high_edge & (chip == 0), again, right)
        grad, r, part = member_call(
            core_arg, at, own, far, left, right, smooth, smooth_beside, g, vf, vt, cxe, cyz, control, part, grad
        )
        returned.append(flip_core(r))
    for (at, c), r in zip(plan, returned):
        grad = finish_call(core_arg, at, r, control, grad)

    pair = part[::2] + flip_core(part[1::2])
    total = pair[0] + flip_chip(pair[1])
    edge_low = up(total[W + cols :])
    edge_high = down(total[:W])
    middle = total[W : W + cols]
    inc = jnp.concatenate([middle[:W] + edge_low, middle[W : cols - W], middle[cols - W :] + edge_high], 0)
    return jnp.transpose(inc, (1, 0, 2)), jnp.transpose(grad, (0, 2, 1, 3))


def solution(mesh):
    placed = (
        P(None, "lev", "tile", None),
        P(None, "lev", "tile", None),
        P("tile", None),
        P(),
        P(),
        P("tile", None),
        P("tile"),
        P("tile", None, "lev"),
    )
    return jax.shard_map(
        local,
        mesh=mesh,
        in_specs=placed,
        out_specs=(P("lev", "tile", None), P(None, "lev", "tile", None)),
        check_vma=False,
    )
```

time: 470 us -> 248 us (0.53); the launches traced: 461 us -> 247 us
  blocking collectives: 140 us -> 0 us
  waiting for transfers between devices: 167 us -> 84.1 us
  Pallas kernels: 0 us -> 74.3 us
  other arithmetic: 59.9 us -> 14.8 us
  local copies, waits for them, and re-layouts: 29.5 us -> 11 us
  matrix products: 5.31 us -> 0 us
    all_to_all x3 -> x0, blocking collectives: 140 us -> none  [the longest x2 76.9 us: localize(): lax.all_to_all(field, 'lev', split_axis=0, concat_axis=1, tiled=True)]
    pallas_call x0 -> x6, Pallas kernels: none -> 74.3 us  [the longest x2 35.4 us: member_call(): pl.pallas_call(body, grid_spec=pltpu.PrefetchScalarGridSpec(num_scalar_pr...]
    ppermute x17 -> x22, waiting for transfers between devices: 151 us -> 76.9 us  [permute(): return lax.ppermute(x, ('tile', 'lev'), pairs)]
    add x6 -> x4, other arithmetic: 27.4 us -> 0.18 us  [the longest x1 0.11 us: local(): pair = part[::2] + flip_core(part[1::2])]
    ppermute x17 -> x22, starting transfers between devices: 28.9 us -> 48.2 us  [permute(): return lax.ppermute(x, ('tile', 'lev'), pairs)]
    all_to_all x3 -> x1, starting transfers between devices: 29.2 us -> 14 us  [local(): lax.all_to_all(message, 'tile', split_axis=0, concat_axis=0, tiled=True)]
    scatter-add x1 -> x0, other arithmetic: 12 us -> none  [local(): jax.ops.segment_sum(got_values.reshape(-1, block), got_cells.reshape(-1),...]
    transpose x2 -> x1, local copies, waits for them, and re-layouts: 12 us -> 0.01 us  [local(): vt = v[:, :2 * lev].T]
  transfers between devices with their start and end apart: 20 -> 23, of which waited for: 16 -> 9; matrix products, arithmetic and copies ran while one was open for 7% -> 8% of each run, Pallas kernels for 0% -> 16%
where the time goes in v1:
time: 248 us; the launch traced here: 247 us
  waiting for transfers between devices  84.1 us (34%)
  Pallas kernels  74.3 us (30%)
  starting transfers between devices  62.1 us (25%)
  other arithmetic  14.8 us (6%)
  local copies, waits for them, and re-layouts  11 us (4%)
    ppermute x22, waiting for transfers between devices, permute(): return lax.ppermute(x, ('tile', 'lev'), pairs)  76.9 us
    ppermute x22, starting transfers between devices, permute(): return lax.ppermute(x, ('tile', 'lev'), pairs)  48.2 us
    pallas_call x2, Pallas kernels, member_call(): pl.pallas_call(body, grid_spec=pltpu.PrefetchScalarGridSpec(num_scalar_pr...  35.4 us
    pallas_call x1, Pallas kernels, smooth_call(): pl.pallas_call(smooth_kernel, grid_spec=pltpu.PrefetchScalarGridSpec(num_...  33.4 us
    all_to_all x1, starting transfers between devices, local(): lax.all_to_all(message, 'tile', split_axis=0, concat_axis=0, tiled=True)  14 us
    all_to_all x1, waiting for transfers between devices, local(): lax.all_to_all(message, 'tile', split_axis=0, concat_axis=0, tiled=True)  7.19 us
  transfers between devices with their start and end apart: 23, of which 9 were waited for; matrix products, arithmetic and copies ran while one was open for 8% of the time, Pallas kernels for 16%

profile of v1, /device:TPU:1, one launch (start us, length us, event | category | flops | bytes accessed | tf_op | source)
XLA Modules:
  0.0 247.5 jit_solution(15882660776677377764)
XLA Ops:
  1.3 2.0 collective-permute-start.5
  3.4 2.6 %broadcast_select_fusion.1 = (bf16[10,12,32,128]{3,2,1,0:T(8,128)(2,1)S(1)}, bf16[10,12,32,128]{3,2,1,0:T(8,128)(2,1)}) fusion(pred[]{:T(512)S(6)} %eq.24, bf16[20,12,32,128]{3,2,1,0:T(8,128)(2,1)} %bitcast.42), kind=kLoop, calls=%fused_computation.12 | loop fusion | flops 983040 | bytes 3932161 | tf_op jit(solution)/shard_map/jit(_where)/select_n | solution.py:317
  8.6 14.0 %all-to-all-start = ((f32[64,1,1152]{2,1,0:T(1,128)}), f32[64,1,1152]{2,1,0:T(1,128)}, u32[]{:S(2)}, u32[]{:S(2)}) async-start(f32[64,1,1152]{2,1,0:T(1,128)} %copy.31), calls=%async_computation | async-start | bytes 589824 | tf_op jit(solution)/shard_map/all_to_all | solution.py:324
  29.4 7.2 %all-to-all-done = f32[64,1,1152]{2,1,0:T(1,128)} async-done(((f32[64,1,1152]{2,1,0:T(1,128)}), f32[64,1,1152]{2,1,0:T(1,128)}, u32[]{:S(2)}, u32[]{:S(2)}) %all-to-all-start) | async-done | bytes 294944 | tf_op jit(solution)/shard_map/all_to_all | solution.py:324
  41.0 7.6 %collective-permute-start.9 = (f32[4,32,128]{2,1,0:T(8,128)S(1)}, f32[4,32,128]{2,1,0:T(8,128)S(1)}, u32[]{:S(2)}, u32[]{:S(2)}) collective-permute-start(f32[4,32,128]{2,1,0:T(8,128)S(1)} %get-tuple-element.44), channel_id=1, source_target_pairs={{0,252},{1,253},{2,254},{3,255},{4,0},{5,1},{6,2},{7,3},{8,4},{9,5... | collective-permute-start | bytes 196616 | tf_op jit(solution)/shard_map/ppermute | solution.py:33
  48.6 3.2 %collective-permute-done.1.far_ref = bf16[2,5,12,32,128]{4,3,2,1,0:T(8,128)(2,1)S(1)} collective-permute-done((bf16[2,5,12,32,128]{4,3,2,1,0:T(8,128)(2,1)S(1)}, bf16[2,5,12,32,128]{4,3,2,1,0:T(8,128)(2,1)S(1)}, u32[]{:S(2)}, u32[]{:S(2)}) %collective-permute-start.1) | collective-permute-done | bytes 983072 | tf_op jit(solution)/shard_map/ppermute | solution.py:33
  52.8 2.0 collective-permute-start.2
  55.7 17.9 %collective-permute-done.12.refs_2_ = bf16[2,5,12,32,128]{4,3,2,1,0:T(8,128)(2,1)} collective-permute-done((bf16[2,5,12,32,128]{4,3,2,1,0:T(8,128)(2,1)S(1)}, bf16[2,5,12,32,128]{4,3,2,1,0:T(8,128)(2,1)}, u32[]{:S(2)}, u32[]{:S(2)}) %collective-permute-start.12) | collective-permute-done | bytes 983072 | tf_op jit(solution)/shard_map/ppermute | solution.py:33
  73.7 8.9 %collective-permute-start.3 = (bf16[4,5,4,32,128]{4,3,2,1,0:T(8,128)(2,1)}, bf16[4,5,4,32,128]{4,3,2,1,0:T(8,128)(2,1)}, u32[]{:S(2)}, u32[]{:S(2)}) collective-permute-start(bf16[4,5,4,32,128]{4,3,2,1,0:T(8,128)(2,1)} %pad_maximum_fusion.4), channel_id=1, source_target_pairs={{0,254},{1,255},{4,0},{5,1},{6,2},{7,3},{8,4},{9,5},{10,6},{11,7},... | collective-permute-start | bytes 1966088 | tf_op jit(solution)/shard_map/ppermute | solution.py:33
  87.5 8.8 %collective-permute-start.14 = (bf16[4,5,4,32,128]{4,3,2,1,0:T(8,128)(2,1)}, bf16[4,5,4,32,128]{4,3,2,1,0:T(8,128)(2,1)}, u32[]{:S(2)}, u32[]{:S(2)}) collective-permute-start(bf16[4,5,4,32,128]{4,3,2,1,0:T(8,128)(2,1)} %pad_maximum_fusion.8), channel_id=1, source_target_pairs={{0,254},{1,255},{4,0},{5,1},{6,2},{7,3},{8,4},{9,5},{10,6},{11,7},... | collective-permute-start | bytes 1966088 | tf_op jit(solution)/shard_map/ppermute | solution.py:33
  96.6 12.3 %collective-permute-done.6 = f32[4,128]{1,0:T(4,128)S(1)} collective-permute-done((f32[4,128]{1,0:T(4,128)S(1)}, f32[4,128]{1,0:T(4,128)S(1)}, u32[]{:S(2)}, u32[]{:S(2)}) %collective-permute-start.6) | collective-permute-done | bytes 2080 | tf_op jit(solution)/shard_map/ppermute | solution.py:33
  109.0 2.1 copy-done
  111.1 33.4 %smooth.1.refs_5_.s0_ref = bf16[20,20,32,128]{3,2,1,0:T(8,128)(2,1)S(1)} custom-call(s32[1]{0:T(128)} %bitcast.c_ref.refs_0_.core_ref._core, f32[20,12,32,128]{3,2,1,0:T(8,128)S(1)} %bitcast.37, f32[20,128]{1,0:T(8,128)S(1)} %pad_maximum_fusion.12.cx_ref.refs_10_, f32[1,128]{1,0:T(1,128)S(1)} %fusion.7.cy_ref.refs_11_), custom_call_target="tpu_custom_call" | custom-call | flops 78643200 | bytes 7864320 | tf_op jit(solution)/shard_map/smooth/pallas_call | solution.py:127
  144.8 3.3 %collective-permute-start.7 = (bf16[10,20,32,128]{3,2,1,0:T(8,128)(2,1)S(1)}, bf16[10,20,32,128]{3,2,1,0:T(8,128)(2,1)S(1)}, u32[]{:S(2)}, u32[]{:S(2)}) collective-permute-start(bf16[10,20,32,128]{3,2,1,0:T(8,128)(2,1)S(1)} %slice.187), channel_id=1, source_target_pairs={{0,1},{1,0},{2,3},{3,2},{4,5},{5,4},{6,7},{7,6},{8,9},{9,8},{10,11... | collective-permute-start | bytes 4915208 | tf_op jit(solution)/shard_map/ppermute | solution.py:33
  149.8 3.7 %collective-permute-start.4 = (bf16[4,5,4,32,128]{4,3,2,1,0:T(8,128)(2,1)S(1)}, bf16[4,5,4,32,128]{4,3,2,1,0:T(8,128)(2,1)S(1)}, u32[]{:S(2)}, u32[]{:S(2)}) collective-permute-start(bf16[4,5,4,32,128]{4,3,2,1,0:T(8,128)(2,1)S(1)} %pad_maximum_fusion.5), channel_id=1, source_target_pairs={{0,2},{1,3},{62,60},{63,61},{64,66},{65,67},{126,124},{127,125},{1... | collective-permute-start | bytes 1966088 | tf_op jit(solution)/shard_map/ppermute | solution.py:33
  155.1 11.9 %collective-permute-done.4 = bf16[4,5,4,32,128]{4,3,2,1,0:T(8,128)(2,1)S(1)} collective-permute-done((bf16[4,5,4,32,128]{4,3,2,1,0:T(8,128)(2,1)S(1)}, bf16[4,5,4,32,128]{4,3,2,1,0:T(8,128)(2,1)S(1)}, u32[]{:S(2)}, u32[]{:S(2)}) %collective-permute-start.4) | collective-permute-done | bytes 655392 | tf_op jit(solution)/shard_map/ppermute | solution.py:33
  168.4 12.6 %collective-permute-done.15 = bf16[4,5,4,32,128]{4,3,2,1,0:T(8,128)(2,1)S(1)} collective-permute-done((bf16[4,5,4,32,128]{4,3,2,1,0:T(8,128)(2,1)S(1)}, bf16[4,5,4,32,128]{4,3,2,1,0:T(8,128)(2,1)S(1)}, u32[]{:S(2)}, u32[]{:S(2)}) %collective-permute-start.15) | collective-permute-done | bytes 655392 | tf_op jit(solution)/shard_map/ppermute | solution.py:33
  182.6 17.7 %members.2 = (f32[20,12,32,128]{3,2,1,0:T(8,128)}, f32[5,12,32,128]{3,2,1,0:T(8,128)S(1)}, f32[4,20,32,128]{3,2,1,0:T(8,128)S(1)}) custom-call(s32[1]{0:T(128)} %bitcast.c_ref.refs_0_.core_ref._core, bf16[2,5,12,32,128]{4,3,2,1,0:T(8,128)(2,1)S(1)} %pad_maximum_fusion.2.refs_1_, bf16[2,5,12,32,128]{4,3,2,1,0:T(8,128)(2,1)} %collective-permute-done.12.refs_2_, ...), custom_call_target="tpu_custom_call" | custom-call | flops 1342177280 | bytes 5242880 | tf_op jit(solution)/shard_map/members/pallas_call | solution.py:250
  200.4 17.7 %members.3 = (f32[20,12,32,128]{3,2,1,0:T(8,128)}, f32[5,12,32,128]{3,2,1,0:T(8,128)S(1)}, f32[4,20,32,128]{3,2,1,0:T(8,128)S(1)}) custom-call(s32[1]{0:T(128)} %bitcast.c_ref.refs_0_.core_ref._core, bf16[2,5,12,32,128]{4,3,2,1,0:T(8,128)(2,1)S(1)} %pad_maximum_fusion.1.own_ref, ...), custom_call_target="tpu_custom_call", output_to_operand_aliasing={{0}: (14, {})} | custom-call | flops 1342177280 | bytes 5242880 | tf_op jit(solution)/shard_map/members/pallas_call | solution.py:250
  221.4 2.1 collective-permute-start.17
  223.5 7.8 %collective-permute-done.17 = f32[20,32,128]{2,1,0:T(8,128)S(1)} collective-permute-done((f32[20,32,128]{2,1,0:T(8,128)S(1)}, f32[20,32,128]{2,1,0:T(8,128)S(1)}, u32[]{:S(2)}, u32[]{:S(2)}) %collective-permute-start.17) | collective-permute-done | bytes 327712 | tf_op jit(solution)/shard_map/ppermute | solution.py:33
  231.4 9.9 %collective-permute-done.18 = f32[4,32,128]{2,1,0:T(8,128)S(1)} collective-permute-done((f32[4,32,128]{2,1,0:T(8,128)S(1)}, f32[4,32,128]{2,1,0:T(8,128)S(1)}, u32[]{:S(2)}, u32[]{:S(2)}) %collective-permute-start.18) | collective-permute-done | bytes 65568 | tf_op jit(solution)/shard_map/ppermute | solution.py:33
  242.6 2.1 finish.2._grad
  244.7 2.1 finish.3
  (124 shorter events, 33.4 us)
Async XLA Ops:
  1.3 84.2 %collective-permute-start.5 = (f32[4,128]{1,0:T(4,128)S(1)}, f32[4,128]{1,0:T(4,128)S(1)}, u32[]{:S(2)}, u32[]{:S(2)}) collective-permute-start(f32[4,128]{1,0:T(4,128)S(1)} %get-tuple-element.49), channel_id=1, source_target_pairs={{0,4},{1,5},{2,6},{3,7},{4,8},{5,9},{6,10},{7,11},{8,12},{9,13},{1... | collective-permute-start | bytes 6152 | tf_op jit(solution)/shard_map/ppermute | solution.py:33
  6.0 16.7 %collective-permute-start = (bf16[10,12,32,128]{3,2,1,0:T(8,128)(2,1)}, bf16[10,12,32,128]{3,2,1,0:T(8,128)(2,1)S(1)}, u32[]{:S(2)}, u32[]{:S(2)}) collective-permute-start(bf16[10,12,32,128]{3,2,1,0:T(8,128)(2,1)} %get-tuple-element.23), channel_id=1, source_target_pairs={{0,1},{1,0},{2,3},{3,2},{4,5},{5,4},{6,7},{7,6},{8,9},{9,8},{10,11... | collective-permute-start | bytes 2949128 | tf_op jit(solution)/shard_map/ppermute | solution.py:33
  8.6 27.9 %all-to-all-start = ((f32[64,1,1152]{2,1,0:T(1,128)}), f32[64,1,1152]{2,1,0:T(1,128)}, u32[]{:S(2)}, u32[]{:S(2)}) async-start(f32[64,1,1152]{2,1,0:T(1,128)} %copy.31), calls=%async_computation | async-start | bytes 589824 | tf_op jit(solution)/shard_map/all_to_all | solution.py:324
  24.6 27.2 %collective-permute-start.1 = (bf16[2,5,12,32,128]{4,3,2,1,0:T(8,128)(2,1)S(1)}, bf16[2,5,12,32,128]{4,3,2,1,0:T(8,128)(2,1)S(1)}, u32[]{:S(2)}, u32[]{:S(2)}) collective-permute-start(bf16[2,5,12,32,128]{4,3,2,1,0:T(8,128)(2,1)S(1)} %pad_maximum_fusion.1.own_ref), channel_id=1, source_target_pairs={{0,2},{1,3},{2,0},{3,1},{4,6},{5,7},{6,4},{7,5},{8,10},{9,11},{10,... | collective-permute-start | bytes 2949128 | tf_op jit(solution)/shard_map/ppermute | solution.py:33
  28.3 45.4 %collective-permute-start.12 = (bf16[2,5,12,32,128]{4,3,2,1,0:T(8,128)(2,1)S(1)}, bf16[2,5,12,32,128]{4,3,2,1,0:T(8,128)(2,1)}, u32[]{:S(2)}, u32[]{:S(2)}) collective-permute-start(bf16[2,5,12,32,128]{4,3,2,1,0:T(8,128)(2,1)S(1)} %pad_maximum_fusion.2.refs_1_), channel_id=1, source_target_pairs={{0,2},{1,3},{2,0},{3,1},{4,6},{5,7},{6,4},{7,5},{8,10},{9,11},{10,... | collective-permute-start | bytes 2949128 | tf_op jit(solution)/shard_map/ppermute | solution.py:33
  40.7 46.8 %collective-permute-start.8 = (f32[4,32,128]{2,1,0:T(8,128)S(1)}, f32[4,32,128]{2,1,0:T(8,128)S(1)}, u32[]{:S(2)}, u32[]{:S(2)}) collective-permute-start(f32[4,32,128]{2,1,0:T(8,128)S(1)} %get-tuple-element.43), channel_id=1, source_target_pairs={{0,4},{1,5},{2,6},{3,7},{4,8},{5,9},{6,10},{7,11},{8,12},{9,13},{1... | collective-permute-start | bytes 196616 | tf_op jit(solution)/shard_map/ppermute | solution.py:33
  41.0 55.5 %collective-permute-start.9 = (f32[4,32,128]{2,1,0:T(8,128)S(1)}, f32[4,32,128]{2,1,0:T(8,128)S(1)}, u32[]{:S(2)}, u32[]{:S(2)}) collective-permute-start(f32[4,32,128]{2,1,0:T(8,128)S(1)} %get-tuple-element.44), channel_id=1, source_target_pairs={{0,252},{1,253},{2,254},{3,255},{4,0},{5,1},{6,2},{7,3},{8,4},{9,5... | collective-permute-start | bytes 196616 | tf_op jit(solution)/shard_map/ppermute | solution.py:33
  51.9 30.7 %copy-start.4 = (bf16[1,5,12,32,128]{4,3,2,1,0:T(8,128)(2,1)S(1)}, bf16[1,5,12,32,128]{4,3,2,1,0:T(8,128)(2,1)}, u32[]{:S(2)}) copy-start(bf16[1,5,12,32,128]{4,3,2,1,0:T(8,128)(2,1)} %copy-done.3) | copy-start | bytes 1474564
  52.8 95.3 %collective-permute-start.2 = (bf16[4,5,4,32,128]{4,3,2,1,0:T(8,128)(2,1)}, bf16[4,5,4,32,128]{4,3,2,1,0:T(8,128)(2,1)}, u32[]{:S(2)}, u32[]{:S(2)}) collective-permute-start(bf16[4,5,4,32,128]{4,3,2,1,0:T(8,128)(2,1)} %pad_maximum_fusion.3), channel_id=1, source_target_pairs={{0,4},{1,5},{2,6},{3,7},{4,8},{5,9},{6,10},{7,11},{8,12},{9,13},{1... | collective-permute-start | bytes 1966088 | tf_op jit(solution)/shard_map/ppermute | solution.py:33
  73.7 74.5 %collective-permute-start.3 = (bf16[4,5,4,32,128]{4,3,2,1,0:T(8,128)(2,1)}, bf16[4,5,4,32,128]{4,3,2,1,0:T(8,128)(2,1)}, u32[]{:S(2)}, u32[]{:S(2)}) collective-permute-start(bf16[4,5,4,32,128]{4,3,2,1,0:T(8,128)(2,1)} %pad_maximum_fusion.4), channel_id=1, source_target_pairs={{0,254},{1,255},{4,0},{5,1},{6,2},{7,3},{8,4},{9,5},{10,6},{11,7},... | collective-permute-start | bytes 1966088 | tf_op jit(solution)/shard_map/ppermute | solution.py:33
  85.6 62.6 %collective-permute-start.13 = (bf16[4,5,4,32,128]{4,3,2,1,0:T(8,128)(2,1)}, bf16[4,5,4,32,128]{4,3,2,1,0:T(8,128)(2,1)}, u32[]{:S(2)}, u32[]{:S(2)}) collective-permute-start(bf16[4,5,4,32,128]{4,3,2,1,0:T(8,128)(2,1)} %pad_maximum_fusion.7), channel_id=1, source_target_pairs={{0,4},{1,5},{2,6},{3,7},{4,8},{5,9},{6,10},{7,11},{8,12},{9,13},{1... | collective-permute-start | bytes 1966088 | tf_op jit(solution)/shard_map/ppermute | solution.py:33
  87.5 60.7 %collective-permute-start.14 = (bf16[4,5,4,32,128]{4,3,2,1,0:T(8,128)(2,1)}, bf16[4,5,4,32,128]{4,3,2,1,0:T(8,128)(2,1)}, u32[]{:S(2)}, u32[]{:S(2)}) collective-permute-start(bf16[4,5,4,32,128]{4,3,2,1,0:T(8,128)(2,1)} %pad_maximum_fusion.8), channel_id=1, source_target_pairs={{0,254},{1,255},{4,0},{5,1},{6,2},{7,3},{8,4},{9,5},{10,6},{11,7},... | collective-permute-start | bytes 1966088 | tf_op jit(solution)/shard_map/ppermute | solution.py:33
  96.5 12.4 %collective-permute-start.6 = (f32[4,128]{1,0:T(4,128)S(1)}, f32[4,128]{1,0:T(4,128)S(1)}, u32[]{:S(2)}, u32[]{:S(2)}) collective-permute-start(f32[4,128]{1,0:T(4,128)S(1)} %get-tuple-element.50), channel_id=1, source_target_pairs={{0,252},{1,253},{2,254},{3,255},{4,0},{5,1},{6,2},{7,3},{8,4},{9,5... | collective-permute-start | bytes 6152 | tf_op jit(solution)/shard_map/ppermute | solution.py:33
  108.9 35.8 %collective-permute-start.10 = (f32[20,32,128]{2,1,0:T(8,128)S(1)}, f32[20,32,128]{2,1,0:T(8,128)S(1)}, u32[]{:S(2)}, u32[]{:S(2)}) collective-permute-start(f32[20,32,128]{2,1,0:T(8,128)S(1)} %get-tuple-element.42), channel_id=1, source_target_pairs={{0,2},{1,3},{2,0},{3,1},{4,6},{5,7},{6,4},{7,5},{8,10},{9,11},{10,... | collective-permute-start | bytes 983048 | tf_op jit(solution)/shard_map/ppermute | solution.py:33
  144.8 37.7 %collective-permute-start.7 = (bf16[10,20,32,128]{3,2,1,0:T(8,128)(2,1)S(1)}, bf16[10,20,32,128]{3,2,1,0:T(8,128)(2,1)S(1)}, u32[]{:S(2)}, u32[]{:S(2)}) collective-permute-start(bf16[10,20,32,128]{3,2,1,0:T(8,128)(2,1)S(1)} %slice.187), channel_id=1, source_target_pairs={{0,1},{1,0},{2,3},{3,2},{4,5},{5,4},{6,7},{7,6},{8,9},{9,8},{10,11... | collective-permute-start | bytes 4915208 | tf_op jit(solution)/shard_map/ppermute | solution.py:33
  148.1 6.9 %collective-permute-start.11 = (f32[2,20,32,128]{3,2,1,0:T(8,128)S(1)}, f32[2,20,32,128]{3,2,1,0:T(8,128)S(1)}, u32[]{:S(2)}, u32[]{:S(2)}) collective-permute-start(f32[2,20,32,128]{3,2,1,0:T(8,128)S(1)} %pad_maximum_fusion.6), channel_id=1, source_target_pairs={{0,1},{1,0},{2,3},{3,2},{4,5},{5,4},{6,7},{7,6},{8,9},{9,8},{10,11... | collective-permute-start | bytes 1966088 | tf_op jit(solution)/shard_map/ppermute | solution.py:33
  149.8 17.3 %collective-permute-start.4 = (bf16[4,5,4,32,128]{4,3,2,1,0:T(8,128)(2,1)S(1)}, bf16[4,5,4,32,128]{4,3,2,1,0:T(8,128)(2,1)S(1)}, u32[]{:S(2)}, u32[]{:S(2)}) collective-permute-start(bf16[4,5,4,32,128]{4,3,2,1,0:T(8,128)(2,1)S(1)} %pad_maximum_fusion.5), channel_id=1, source_target_pairs={{0,2},{1,3},{62,60},{63,61},{64,66},{65,67},{126,124},{127,125},{1... | collective-permute-start | bytes 1966088 | tf_op jit(solution)/shard_map/ppermute | solution.py:33
  153.6 27.5 %collective-permute-start.15 = (bf16[4,5,4,32,128]{4,3,2,1,0:T(8,128)(2,1)S(1)}, bf16[4,5,4,32,128]{4,3,2,1,0:T(8,128)(2,1)S(1)}, u32[]{:S(2)}, u32[]{:S(2)}) collective-permute-start(bf16[4,5,4,32,128]{4,3,2,1,0:T(8,128)(2,1)S(1)} %pad_maximum_fusion.9), channel_id=1, source_target_pairs={{0,2},{1,3},{62,60},{63,61},{64,66},{65,67},{126,124},{127,125},{1... | collective-permute-start | bytes 1966088 | tf_op jit(solution)/shard_map/ppermute | solution.py:33
  218.1 3.1 %collective-permute-start.16 = (f32[2,20,32,128]{3,2,1,0:T(8,128)S(1)}, f32[2,20,32,128]{3,2,1,0:T(8,128)S(1)}, u32[]{:S(2)}, u32[]{:S(2)}) collective-permute-start(f32[2,20,32,128]{3,2,1,0:T(8,128)S(1)} %slice.167), channel_id=1, source_target_pairs={{0,1},{1,0},{2,3},{3,2},{4,5},{5,4},{6,7},{7,6},{8,9},{9,8},{10,11... | collective-permute-start | bytes 1966088 | tf_op jit(solution)/shard_map/ppermute | solution.py:33
  219.5 25.2 %collective-permute-start.20 = (f32[5,12,32,128]{3,2,1,0:T(8,128)S(1)}, f32[5,12,32,128]{3,2,1,0:T(8,128)S(1)}, u32[]{:S(2)}, u32[]{:S(2)}) collective-permute-start(f32[5,12,32,128]{3,2,1,0:T(8,128)S(1)} %get-tuple-element.11), channel_id=1, source_target_pairs={{0,1},{1,0},{2,3},{3,2},{4,5},{5,4},{6,7},{7,6},{8,9},{9,8},{10,11... | collective-permute-start | bytes 2949128 | tf_op jit(solution)/shard_map/ppermute | solution.py:33
  219.6 23.0 %collective-permute-start.21 = (f32[5,12,32,128]{3,2,1,0:T(8,128)S(1)}, f32[5,12,32,128]{3,2,1,0:T(8,128)S(1)}, u32[]{:S(2)}, u32[]{:S(2)}) collective-permute-start(f32[5,12,32,128]{3,2,1,0:T(8,128)S(1)} %get-tuple-element.12), channel_id=1, source_target_pairs={{0,1},{1,0},{2,3},{3,2},{4,5},{5,4},{6,7},{7,6},{8,9},{9,8},{10,11... | collective-permute-start | bytes 2949128 | tf_op jit(solution)/shard_map/ppermute | solution.py:33
  221.4 9.9 %collective-permute-start.17 = (f32[20,32,128]{2,1,0:T(8,128)S(1)}, f32[20,32,128]{2,1,0:T(8,128)S(1)}, u32[]{:S(2)}, u32[]{:S(2)}) collective-permute-start(f32[20,32,128]{2,1,0:T(8,128)S(1)} %slice_bitcast_fusion.4), channel_id=1, source_target_pairs={{0,2},{1,3},{2,0},{3,1},{4,6},{5,7},{6,4},{7,5},{8,10},{9,11},{10,... | collective-permute-start | bytes 983048 | tf_op jit(solution)/shard_map/ppermute | solution.py:33
  231.3 10.0 %collective-permute-start.18 = (f32[4,32,128]{2,1,0:T(8,128)S(1)}, f32[4,32,128]{2,1,0:T(8,128)S(1)}, u32[]{:S(2)}, u32[]{:S(2)}) collective-permute-start(f32[4,32,128]{2,1,0:T(8,128)S(1)} %slice.210), channel_id=1, source_target_pairs={{0,4},{1,5},{2,6},{3,7},{4,8},{5,9},{6,10},{7,11},{8,12},{9,13},{1... | collective-permute-start | bytes 196616 | tf_op jit(solution)/shard_map/ppermute | solution.py:33
  241.3 5.4 %collective-permute-start.19 = (f32[4,32,128]{2,1,0:T(8,128)S(1)}, f32[4,32,128]{2,1,0:T(8,128)S(1)}, u32[]{:S(2)}, u32[]{:S(2)}) collective-permute-start(f32[4,32,128]{2,1,0:T(8,128)S(1)} %get-tuple-element.39), channel_id=1, source_target_pairs={{0,252},{1,253},{2,254},{3,255},{4,0},{5,1},{6,2},{7,3},{8,4},{9,5... | collective-permute-start | bytes 196616 | tf_op jit(solution)/shard_map/ppermute | solution.py:33
  (18 other events, 166.6 us)

commit v2 on v1

v2 whole, which is shorter than its diff:
```python
import functools

import jax
import jax.numpy as jnp
from jax import lax
from jax.experimental import pallas as pl
from jax.experimental.pallas import tpu as pltpu
from jax.sharding import PartitionSpec as P

STEPS = 4
W = STEPS
PLANE = 16
COST = pl.CostEstimate(flops=1, bytes_accessed=1, transcendentals=0)


def chunks_of(half):
    sizes = [half - 2 * (2 * half // 5), 2 * half // 5, 2 * half // 5]
    out, at = [], 0
    for s in sizes:
        if s:
            out.append((at, s))
            at += s
    return out


def permute(x, route):
    tiles, levs = lax.axis_size("tile"), lax.axis_size("lev")
    pairs = []
    for t in range(tiles):
        for j in range(levs):
            to = route(t, j)
            if to is not None:
                pairs.append((t * levs + j, (to[0] % tiles) * levs + to[1]))
    return lax.ppermute(x, ("tile", "lev"), pairs)


def flip_core(x):
    return permute(x, lambda t, j: (t, j ^ 1))


def flip_chip(x):
    return permute(x, lambda t, j: (t, j ^ 2))


def swap_first(x):
    return permute(x, lambda t, j: (t + 1 if t % 2 == 0 else t - 1, j))


def swap_second(x):
    return permute(x, lambda t, j: (t - 1 if t % 2 == 0 else t + 1, j))


def swap_second_near(x):
    def route(t, j):
        to = t - 1 if t % 2 == 0 else t + 1
        if t % PLANE == 0:
            return (to, j ^ 2) if j < 2 else None
        if t % PLANE == PLANE - 1:
            return (to, j ^ 2) if j >= 2 else None
        return (to, j)

    return permute(x, route)


def beside_tile(even, top, bottom):
    a = swap_first(jnp.where(even, top, bottom))
    b = swap_second(jnp.where(even, bottom, top))
    return jnp.where(even, b, a), jnp.where(even, a, b)


def relay(x):
    def route(t, j):
        if (t % PLANE == 0 and j < 2) or (t % PLANE == PLANE - 1 and j >= 2):
            return (t, j ^ 2)
        return None

    return permute(x, route)


def reach(x):
    def route(t, j):
        if t % PLANE == PLANE - 1 and j >= 2:
            return (t + 1, j)
        if t % PLANE == 0 and j < 2:
            return (t - 1, j)
        return None

    return permute(x, route)


def sweep(u_ref, lo, hi, coef, emit):
    cx_ref, mid_ref, cy_ref = coef
    count, n = u_ref.shape[0], u_ref.shape[2]
    prev = u_ref[lo - 1] if lo > 0 else None
    cur = u_ref[lo]
    for x in range(lo, hi + 1):
        nxt = u_ref[x + 1] if x + 1 < count else None
        new = mid_ref[x : x + 1] * cur + (
            cy_ref[0:1] * pltpu.roll(cur, n - 1, 1) + cy_ref[1:2] * pltpu.roll(cur, 1, 1)
        )
        if nxt is not None:
            new = new + cx_ref[x : x + 1] * nxt
        if prev is not None:
            new = new + cx_ref[x - 1 : x] * prev
        emit(x, new)
        prev, cur = cur, nxt


def flat(shape):
    return pl.BlockSpec(shape, lambda i, k: (0,) * len(shape))


def smooth_kernel(_core, ctl_ref, cx_ref, mid_ref, cy_ref, out_ref, u_ref):
    cols = ctl_ref.shape[1]
    zero = jnp.zeros(u_ref.shape[1:], u_ref.dtype)
    for x in range(W):
        u_ref[x] = zero
        u_ref[W + cols + x] = zero
    for x in range(cols):
        u_ref[W + x] = ctl_ref[0, x]

    def keep(x, v):
        u_ref[x] = v

    def give(x, v):
        out_ref[0, x] = v.astype(out_ref.dtype)

    for step in range(1, STEPS + 1):
        emit = keep if step < STEPS else give
        sweep(u_ref, W - step, W + cols - 1 + step, (cx_ref, mid_ref, cy_ref), emit)


def smooth_call(core, control, coef, mine):
    m, cols, lev, cy = control.shape
    half = m // 2
    ext = cols + 2 * W

    def member(i, k):
        return ((k[0] if mine else 1 - k[0]) * half + i, 0, 0, 0)

    return pl.pallas_call(
        smooth_kernel,
        grid_spec=pltpu.PrefetchScalarGridSpec(
            num_scalar_prefetch=1,
            grid=(half,),
            in_specs=[pl.BlockSpec((1, cols, lev, cy), member)] + [flat(c.shape) for c in coef],
            out_specs=pl.BlockSpec((1, ext, lev, cy), lambda i, k: (i, 0, 0, 0)),
            scratch_shapes=[pltpu.VMEM((ext, lev, cy), jnp.float32)],
        ),
        out_shape=jax.ShapeDtypeStruct((half, ext, lev, cy), jnp.bfloat16),
        compiler_params=pltpu.CompilerParams(vmem_limit_bytes=32 * 2**20),
        cost_estimate=COST,
        name="smooth",
    )(core, control, *coef)


VMEM = pl.BlockSpec(memory_space=pltpu.VMEM)


def message_kernel(values_ref, cells_ref, counts_ref, out_ref):
    cap, lev, rows = values_ref.shape
    lanes = out_ref.shape[1]
    per = lanes // lev
    groups = cap // per
    counts = counts_ref[...]
    for k in range(groups):
        part = [jnp.where(k * per + a < counts, values_ref[k * per + a], jnp.float32(0.0)) for a in range(per)]
        out_ref[pl.ds(k, rows, stride=groups + 1), :] = jnp.concatenate(part, 0).T
    cells = jnp.concatenate([cells_ref[...].astype(jnp.float32), jnp.zeros((lanes - cap, rows), jnp.float32)], 0)
    out_ref[pl.ds(groups, rows, stride=groups + 1), :] = cells.T


def message_call(values, cells, counts, lanes):
    cap, lev, rows = values.shape
    return pl.pallas_call(
        message_kernel,
        out_shape=jax.ShapeDtypeStruct((rows * (cap * lev // lanes + 1), lanes), jnp.float32),
        in_specs=[VMEM] * 3,
        out_specs=VMEM,
        compiler_params=pltpu.CompilerParams(vmem_limit_bytes=16 * 2**20),
        cost_estimate=COST,
        name="message",
    )(values, cells, counts)


def scatter_kernel(cap, got_ref, out_ref):
    cols, lev, cy = out_ref.shape
    lanes = got_ref.shape[1]
    per = lanes // lev
    groups = cap // per
    senders = got_ref.shape[0] // (groups + 1)
    vals = jnp.concatenate([got_ref[pl.ds(k, senders, stride=groups + 1), :] for k in range(groups)], 0)
    cells = got_ref[pl.ds(groups, senders, stride=groups + 1), :]
    rows = vals.shape[0]
    vt = vals.T
    high = vt.astype(jnp.bfloat16)
    low = (vt - high.astype(jnp.float32)).astype(jnp.bfloat16)
    lane = lax.broadcasted_iota(jnp.int32, (rows, cy), 1)
    total = [jnp.zeros((2 * lev, cy), jnp.float32) for _ in range(cols)]
    for a in range(per):
        part = slice(a * lev, (a + 1) * lev)
        both = jnp.concatenate([high[part], low[part]], 0)
        at = jnp.concatenate([cells[:, k * per + a : k * per + a + 1] for k in range(groups)], 0)
        cell = jnp.broadcast_to(at, (rows, cy)).astype(jnp.int32) - lane
        for x in range(cols):
            hot = jnp.where(cell == x * cy, jnp.float32(1), jnp.float32(0)).astype(jnp.bfloat16)
            total[x] = total[x] + jnp.dot(both, hot, preferred_element_type=jnp.float32)
    for x in range(cols):
        out_ref[x] = total[x][:lev] + total[x][lev:]


def scatter_call(got, cap, cols, lev, cy):
    return pl.pallas_call(
        functools.partial(scatter_kernel, cap),
        out_shape=jax.ShapeDtypeStruct((cols, lev, cy), jnp.float32),
        in_specs=[VMEM],
        out_specs=VMEM,
        compiler_params=pltpu.CompilerParams(vmem_limit_bytes=32 * 2**20),
        cost_estimate=COST,
        name="scatter",
    )(got)


def order_kernel(j_ref, v_ref, vf_ref, vt_ref, rows_ref):
    lev = v_ref.shape[0] // 4

    def ordered(take):
        return jnp.concatenate([take(pl.ds(pl.multiple_of((j_ref[0] ^ b) * lev, lev), lev)) for b in range(4)], 0)

    rows_ref[...] = v_ref[...].astype(jnp.float32)
    rows_ref[...] = ordered(lambda at: rows_ref[at, :]).T
    turned = ordered(lambda at: rows_ref[at, :])[: 2 * lev]
    vt_ref[...] = turned.astype(vt_ref.dtype)
    vf_ref[...] = turned.T.astype(vf_ref.dtype)


def order_call(j, v):
    n = v.shape[0]
    return pl.pallas_call(
        order_kernel,
        out_shape=[jax.ShapeDtypeStruct((n, n // 2), v.dtype), jax.ShapeDtypeStruct((n // 2, n), v.dtype)],
        in_specs=[pl.BlockSpec(memory_space=pltpu.SMEM), VMEM],
        out_specs=[VMEM, VMEM],
        scratch_shapes=[pltpu.VMEM((n, n), jnp.float32)],
        cost_estimate=COST,
        name="order",
    )(j, v)


def forward_kernel(edges, *refs):
    e_refs, (s0_ref, s1_ref, vf_ref, inc_ref) = refs[:4], refs[4:]
    lev = inc_ref.shape[2]
    count = inc_ref.shape[1]

    @pl.when(pl.program_id(0) == 0)
    def _():
        inc_ref[...] = jnp.zeros(inc_ref.shape, inc_ref.dtype)

    def block(b, x):
        return halo(e_refs, b, x) if edges else e_refs[b][0, x]

    ext = s0_ref.shape[1]
    for x in range(0, count, 2):
        at = [(y if y < W else ext - 2 * W + y) if edges else y + W for y in (x, x + 1)]
        smooth = [jnp.concatenate([s0_ref[0, y], s1_ref[0, y]], 0) for y in at]
        local = jnp.dot(vf_ref[...], jnp.concatenate(smooth, 1), preferred_element_type=jnp.float32)
        width = local.shape[1] // 2
        for i, y in enumerate((x, x + 1)):
            for b in range(4):
                e = block(b, y).astype(jnp.float32)
                inc_ref[b, y] += e * local[b * lev : (b + 1) * lev, i * width : (i + 1) * width]


def halo(refs, b, x):
    return refs[x // W * 2 + b // 2][b % 2, 0, x % W]


def rows_of(array, start):
    return pl.BlockSpec((1,) + array.shape[1:], lambda i, *k: (start + i, 0, 0, 0))


def halo_of(array, start):
    return pl.BlockSpec((array.shape[0], 1) + array.shape[2:], lambda i, *k: (0, start + i, 0, 0, 0))


def forward_call(edges, e, s0, s1, vf):
    members, ext, lev, cy = s0.shape
    count = 2 * W if edges else ext - 2 * W
    spec_of = halo_of if edges else rows_of
    return pl.pallas_call(
        functools.partial(forward_kernel, edges),
        grid=(members,),
        in_specs=[spec_of(x, 0) for x in e] + [rows_of(s0, 0), rows_of(s1, 0), pl.BlockSpec(vf.shape, lambda i: (0, 0))],
        out_specs=pl.BlockSpec((4, count, lev, cy), lambda i: (0, 0, 0, 0)),
        out_shape=jax.ShapeDtypeStruct((4, count, lev, cy), jnp.float32),
        compiler_params=pltpu.CompilerParams(vmem_limit_bytes=32 * 2**20),
        cost_estimate=COST,
        name="edges" if edges else "inner",
    )(*e, s0, s1, vf)


def adjoint_kernel(_core, e0_ref, e1_ref, e2_ref, e3_ref, *refs):
    halos, refs = refs[:4], refs[4:]
    g_ref, vt_ref, cx_ref, mid_ref, cy_ref, ctl_ref = refs[:6]
    grad_ref, other_ref, u_ref = refs[-3:]
    cols, lev, _ = grad_ref.shape[1:]
    ext = cols + 2 * W
    def block(b, x):
        if W <= x < W + cols:
            return (e0_ref, e1_ref, e2_ref, e3_ref)[b][0, x - W]
        return halo(halos, b, x if x < W else x - cols)

    for x in range(0, ext, 2):
        weighted = []
        for y in (x, x + 1):
            weighted.append(
                jnp.concatenate([(block(b, y).astype(jnp.float32) * g_ref[b, y]).astype(jnp.bfloat16) for b in range(4)], 0)
            )
        back = jnp.dot(vt_ref[...], jnp.concatenate(weighted, 1), preferred_element_type=jnp.float32)
        width = back.shape[1] // 2
        for i, y in enumerate((x, x + 1)):
            u_ref[y] = back[:, i * width : (i + 1) * width]

    def keep(x, v):
        u_ref[x] = v

    def give(x, v):
        grad_ref[0, x - W] = ctl_ref[0, x - W] + v[:lev]
        other_ref[0, x - W] = v[lev:]

    for step in range(1, STEPS + 1):
        sweep(u_ref, step, ext - 1 - step, (cx_ref, mid_ref, cy_ref), keep if step < STEPS else give)


def adjoint_call(core, at, c, e, halos, g, vt, coef, control, grad):
    m, cols, lev, cy = control.shape
    half = m // 2
    ext = cols + 2 * W
    mine = pl.BlockSpec((1, cols, lev, cy), lambda i, k: (k[0] * half + at + i, 0, 0, 0))
    in_specs = [rows_of(x, at) for x in e] + [halo_of(x, at) for x in halos]
    in_specs += [flat(g.shape), flat(vt.shape)] + [flat(x.shape) for x in coef] + [mine]
    args = [*e, *halos, g, vt, *coef, control]
    aliases = {}
    if grad is not None:
        in_specs.append(pl.BlockSpec(memory_space=pl.ANY))
        args.append(grad)
        aliases = {len(args): 0}
    return pl.pallas_call(
        adjoint_kernel,
        grid_spec=pltpu.PrefetchScalarGridSpec(
            num_scalar_prefetch=1,
            grid=(c,),
            in_specs=in_specs,
            out_specs=[mine, pl.BlockSpec((1, cols, lev, cy), lambda i, k: (i, 0, 0, 0))],
            scratch_shapes=[pltpu.VMEM((ext, 2 * lev, cy), jnp.float32)],
        ),
        out_shape=[
            jax.ShapeDtypeStruct(control.shape, jnp.float32),
            jax.ShapeDtypeStruct((c, cols, lev, cy), jnp.float32),
        ],
        input_output_aliases=aliases,
        compiler_params=pltpu.CompilerParams(vmem_limit_bytes=40 * 2**20),
        cost_estimate=COST,
        name="adjoint",
    )(core, *args)


def finish_kernel(_core, r_ref, ctl_ref, _grad, out_ref):
    out_ref[...] = ctl_ref[...] + r_ref[...]


def finish_call(core, at, r, control, grad):
    c, cols, lev, cy = r.shape
    half = control.shape[0] // 2
    n = 2 if c % 2 == 0 and at % 2 == 0 and half % 2 == 0 else 1
    theirs = pl.BlockSpec((n, cols, lev, cy), lambda i, k: (((1 - k[0]) * half + at) // n + i, 0, 0, 0))
    return pl.pallas_call(
        finish_kernel,
        grid_spec=pltpu.PrefetchScalarGridSpec(
            num_scalar_prefetch=1,
            grid=(c // n,),
            in_specs=[pl.BlockSpec((n, cols, lev, cy), lambda i, k: (i, 0, 0, 0)), theirs, pl.BlockSpec(memory_space=pl.ANY)],
            out_specs=theirs,
        ),
        out_shape=jax.ShapeDtypeStruct(control.shape, jnp.float32),
        input_output_aliases={3: 0},
        compiler_params=pltpu.CompilerParams(vmem_limit_bytes=16 * 2**20),
        cost_estimate=COST,
        name="finish",
    )(core, r, control, grad)


def after(x, *first):
    return lax.optimization_barrier((x, first))[0]


def local(control, ensemble, coupling_x, coupling_y, vertical_loc, obs_cells, obs_counts, obs_values):
    m, lev, cols, cy = control.shape
    rows, cap = obs_cells.shape
    half = m // 2
    tile, j = lax.axis_index("tile"), lax.axis_index("lev")
    core, chip = j % 2, j // 2
    even = tile % 2 == 0
    low_edge, high_edge = tile % PLANE == 0, tile % PLANE == PLANE - 1
    facing = (low_edge & (chip == 0)) | (high_edge & (chip == 1))
    served = (low_edge & (chip == 1)) | (high_edge & (chip == 0))
    core_arg = core.astype(jnp.int32).reshape(1)
    control = jnp.transpose(control, (0, 2, 1, 3))
    ens = jnp.transpose(ensemble, (0, 2, 1, 3))

    def top(x):
        return x[:, cols - W :]

    def bottom(x):
        return x[:, :W]

    def payloads(pair):
        return (
            jnp.stack([jnp.where(even, top(x), bottom(x)) for x in pair]),
            jnp.stack([jnp.where(even, bottom(x), top(x)) for x in pair]),
        )

    cx_low, cx_high = beside_tile(even, coupling_x[cols - W :], coupling_x[:W])
    cxe = jnp.concatenate([cx_low, coupling_x, cx_high], 0)
    at_y = lax.broadcasted_iota(jnp.int32, (cy,), 0)
    north = jnp.where(at_y < cy - 1, coupling_y, jnp.float32(0.0))
    south = jnp.where(at_y > 0, jnp.roll(coupling_y, 1), jnp.float32(0.0))
    cxe_before = jnp.concatenate([cxe[:1], cxe[:-1]], 0)
    coef = (cxe, (1.0 - north - south) - (cxe + cxe_before), jnp.stack([north, south]))

    other = jnp.where(core == 0, ens[half:], ens[:half])
    mine = jnp.where(core == 0, ens[:half], ens[half:])
    beside = flip_core(other)
    far_mine, far_beside = flip_chip(mine), flip_chip(beside)
    own_send = payloads((mine, beside))
    own_first, own_second = swap_first(own_send[0]), swap_second_near(own_send[1])

    message = message_call(
        jnp.transpose(obs_values, (1, 2, 0)), after(obs_cells.T, own_send), obs_counts[None], 128
    )
    got = lax.all_to_all(message.reshape(rows, -1), "tile", split_axis=0, concat_axis=0, tiled=True)

    vf, vt = order_call(j.astype(jnp.int32).reshape(1), vertical_loc)

    smooth_send = smooth_call(core_arg, after(control, message, vf), coef, False)
    s1 = flip_core(smooth_send)
    s0 = smooth_call(core_arg, after(control, smooth_send), coef, True)

    relayed = relay(after(own_second, s0))
    got = after(got, s0, own_first, own_second, far_mine)
    g_own = scatter_call(got.reshape(message.shape), cap, cols, lev, cy)
    g_raw = g_own
    g_low, g_high = beside_tile(even, g_own[cols - W :], g_own[:W])
    g_own = jnp.concatenate([g_low, after(g_own, s1), g_high], 0)
    g_far = flip_chip(g_own)
    g_beside = flip_core(jnp.stack([g_own, g_far]))
    g = jnp.stack([g_own, g_beside[0], g_far, g_beside[1]])

    far_send = payloads((far_mine, after(far_beside, g_raw)))
    far_first = swap_first(far_send[0])
    far_second = swap_second_near(far_send[1])
    reached = reach(after(far_send[1], g_own))
    e = [mine, beside, far_mine, after(far_beside, far_send)]
    inner = forward_call(False, e, s0, s1, vf)

    own_outer = jnp.where(served, relayed, jnp.where(facing, far_second, own_second))
    far_outer = jnp.where(served, reached, jnp.where(facing, own_second, far_second))
    halos = [
        jnp.where(even, own_outer, own_first),
        jnp.where(even, far_outer, far_first),
        jnp.where(even, own_first, own_outer),
        jnp.where(even, far_first, far_outer),
    ]
    edges = forward_call(True, halos, s0, after(s1, inner), vf)
    def over_cores(part):
        return part[::2] + flip_core(part[1::2])

    def over_chips(pair):
        return pair[0] + flip_chip(pair[1])

    def adjoint(n, grad, *first):
        at, c = plan[n]
        return adjoint_call(core_arg, at, c, e, halos, after(g, first), vt, coef, control, grad)

    plan = chunks_of(half)
    inner = over_chips(over_cores(inner))
    grad, r = adjoint(0, None, edges)
    returned = [flip_core(r)]
    edges = over_chips(over_cores(edges))
    grad, r = adjoint(1, grad)
    returned.append(flip_core(r))
    edge_low, edge_high = beside_tile(even, edges[W:], edges[:W])
    grad = finish_call(core_arg, plan[0][0], returned[0], control, grad)
    grad, r = adjoint(2, grad, edges)
    returned.append(flip_core(r))
    for n in (1, 2):
        grad = finish_call(core_arg, plan[n][0], returned[n], control, grad)
    inc = jnp.concatenate([inner[:W] + edge_low, inner[W : cols - W], inner[cols - W :] + edge_high], 0)
    return jnp.transpose(inc, (1, 0, 2)), jnp.transpose(grad, (0, 2, 1, 3))


def solution(mesh):
    placed = (
        P(None, "lev", "tile", None),
        P(None, "lev", "tile", None),
        P("tile", None),
        P(),
        P(),
        P("tile", None),
        P("tile"),
        P("tile", None, "lev"),
    )
    return jax.shard_map(
        local,
        mesh=mesh,
        in_specs=placed,
        out_specs=(P("lev", "tile", None), P(None, "lev", "tile", None)),
        check_vma=False,
    )
```

time: 248 us -> 171 us (0.69)
  waiting for transfers between devices: 84.1 us -> 36.1 us
  Pallas kernels: 74.3 us -> 50.8 us
  starting transfers between devices: 62.1 us -> 58.4 us
    ppermute x22 -> x25, waiting for transfers between devices: 76.9 us -> 36.1 us  [permute(): return lax.ppermute(x, ('tile', 'lev'), pairs)]
    pallas_call x1 -> x2, Pallas kernels: 33.4 us -> 13.5 us  [smooth_call(): pl.pallas_call(smooth_kernel, grid_spec=pltpu.PrefetchScalarGridSpec(num_...]
    all_to_all x1, waiting for transfers between devices: 7.19 us -> 0.01 us  [local(): lax.all_to_all(message.reshape(rows, -1), 'tile', split_axis=0, concat_ax...]
    all_to_all x1, starting transfers between devices: 14 us -> 6.92 us  [local(): lax.all_to_all(message.reshape(rows, -1), 'tile', split_axis=0, concat_ax...]
    another operation x3 -> x11, other arithmetic: 1.3 us -> 6.44 us  [the longest x6 3.82 us: payloads(): jnp.stack([jnp.where(even, bottom(x), top(x)) for x in pair])]
    concatenate x8 -> x1, other arithmetic: 3.82 us -> 0.01 us  [local(): cxe = jnp.concatenate([cx_low, coupling_x, cx_high], 0)]
    ppermute x22 -> x25, starting transfers between devices: 48.2 us -> 51.5 us  [permute(): return lax.ppermute(x, ('tile', 'lev'), pairs)]
    unnamed x39 -> x27, local copies, waits for them, and re-layouts: 4.88 us -> 7.41 us
  transfers between devices with their start and end apart: 23 -> 26, of which waited for: 9 -> 6; matrix products, arithmetic and copies ran while one was open for 8% -> 10% of each run, Pallas kernels for 16% -> 29%
where the time goes in v2:
time: 171 us; the launch traced here: 170 us
  starting transfers between devices  58.4 us (34%)
  Pallas kernels  50.8 us (30%)
  waiting for transfers between devices  36.1 us (21%)
  other arithmetic  14.5 us (8%)
  local copies, waits for them, and re-layouts  9.09 us (5%)
    ppermute x25, starting transfers between devices, permute(): return lax.ppermute(x, ('tile', 'lev'), pairs)  51.5 us
    ppermute x25, waiting for transfers between devices, permute(): return lax.ppermute(x, ('tile', 'lev'), pairs)  36.1 us
    pallas_call x3, Pallas kernels, adjoint_call(): pl.pallas_call(adjoint_kernel, grid_spec=pltpu.PrefetchScalarGridSpec(num...  18.1 us
    pallas_call x2, Pallas kernels, smooth_call(): pl.pallas_call(smooth_kernel, grid_spec=pltpu.PrefetchScalarGridSpec(num_...  13.5 us
    pallas_call x2, Pallas kernels, forward_call(): pl.pallas_call(functools.partial(forward_kernel, edges), grid=(members,),...  12.8 us
    unnamed x27, local copies, waits for them, and re-layouts  7.41 us
    all_to_all x1, starting transfers between devices, local(): lax.all_to_all(message.reshape(rows, -1), 'tile', split_axis=0, concat_ax...  6.92 us
    another operation x6, other arithmetic, payloads(): jnp.stack([jnp.where(even, bottom(x), top(x)) for x in pair])  3.82 us
  transfers between devices with their start and end apart: 26, of which 6 were waited for; matrix products, arithmetic and copies ran while one was open for 10% of the time, Pallas kernels for 29%

profile of v2, /device:TPU:1, one launch (start us, length us, event | category | flops | bytes accessed | tf_op | source)
XLA Modules:
  0.0 169.9 jit_solution(7454706721048041656)
XLA Ops:
  1.4 11.5 %collective-permute-start.3 = (f32[4,128]{1,0:T(4,128)S(1)}, f32[4,128]{1,0:T(4,128)S(1)}, u32[]{:S(2)}, u32[]{:S(2)}) collective-permute-start(f32[4,128]{1,0:T(4,128)S(1)} %get-tuple-element.71), channel_id=1, source_target_pairs={{0,252},{1,253},{2,254},{3,255},{4,8},{5,9},{6,10},{7,11},{8,4},{9... | collective-permute-start | bytes 6152 | tf_op jit(solution)/shard_map/ppermute | solution.py:34
  12.9 2.6 %broadcast_select_fusion = (bf16[10,12,32,128]{3,2,1,0:T(8,128)(2,1)}, bf16[10,12,32,128]{3,2,1,0:T(8,128)(2,1)S(1)}) fusion(pred[]{:T(512)S(6)} %eq.26, bf16[20,12,32,128]{3,2,1,0:T(8,128)(2,1)} %bitcast.64), kind=kLoop, calls=%fused_computation.1 | loop fusion | flops 983040 | bytes 3932161 | tf_op jit(solution)/shard_map/jit(_where)/select_n | solution.py:431
  25.2 1.9 %collective-permute-start.6 = (bf16[2,10,4,32,128]{4,3,2,1,0:T(8,128)(2,1)}, bf16[2,10,4,32,128]{4,3,2,1,0:T(8,128)(2,1)}, u32[]{:S(2)}, u32[]{:S(2)}) collective-permute-start(bf16[2,10,4,32,128]{4,3,2,1,0:T(8,128)(2,1)} %pad_maximum_fusion.2), channel_id=1, source_target_pairs={{0,254},{1,255},{4,8},{5,9},{6,10},{7,11},{8,4},{9,5},{10,6},{11,7... | collective-permute-start | bytes 1966088 | tf_op jit(solution)/shard_map/ppermute | solution.py:34
  28.2 6.9 %all-to-all-start = ((f32[64,1,1152]{2,1,0:T(1,128)}), f32[64,1,1152]{2,1,0:T(1,128)S(1)}, u32[]{:S(2)}, u32[]{:S(2)}) async-start(f32[64,1,1152]{2,1,0:T(1,128)} %bitcast.9), calls=%async_computation | async-start | bytes 589824 | tf_op jit(solution)/shard_map/all_to_all | solution.py:441
  35.1 2.1 %copy-done = f32[20,32,12,128]{3,1,2,0:T(8,128)S(1)} copy-done((f32[20,32,12,128]{3,1,2,0:T(8,128)S(1)}, f32[20,32,12,128]{3,1,2,0:T(8,128)}, u32[]{:S(2)}) %copy-start) | copy-done | bytes 3932184
  37.2 7.1 %smooth.2 = bf16[10,20,32,128]{3,2,1,0:T(8,128)(2,1)} custom-call(s32[1]{0:T(128)} %bitcast.10._core, f32[20,12,32,128]{3,2,1,0:T(8,128)S(1)} %bitcast.51, f32[20,128]{1,0:T(8,128)S(1)} %pad_maximum_fusion.7.cx_ref.refs_6_, f32[20,128]{1,0:T(8,128)S(1)} %fusion.2.mid_ref.refs_7_, f32[2,128]{1,0:T(2,128)S(1)} %pad_maximum_fusion.8.cy_ref.refs_8_), custom_call_target="tpu_custom_call" | custom-call | flops 1 | bytes 1 | tf_op jit(solution)/shard_map/smooth/pallas_call | solution.py:141
  45.5 3.4 %collective-permute-start.2 = (bf16[10,12,32,128]{3,2,1,0:T(8,128)(2,1)S(1)}, bf16[10,12,32,128]{3,2,1,0:T(8,128)(2,1)}, u32[]{:S(2)}, u32[]{:S(2)}) collective-permute-start(bf16[10,12,32,128]{3,2,1,0:T(8,128)(2,1)S(1)} %collective-permute-done.refs_1_.e1_ref), channel_id=1, source_target_pairs={{0,2},{1,3},{2,0},{3,1},{4,6},{5,7},{6,4},{7,5},{8,10},{9,11},{10,... | collective-permute-start | bytes 2949128 | tf_op jit(solution)/shard_map/ppermute | solution.py:34
  48.9 6.3 %smooth.3.refs_4_ = bf16[10,20,32,128]{3,2,1,0:T(8,128)(2,1)S(1)} custom-call(s32[1]{0:T(128)} %bitcast.10._core, f32[20,12,32,128]{3,2,1,0:T(8,128)S(1)} %bitcast.52, f32[20,128]{1,0:T(8,128)S(1)} %pad_maximum_fusion.7.cx_ref.refs_6_, f32[20,128]{1,0:T(8,128)S(1)} %fusion.2.mid_ref.refs_7_, f32[2,128]{1,0:T(2,128)S(1)} %pad_maximum_fusion.8.cy_ref.refs_8_), custom_call_target="tpu_custom_call" | custom-call | flops 1 | bytes 1 | tf_op jit(solution)/shard_map/smooth/pallas_call | solution.py:141
  59.5 8.0 %collective-permute-start.12 = (f32[4,32,128]{2,1,0:T(8,128)S(1)}, f32[4,32,128]{2,1,0:T(8,128)S(1)}, u32[]{:S(2)}, u32[]{:S(2)}) collective-permute-start(f32[4,32,128]{2,1,0:T(8,128)S(1)} %get-tuple-element.65), channel_id=1, source_target_pairs={{0,252},{1,253},{2,254},{3,255},{4,8},{5,9},{6,10},{7,11},{8,4},{9... | collective-permute-start | bytes 196616 | tf_op jit(solution)/shard_map/ppermute | solution.py:34
  67.6 2.8 %collective-permute-start.10 = (bf16[2,10,4,32,128]{4,3,2,1,0:T(8,128)(2,1)}, bf16[2,10,4,32,128]{4,3,2,1,0:T(8,128)(2,1)}, u32[]{:S(2)}, u32[]{:S(2)}) collective-permute-start(bf16[2,10,4,32,128]{4,3,2,1,0:T(8,128)(2,1)} %collective-permute-done.6), channel_id=1, source_target_pairs={{0,2},{1,3},{62,60},{63,61},{64,66},{65,67},{126,124},{127,125},{1... | collective-permute-start | bytes 1966088 | tf_op jit(solution)/shard_map/ppermute | solution.py:34
  70.4 11.2 %collective-permute-done.12 = f32[4,32,128]{2,1,0:T(8,128)S(1)} collective-permute-done((f32[4,32,128]{2,1,0:T(8,128)S(1)}, f32[4,32,128]{2,1,0:T(8,128)S(1)}, u32[]{:S(2)}, u32[]{:S(2)}) %collective-permute-start.12) | collective-permute-done | bytes 65568 | tf_op jit(solution)/shard_map/ppermute | solution.py:34
  84.6 1.9 %collective-permute-start.11 = (bf16[2,10,4,32,128]{4,3,2,1,0:T(8,128)(2,1)}, bf16[2,10,4,32,128]{4,3,2,1,0:T(8,128)(2,1)}, u32[]{:S(2)}, u32[]{:S(2)}) collective-permute-start(bf16[2,10,4,32,128]{4,3,2,1,0:T(8,128)(2,1)} %pad_maximum_fusion.4), channel_id=1, source_target_pairs={{0,254},{1,255},{4,8},{5,9},{6,10},{7,11},{8,4},{9,5},{10,6},{11,7... | collective-permute-start | bytes 1966088 | tf_op jit(solution)/shard_map/ppermute | solution.py:34
  87.3 2.1 %collective-permute-start.14 = (bf16[2,10,4,32,128]{4,3,2,1,0:T(8,128)(2,1)}, bf16[2,10,4,32,128]{4,3,2,1,0:T(8,128)(2,1)}, u32[]{:S(2)}, u32[]{:S(2)}) collective-permute-start(bf16[2,10,4,32,128]{4,3,2,1,0:T(8,128)(2,1)} %pad_maximum_fusion.4), channel_id=1, source_target_pairs={{0,252},{1,253},{62,66},{63,67},{64,60},{65,61},{126,130},{127,131... | collective-permute-start | bytes 1966088 | tf_op jit(solution)/shard_map/ppermute | solution.py:34
  90.9 6.5 %inner.1 = f32[4,12,32,128]{3,2,1,0:T(8,128)S(1)} custom-call(bf16[10,12,32,128]{3,2,1,0:T(8,128)(2,1)S(1)} %get-tuple-element.47.refs_0_.e0_ref, bf16[10,12,32,128]{3,2,1,0:T(8,128)(2,1)S(1)} %collective-permute-done.refs_1_.e1_ref, bf16[10,12,32,128]{3,2,1,0:T(8,128)(2,1)S(1)} %collective-permute-done.1.refs_2_.e2_ref, ...), custom_call_target="tpu_custom_call" | custom-call | flops 1 | bytes 1 | tf_op jit(solution)/shard_map/inner/pallas_call | solution.py:290
  99.5 8.2 %collective-permute-done.11 = bf16[2,10,4,32,128]{4,3,2,1,0:T(8,128)(2,1)} collective-permute-done((bf16[2,10,4,32,128]{4,3,2,1,0:T(8,128)(2,1)}, bf16[2,10,4,32,128]{4,3,2,1,0:T(8,128)(2,1)}, u32[]{:S(2)}, u32[]{:S(2)}) %collective-permute-start.11) | collective-permute-done | bytes 655392 | tf_op jit(solution)/shard_map/ppermute | solution.py:34
  107.7 6.7 %collective-permute-done.14 = bf16[2,10,4,32,128]{4,3,2,1,0:T(8,128)(2,1)} collective-permute-done((bf16[2,10,4,32,128]{4,3,2,1,0:T(8,128)(2,1)}, bf16[2,10,4,32,128]{4,3,2,1,0:T(8,128)(2,1)}, u32[]{:S(2)}, u32[]{:S(2)}) %collective-permute-start.14) | collective-permute-done | bytes 655392 | tf_op jit(solution)/shard_map/ppermute | solution.py:34
  114.4 1.9 %broadcast_select_fusion.2 = (bf16[2,10,4,32,128]{4,3,2,1,0:T(8,128)(2,1)S(1)}, bf16[2,10,4,32,128]{4,3,2,1,0:T(8,128)(2,1)S(1)}, bf16[2,10,4,32,128]{4,3,2,1,0:T(8,128)(2,1)S(1)}, bf16[2,10,4,32,128]{4,3,2,1,0:T(8,128)(2,1)S(1)}) fusion(bf16[2,10,4,32,128]{4,3,2,1,0:T(8,128)(2,1)} %collective-permute-done.15, pred[]{:T(512)S(6)} %eq.27, ...), kind=kLoop, calls=%fused_computation.10 | loop fusion | flops 1966080 | bytes 6553603 | tf_op jit(solution)/shard_map/jit(_where)/select_n | solution.py:472
  116.6 6.2 %edges.1 = f32[4,8,32,128]{3,2,1,0:T(8,128)S(1)} custom-call(bf16[2,10,4,32,128]{4,3,2,1,0:T(8,128)(2,1)S(1)} %get-tuple-element.80.refs_0_, bf16[2,10,4,32,128]{4,3,2,1,0:T(8,128)(2,1)S(1)} %get-tuple-element.79.refs_1_, bf16[2,10,4,32,128]{4,3,2,1,0:T(8,128)(2,1)S(1)} %get-tuple-element.48.refs_2_, ...), custom_call_target="tpu_custom_call" | custom-call | flops 1 | bytes 1 | tf_op jit(solution)/shard_map/edges/pallas_call | solution.py:290
  125.5 9.3 %collective-permute-start.17 = (f32[8,32,128]{2,1,0:T(8,128)S(1)}, f32[8,32,128]{2,1,0:T(8,128)S(1)}, u32[]{:S(2)}, u32[]{:S(2)}) collective-permute-start(f32[8,32,128]{2,1,0:T(8,128)S(1)} %slice_bitcast_fusion.2), channel_id=1, source_target_pairs={{0,2},{1,3},{2,0},{3,1},{4,6},{5,7},{6,4},{7,5},{8,10},{9,11},{10,... | collective-permute-start | bytes 393224 | tf_op jit(solution)/shard_map/ppermute | solution.py:34
  135.0 1.9 %copy-done.1 = f32[20,32,12,128]{3,1,2,0:T(8,128)S(1)} copy-done((f32[20,32,12,128]{3,1,2,0:T(8,128)S(1)}, f32[20,32,12,128]{3,1,2,0:T(8,128)}, u32[]{:S(2)}) %copy-start.1) | copy-done | bytes 3932184
  136.9 4.2 %adjoint.3 = (f32[20,12,32,128]{3,2,1,0:T(8,128)}, f32[2,12,32,128]{3,2,1,0:T(8,128)S(1)}) custom-call(s32[1]{0:T(128)} %bitcast.10._core, bf16[10,12,32,128]{3,2,1,0:T(8,128)(2,1)S(1)} %get-tuple-element.47.refs_0_.e0_ref, bf16[10,12,32,128]{3,2,1,0:T(8,128)(2,1)S(1)} %collective-permute-done.refs_1_.e1_ref, ...), custom_call_target="tpu_custom_call" | custom-call | flops 1 | bytes 1 | tf_op jit(solution)/shard_map/adjoint/pallas_call | solution.py:348
  142.4 6.9 %adjoint.4 = (f32[20,12,32,128]{3,2,1,0:T(8,128)}, f32[4,12,32,128]{3,2,1,0:T(8,128)S(1)}) custom-call(s32[1]{0:T(128)} %bitcast.10._core, bf16[10,12,32,128]{3,2,1,0:T(8,128)(2,1)S(1)} %get-tuple-element.47.refs_0_.e0_ref, bf16[10,12,32,128]{3,2,1,0:T(8,128)(2,1)S(1)} %collective-permute-done.refs_1_.e1_ref, ...), custom_call_target="tpu_custom_call", output_to_operand_aliasing={{0}: (15, {})} | custom-call | flops 1 | bytes 1 | tf_op jit(solution)/shard_map/adjoint/pallas_call | solution.py:348
  150.7 6.9 %adjoint.5 = (f32[20,12,32,128]{3,2,1,0:T(8,128)}, f32[4,12,32,128]{3,2,1,0:T(8,128)S(1)}) custom-call(s32[1]{0:T(128)} %bitcast.10._core, bf16[10,12,32,128]{3,2,1,0:T(8,128)(2,1)S(1)} %get-tuple-element.47.refs_0_.e0_ref, bf16[10,12,32,128]{3,2,1,0:T(8,128)(2,1)S(1)} %collective-permute-done.refs_1_.e1_ref, ...), custom_call_target="tpu_custom_call", output_to_operand_aliasing={{0}: (15, {})} | custom-call | flops 1 | bytes 1 | tf_op jit(solution)/shard_map/adjoint/pallas_call | solution.py:348
  159.3 8.1 %collective-permute-done.18 = f32[4,32,128]{2,1,0:T(8,128)S(1)} collective-permute-done((f32[4,32,128]{2,1,0:T(8,128)S(1)}, f32[4,32,128]{2,1,0:T(8,128)S(1)}, u32[]{:S(2)}, u32[]{:S(2)}) %collective-permute-start.18) | collective-permute-done | bytes 65568 | tf_op jit(solution)/shard_map/ppermute | solution.py:34
  (107 shorter events, 34.0 us)
Async XLA Ops:
  1.4 20.2 %collective-permute-start.3 = (f32[4,128]{1,0:T(4,128)S(1)}, f32[4,128]{1,0:T(4,128)S(1)}, u32[]{:S(2)}, u32[]{:S(2)}) collective-permute-start(f32[4,128]{1,0:T(4,128)S(1)} %get-tuple-element.71), channel_id=1, source_target_pairs={{0,252},{1,253},{2,254},{3,255},{4,8},{5,9},{6,10},{7,11},{8,4},{9... | collective-permute-start | bytes 6152 | tf_op jit(solution)/shard_map/ppermute | solution.py:34
  12.8 8.7 %collective-permute-start.4 = (f32[4,128]{1,0:T(4,128)S(1)}, f32[4,128]{1,0:T(4,128)S(1)}, u32[]{:S(2)}, u32[]{:S(2)}) collective-permute-start(f32[4,128]{1,0:T(4,128)S(1)} %get-tuple-element.72), channel_id=1, source_target_pairs={{0,4},{1,5},{2,6},{3,7},{4,0},{5,1},{6,2},{7,3},{8,12},{9,13},{10,... | collective-permute-start | bytes 6152 | tf_op jit(solution)/shard_map/ppermute | solution.py:34
  16.4 40.8 %collective-permute-start.1 = (bf16[10,12,32,128]{3,2,1,0:T(8,128)(2,1)S(1)}, bf16[10,12,32,128]{3,2,1,0:T(8,128)(2,1)S(1)}, u32[]{:S(2)}, u32[]{:S(2)}) collective-permute-start(bf16[10,12,32,128]{3,2,1,0:T(8,128)(2,1)S(1)} %get-tuple-element.47.refs_0_.e0_ref), channel_id=1, source_target_pairs={{0,2},{1,3},{2,0},{3,1},{4,6},{5,7},{6,4},{7,5},{8,10},{9,11},{10,... | collective-permute-start | bytes 2949128 | tf_op jit(solution)/shard_map/ppermute | solution.py:34
  22.6 34.6 %collective-permute-start.5 = (bf16[2,10,4,32,128]{4,3,2,1,0:T(8,128)(2,1)}, bf16[2,10,4,32,128]{4,3,2,1,0:T(8,128)(2,1)}, u32[]{:S(2)}, u32[]{:S(2)}) collective-permute-start(bf16[2,10,4,32,128]{4,3,2,1,0:T(8,128)(2,1)} %pad_maximum_fusion.1), channel_id=1, source_target_pairs={{0,4},{1,5},{2,6},{3,7},{4,0},{5,1},{6,2},{7,3},{8,12},{9,13},{10,... | collective-permute-start | bytes 1966088 | tf_op jit(solution)/shard_map/ppermute | solution.py:34
  25.2 31.9 %collective-permute-start.6 = (bf16[2,10,4,32,128]{4,3,2,1,0:T(8,128)(2,1)}, bf16[2,10,4,32,128]{4,3,2,1,0:T(8,128)(2,1)}, u32[]{:S(2)}, u32[]{:S(2)}) collective-permute-start(bf16[2,10,4,32,128]{4,3,2,1,0:T(8,128)(2,1)} %pad_maximum_fusion.2), channel_id=1, source_target_pairs={{0,254},{1,255},{4,8},{5,9},{6,10},{7,11},{8,4},{9,5},{10,6},{11,7... | collective-permute-start | bytes 1966088 | tf_op jit(solution)/shard_map/ppermute | solution.py:34
  28.2 28.3 %all-to-all-start = ((f32[64,1,1152]{2,1,0:T(1,128)}), f32[64,1,1152]{2,1,0:T(1,128)S(1)}, u32[]{:S(2)}, u32[]{:S(2)}) async-start(f32[64,1,1152]{2,1,0:T(1,128)} %bitcast.9), calls=%async_computation | async-start | bytes 589824 | tf_op jit(solution)/shard_map/all_to_all | solution.py:441
  44.3 42.2 %collective-permute-start.7 = (bf16[10,20,32,128]{3,2,1,0:T(8,128)(2,1)}, bf16[10,20,32,128]{3,2,1,0:T(8,128)(2,1)}, u32[]{:S(2)}, u32[]{:S(2)}) collective-permute-start(bf16[10,20,32,128]{3,2,1,0:T(8,128)(2,1)} %smooth.2), channel_id=1, source_target_pairs={{0,1},{1,0},{2,3},{3,2},{4,5},{5,4},{6,7},{7,6},{8,9},{9,8},{10,11... | collective-permute-start | bytes 4915208 | tf_op jit(solution)/shard_map/ppermute | solution.py:34
  45.5 36.1 %collective-permute-start.2 = (bf16[10,12,32,128]{3,2,1,0:T(8,128)(2,1)S(1)}, bf16[10,12,32,128]{3,2,1,0:T(8,128)(2,1)}, u32[]{:S(2)}, u32[]{:S(2)}) collective-permute-start(bf16[10,12,32,128]{3,2,1,0:T(8,128)(2,1)S(1)} %collective-permute-done.refs_1_.e1_ref), channel_id=1, source_target_pairs={{0,2},{1,3},{2,0},{3,1},{4,6},{5,7},{6,4},{7,5},{8,10},{9,11},{10,... | collective-permute-start | bytes 2949128 | tf_op jit(solution)/shard_map/ppermute | solution.py:34
  59.5 22.0 %collective-permute-start.12 = (f32[4,32,128]{2,1,0:T(8,128)S(1)}, f32[4,32,128]{2,1,0:T(8,128)S(1)}, u32[]{:S(2)}, u32[]{:S(2)}) collective-permute-start(f32[4,32,128]{2,1,0:T(8,128)S(1)} %get-tuple-element.65), channel_id=1, source_target_pairs={{0,252},{1,253},{2,254},{3,255},{4,8},{5,9},{6,10},{7,11},{8,4},{9... | collective-permute-start | bytes 196616 | tf_op jit(solution)/shard_map/ppermute | solution.py:34
  67.5 14.0 %collective-permute-start.13 = (f32[4,32,128]{2,1,0:T(8,128)S(1)}, f32[4,32,128]{2,1,0:T(8,128)S(1)}, u32[]{:S(2)}, u32[]{:S(2)}) collective-permute-start(f32[4,32,128]{2,1,0:T(8,128)S(1)} %get-tuple-element.66), channel_id=1, source_target_pairs={{0,4},{1,5},{2,6},{3,7},{4,0},{5,1},{6,2},{7,3},{8,12},{9,13},{10,... | collective-permute-start | bytes 196616 | tf_op jit(solution)/shard_map/ppermute | solution.py:34
  67.6 29.9 %collective-permute-start.10 = (bf16[2,10,4,32,128]{4,3,2,1,0:T(8,128)(2,1)}, bf16[2,10,4,32,128]{4,3,2,1,0:T(8,128)(2,1)}, u32[]{:S(2)}, u32[]{:S(2)}) collective-permute-start(bf16[2,10,4,32,128]{4,3,2,1,0:T(8,128)(2,1)} %collective-permute-done.6), channel_id=1, source_target_pairs={{0,2},{1,3},{62,60},{63,61},{64,66},{65,67},{126,124},{127,125},{1... | collective-permute-start | bytes 1966088 | tf_op jit(solution)/shard_map/ppermute | solution.py:34
  83.7 15.8 %collective-permute-start.15 = (bf16[2,10,4,32,128]{4,3,2,1,0:T(8,128)(2,1)}, bf16[2,10,4,32,128]{4,3,2,1,0:T(8,128)(2,1)}, u32[]{:S(2)}, u32[]{:S(2)}) collective-permute-start(bf16[2,10,4,32,128]{4,3,2,1,0:T(8,128)(2,1)} %pad_maximum_fusion.3), channel_id=1, source_target_pairs={{0,4},{1,5},{2,6},{3,7},{4,0},{5,1},{6,2},{7,3},{8,12},{9,13},{10,... | collective-permute-start | bytes 1966088 | tf_op jit(solution)/shard_map/ppermute | solution.py:34
  84.6 23.1 %collective-permute-start.11 = (bf16[2,10,4,32,128]{4,3,2,1,0:T(8,128)(2,1)}, bf16[2,10,4,32,128]{4,3,2,1,0:T(8,128)(2,1)}, u32[]{:S(2)}, u32[]{:S(2)}) collective-permute-start(bf16[2,10,4,32,128]{4,3,2,1,0:T(8,128)(2,1)} %pad_maximum_fusion.4), channel_id=1, source_target_pairs={{0,254},{1,255},{4,8},{5,9},{6,10},{7,11},{8,4},{9,5},{10,6},{11,7... | collective-permute-start | bytes 1966088 | tf_op jit(solution)/shard_map/ppermute | solution.py:34
  87.3 27.1 %collective-permute-start.14 = (bf16[2,10,4,32,128]{4,3,2,1,0:T(8,128)(2,1)}, bf16[2,10,4,32,128]{4,3,2,1,0:T(8,128)(2,1)}, u32[]{:S(2)}, u32[]{:S(2)}) collective-permute-start(bf16[2,10,4,32,128]{4,3,2,1,0:T(8,128)(2,1)} %pad_maximum_fusion.4), channel_id=1, source_target_pairs={{0,252},{1,253},{62,66},{63,67},{64,60},{65,61},{126,130},{127,131... | collective-permute-start | bytes 1966088 | tf_op jit(solution)/shard_map/ppermute | solution.py:34
  89.5 34.9 %collective-permute-start.20 = (f32[20,32,128]{2,1,0:T(8,128)S(1)}, f32[20,32,128]{2,1,0:T(8,128)S(1)}, u32[]{:S(2)}, u32[]{:S(2)}) collective-permute-start(f32[20,32,128]{2,1,0:T(8,128)S(1)} %get-tuple-element.61), channel_id=1, source_target_pairs={{0,2},{1,3},{2,0},{3,1},{4,6},{5,7},{6,4},{7,5},{8,10},{9,11},{10,... | collective-permute-start | bytes 983048 | tf_op jit(solution)/shard_map/ppermute | solution.py:34
  97.5 27.0 %collective-permute-start.8 = (f32[2,12,32,128]{3,2,1,0:T(8,128)S(1)}, f32[2,12,32,128]{3,2,1,0:T(8,128)S(1)}, u32[]{:S(2)}, u32[]{:S(2)}) collective-permute-start(f32[2,12,32,128]{3,2,1,0:T(8,128)S(1)} %slice.128), channel_id=1, source_target_pairs={{0,1},{1,0},{2,3},{3,2},{4,5},{5,4},{6,7},{7,6},{8,9},{9,8},{10,11... | collective-permute-start | bytes 1179656 | tf_op jit(solution)/shard_map/ppermute | solution.py:34
  124.4 10.5 %collective-permute-start.21 = (f32[2,20,32,128]{3,2,1,0:T(8,128)S(1)}, f32[2,20,32,128]{3,2,1,0:T(8,128)S(1)}, u32[]{:S(2)}, u32[]{:S(2)}) collective-permute-start(f32[2,20,32,128]{3,2,1,0:T(8,128)S(1)} %pad_maximum_fusion.5), channel_id=1, source_target_pairs={{0,1},{1,0},{2,3},{3,2},{4,5},{5,4},{6,7},{7,6},{8,9},{9,8},{10,11... | collective-permute-start | bytes 1966088 | tf_op jit(solution)/shard_map/ppermute | solution.py:34
  125.5 24.4 %collective-permute-start.17 = (f32[8,32,128]{2,1,0:T(8,128)S(1)}, f32[8,32,128]{2,1,0:T(8,128)S(1)}, u32[]{:S(2)}, u32[]{:S(2)}) collective-permute-start(f32[8,32,128]{2,1,0:T(8,128)S(1)} %slice_bitcast_fusion.2), channel_id=1, source_target_pairs={{0,2},{1,3},{2,0},{3,1},{4,6},{5,7},{6,4},{7,5},{8,10},{9,11},{10,... | collective-permute-start | bytes 393224 | tf_op jit(solution)/shard_map/ppermute | solution.py:34
  141.1 8.8 %collective-permute-start.22 = (f32[2,12,32,128]{3,2,1,0:T(8,128)S(1)}, f32[2,12,32,128]{3,2,1,0:T(8,128)S(1)}, u32[]{:S(2)}, u32[]{:S(2)}) collective-permute-start(f32[2,12,32,128]{3,2,1,0:T(8,128)S(1)} %get-tuple-element.36), channel_id=1, source_target_pairs={{0,1},{1,0},{2,3},{3,2},{4,5},{5,4},{6,7},{7,6},{8,9},{9,8},{10,11... | collective-permute-start | bytes 1179656 | tf_op jit(solution)/shard_map/ppermute | solution.py:34
  141.8 17.5 %collective-permute-start.9 = (f32[12,32,128]{2,1,0:T(8,128)S(1)}, f32[12,32,128]{2,1,0:T(8,128)S(1)}, u32[]{:S(2)}, u32[]{:S(2)}) collective-permute-start(f32[12,32,128]{2,1,0:T(8,128)S(1)} %slice_bitcast_fusion), channel_id=1, source_target_pairs={{0,2},{1,3},{2,0},{3,1},{4,6},{5,7},{6,4},{7,5},{8,10},{9,11},{10,... | collective-permute-start | bytes 589832 | tf_op jit(solution)/shard_map/ppermute | solution.py:34
  149.3 18.8 %collective-permute-start.24 = (f32[4,12,32,128]{3,2,1,0:T(8,128)S(1)}, f32[4,12,32,128]{3,2,1,0:T(8,128)S(1)}, u32[]{:S(2)}, u32[]{:S(2)}) collective-permute-start(f32[4,12,32,128]{3,2,1,0:T(8,128)S(1)} %get-tuple-element.40), channel_id=1, source_target_pairs={{0,1},{1,0},{2,3},{3,2},{4,5},{5,4},{6,7},{7,6},{8,9},{9,8},{10,11... | collective-permute-start | bytes 2359304 | tf_op jit(solution)/shard_map/ppermute | solution.py:34
  157.6 11.4 %collective-permute-start.23 = (f32[4,12,32,128]{3,2,1,0:T(8,128)S(1)}, f32[4,12,32,128]{3,2,1,0:T(8,128)S(1)}, u32[]{:S(2)}, u32[]{:S(2)}) collective-permute-start(f32[4,12,32,128]{3,2,1,0:T(8,128)S(1)} %get-tuple-element.39), channel_id=1, source_target_pairs={{0,1},{1,0},{2,3},{3,2},{4,5},{5,4},{6,7},{7,6},{8,9},{9,8},{10,11... | collective-permute-start | bytes 2359304 | tf_op jit(solution)/shard_map/ppermute | solution.py:34
  157.7 9.7 %collective-permute-start.18 = (f32[4,32,128]{2,1,0:T(8,128)S(1)}, f32[4,32,128]{2,1,0:T(8,128)S(1)}, u32[]{:S(2)}, u32[]{:S(2)}) collective-permute-start(f32[4,32,128]{2,1,0:T(8,128)S(1)} %get-tuple-element.67), channel_id=1, source_target_pairs={{0,252},{1,253},{2,254},{3,255},{4,8},{5,9},{6,10},{7,11},{8,4},{9... | collective-permute-start | bytes 196616 | tf_op jit(solution)/shard_map/ppermute | solution.py:34
  159.3 8.1 %collective-permute-start.19 = (f32[4,32,128]{2,1,0:T(8,128)S(1)}, f32[4,32,128]{2,1,0:T(8,128)S(1)}, u32[]{:S(2)}, u32[]{:S(2)}) collective-permute-start(f32[4,32,128]{2,1,0:T(8,128)S(1)} %get-tuple-element.68), channel_id=1, source_target_pairs={{0,4},{1,5},{2,6},{3,7},{4,0},{5,1},{6,2},{7,3},{8,12},{9,13},{10,... | collective-permute-start | bytes 196616 | tf_op jit(solution)/shard_map/ppermute | solution.py:34
  (15 other events, 68.8 us)

commit v3 on v2

--- a/solution.py
+++ b/solution.py
@@ -248,7 +248,7 @@
 
 
 def forward_kernel(edges, *refs):
-    e_refs, (s0_ref, s1_ref, vf_ref, inc_ref) = refs[:4], refs[4:]
+    e_refs, s_refs, (vf_ref, inc_ref) = refs[:4], refs[4:-2], refs[-2:]
     lev = inc_ref.shape[2]
     count = inc_ref.shape[1]
 
@@ -259,10 +259,13 @@
     def block(b, x):
         return halo(e_refs, b, x) if edges else e_refs[b][0, x]
 
-    ext = s0_ref.shape[1]
+    def smooth_of(x):
+        if edges:
+            return jnp.concatenate([s_refs[i + x // W][0, x % W] for i in (0, 2)], 0)
+        return jnp.concatenate([s[0, x + W] for s in s_refs], 0)
+
     for x in range(0, count, 2):
-        at = [(y if y < W else ext - 2 * W + y) if edges else y + W for y in (x, x + 1)]
-        smooth = [jnp.concatenate([s0_ref[0, y], s1_ref[0, y]], 0) for y in at]
+        smooth = [smooth_of(y) for y in (x, x + 1)]
         local = jnp.dot(vf_ref[...], jnp.concatenate(smooth, 1), preferred_element_type=jnp.float32)
         width = local.shape[1] // 2
         for i, y in enumerate((x, x + 1)):
@@ -286,17 +289,21 @@
 def forward_call(edges, e, s0, s1, vf):
     members, ext, lev, cy = s0.shape
     count = 2 * W if edges else ext - 2 * W
-    spec_of = halo_of if edges else rows_of
+    if edges:
+        ends = [pl.BlockSpec((1, W, lev, cy), lambda i, n=n: (i, n, 0, 0)) for n in (0, ext // W - 1)]
+        specs, s = [halo_of(x, 0) for x in e] + ends + ends, [s0, s0, s1, s1]
+    else:
+        specs, s = [rows_of(x, 0) for x in (*e, s0, s1)], [s0, s1]
     return pl.pallas_call(
         functools.partial(forward_kernel, edges),
         grid=(members,),
-        in_specs=[spec_of(x, 0) for x in e] + [rows_of(s0, 0), rows_of(s1, 0), pl.BlockSpec(vf.shape, lambda i: (0, 0))],
+        in_specs=specs + [pl.BlockSpec(vf.shape, lambda i: (0, 0))],
         out_specs=pl.BlockSpec((4, count, lev, cy), lambda i: (0, 0, 0, 0)),
         out_shape=jax.ShapeDtypeStruct((4, count, lev, cy), jnp.float32),
         compiler_params=pltpu.CompilerParams(vmem_limit_bytes=32 * 2**20),
         cost_estimate=COST,
         name="edges" if edges else "inner",
-    )(*e, s0, s1, vf)
+    )(*e, *s, vf)
 
 
 def adjoint_kernel(_core, e0_ref, e1_ref, e2_ref, e3_ref, *refs):
@@ -449,17 +456,16 @@
     relayed = relay(after(own_second, s0))
     got = after(got, s0, own_first, own_second, far_mine)
     g_own = scatter_call(got.reshape(message.shape), cap, cols, lev, cy)
-    g_raw = g_own
     g_low, g_high = beside_tile(even, g_own[cols - W :], g_own[:W])
     g_own = jnp.concatenate([g_low, after(g_own, s1), g_high], 0)
     g_far = flip_chip(g_own)
     g_beside = flip_core(jnp.stack([g_own, g_far]))
     g = jnp.stack([g_own, g_beside[0], g_far, g_beside[1]])
 
-    far_send = payloads((far_mine, after(far_beside, g_raw)))
+    far_send = payloads((far_mine, after(far_beside, g_own)))
     far_first = swap_first(far_send[0])
     far_second = swap_second_near(far_send[1])
-    reached = reach(after(far_send[1], g_own))
+    reached = reach(far_send[1])
     e = [mine, beside, far_mine, after(far_beside, far_send)]
     inner = forward_call(False, e, s0, s1, vf)
 
@@ -475,27 +481,25 @@
     def over_cores(part):
         return part[::2] + flip_core(part[1::2])
 
-    def over_chips(pair):
-        return pair[0] + flip_chip(pair[1])
-
     def adjoint(n, grad, *first):
         at, c = plan[n]
         return adjoint_call(core_arg, at, c, e, halos, after(g, first), vt, coef, control, grad)
 
     plan = chunks_of(half)
-    inner = over_chips(over_cores(inner))
+    inner = over_cores(inner)
     grad, r = adjoint(0, None, edges)
     returned = [flip_core(r)]
-    edges = over_chips(over_cores(edges))
-    grad, r = adjoint(1, grad)
+    edges = over_cores(edges)
+    edge_low, edge_high = beside_tile(even, edges[:, W:], edges[:, :W])
+    grad, r = adjoint(1, grad, edges)
     returned.append(flip_core(r))
-    edge_low, edge_high = beside_tile(even, edges[W:], edges[:W])
+    inc = jnp.concatenate([inner[:, :W] + edge_low, inner[:, W : cols - W], inner[:, cols - W :] + edge_high], 1)
+    inc = inc[0] + flip_chip(inc[1])
     grad = finish_call(core_arg, plan[0][0], returned[0], control, grad)
-    grad, r = adjoint(2, grad, edges)
+    grad, r = adjoint(2, grad)
     returned.append(flip_core(r))
     for n in (1, 2):
         grad = finish_call(core_arg, plan[n][0], returned[n], control, grad)
-    inc = jnp.concatenate([inner[:W] + edge_low, inner[W : cols - W], inner[cols - W :] + edge_high], 0)
     return jnp.transpose(inc, (1, 0, 2)), jnp.transpose(grad, (0, 2, 1, 3))
 
 

time: 171 us -> 164 us (0.959)
  starting transfers between devices: 58.4 us -> 47.8 us
  waiting for transfers between devices: 36.1 us -> 42.5 us
  local copies, waits for them, and re-layouts: 9.09 us -> 3.79 us
  other arithmetic: 14.5 us -> 17 us
    ppermute x25 -> x24, starting transfers between devices: 51.5 us -> 41.7 us  [permute(): return lax.ppermute(x, ('tile', 'lev'), pairs)]
    unnamed x27 -> x21, local copies, waits for them, and re-layouts: 7.41 us -> 3.08 us
    ppermute x25 -> x24, waiting for transfers between devices: 36.1 us -> 39.9 us  [permute(): return lax.ppermute(x, ('tile', 'lev'), pairs)]
    all_to_all x1, waiting for transfers between devices: 0.01 us -> 2.6 us  [local(): lax.all_to_all(message.reshape(rows, -1), 'tile', split_axis=0, concat_ax...]
  transfers between devices with their start and end apart: 26 -> 25, of which waited for: 6 -> 8; matrix products, arithmetic and copies ran while one was open for 10% -> 10% of each run, Pallas kernels for 29% -> 31%
where the time goes in v3:
time: 164 us; the launch traced here: 163 us
  Pallas kernels  50.8 us (31%)
  starting transfers between devices  47.8 us (29%)
  waiting for transfers between devices  42.5 us (26%)
  other arithmetic  17 us (10%)
  local copies, waits for them, and re-layouts  3.79 us (2%)
    ppermute x24, starting transfers between devices, permute(): return lax.ppermute(x, ('tile', 'lev'), pairs)  41.7 us
    ppermute x24, waiting for transfers between devices, permute(): return lax.ppermute(x, ('tile', 'lev'), pairs)  39.9 us
    pallas_call x3, Pallas kernels, adjoint_call(): pl.pallas_call(adjoint_kernel, grid_spec=pltpu.PrefetchScalarGridSpec(num...  18.4 us
    pallas_call x2, Pallas kernels, smooth_call(): pl.pallas_call(smooth_kernel, grid_spec=pltpu.PrefetchScalarGridSpec(num_...  13.5 us
    pallas_call x2, Pallas kernels, forward_call(): pl.pallas_call(functools.partial(forward_kernel, edges), grid=(members,),...  12.4 us
    all_to_all x1, starting transfers between devices, local(): lax.all_to_all(message.reshape(rows, -1), 'tile', split_axis=0, concat_ax...  6.06 us
    another operation x6, other arithmetic, payloads(): jnp.stack([jnp.where(even, bottom(x), top(x)) for x in pair])  5.38 us
  transfers between devices with their start and end apart: 25, of which 8 were waited for; matrix products, arithmetic and copies ran while one was open for 10% of the time, Pallas kernels for 31%

profile of v3, /device:TPU:1, one launch (start us, length us, event | category | flops | bytes accessed | tf_op | source)
XLA Modules:
  0.0 163.0 jit_solution(6338215870619451083)
XLA Ops:
  1.4 11.5 %collective-permute-start.3 = (f32[4,128]{1,0:T(4,128)S(1)}, f32[4,128]{1,0:T(4,128)S(1)}, u32[]{:S(2)}, u32[]{:S(2)}) collective-permute-start(f32[4,128]{1,0:T(4,128)S(1)} %get-tuple-element.69), channel_id=1, source_target_pairs={{0,252},{1,253},{2,254},{3,255},{4,8},{5,9},{6,10},{7,11},{8,4},{9... | collective-permute-start | bytes 6152 | tf_op jit(solution)/shard_map/ppermute | solution.py:34
  24.2 7.1 %smooth.2 = bf16[10,20,32,128]{3,2,1,0:T(8,128)(2,1)} custom-call(s32[1]{0:T(128)} %bitcast.10._core, f32[20,12,32,128]{3,2,1,0:T(8,128)S(1)} %bitcast.47, f32[20,128]{1,0:T(8,128)S(1)} %pad_maximum_fusion.8.cx_ref.refs_6_, f32[20,128]{1,0:T(8,128)S(1)} %fusion.2.mid_ref.refs_7_, f32[2,128]{1,0:T(2,128)S(1)} %pad_maximum_fusion.9.cy_ref.refs_8_), custom_call_target="tpu_custom_call" | custom-call | flops 1 | bytes 1 | tf_op jit(solution)/shard_map/smooth/pallas_call | solution.py:141
  33.4 2.8 %collective-permute-start.6 = (bf16[2,10,4,32,128]{4,3,2,1,0:T(8,128)(2,1)}, bf16[2,10,4,32,128]{4,3,2,1,0:T(8,128)(2,1)}, u32[]{:S(2)}, u32[]{:S(2)}) collective-permute-start(bf16[2,10,4,32,128]{4,3,2,1,0:T(8,128)(2,1)} %pad_maximum_fusion.2), channel_id=1, source_target_pairs={{0,254},{1,255},{4,8},{5,9},{6,10},{7,11},{8,4},{9,5},{10,6},{11,7... | collective-permute-start | bytes 1966088 | tf_op jit(solution)/shard_map/ppermute | solution.py:34
  36.2 6.1 %all-to-all-start = ((f32[64,1,1152]{2,1,0:T(1,128)}), f32[64,1,1152]{2,1,0:T(1,128)S(1)}, u32[]{:S(2)}, u32[]{:S(2)}) async-start(f32[64,1,1152]{2,1,0:T(1,128)} %bitcast.9), calls=%async_computation | async-start | bytes 589824 | tf_op jit(solution)/shard_map/all_to_all | solution.py:448
  42.3 3.5 %collective-permute-start.2 = (bf16[10,12,32,128]{3,2,1,0:T(8,128)(2,1)}, bf16[10,12,32,128]{3,2,1,0:T(8,128)(2,1)}, u32[]{:S(2)}, u32[]{:S(2)}) collective-permute-start(bf16[10,12,32,128]{3,2,1,0:T(8,128)(2,1)} %collective-permute-done.refs_1_.e1_ref), channel_id=1, source_target_pairs={{0,2},{1,3},{2,0},{3,1},{4,6},{5,7},{6,4},{7,5},{8,10},{9,11},{10,... | collective-permute-start | bytes 2949128 | tf_op jit(solution)/shard_map/ppermute | solution.py:34
  45.8 2.1 %copy-done.1 = f32[20,32,12,128]{3,1,2,0:T(8,128)S(1)} copy-done((f32[20,32,12,128]{3,1,2,0:T(8,128)S(1)}, f32[20,32,12,128]{3,1,2,0:T(8,128)}, u32[]{:S(2)}) %copy-start.1) | copy-done | bytes 3932184
  47.9 6.4 %smooth.3.refs_4_.refs_5_ = bf16[10,20,32,128]{3,2,1,0:T(8,128)(2,1)S(1)} custom-call(s32[1]{0:T(128)} %bitcast.10._core, f32[20,12,32,128]{3,2,1,0:T(8,128)S(1)} %bitcast.48, f32[20,128]{1,0:T(8,128)S(1)} %pad_maximum_fusion.8.cx_ref.refs_6_, f32[20,128]{1,0:T(8,128)S(1)} %fusion.2.mid_ref.refs_7_, f32[2,128]{1,0:T(2,128)S(1)} %pad_maximum_fusion.9.cy_ref.refs_8_), custom_call_target="tpu_custom_call" | custom-call | flops 1 | bytes 1 | tf_op jit(solution)/shard_map/smooth/pallas_call | solution.py:141
  54.3 2.6 %all-to-all-done = f32[64,1,1152]{2,1,0:T(1,128)S(1)} async-done(((f32[64,1,1152]{2,1,0:T(1,128)}), f32[64,1,1152]{2,1,0:T(1,128)S(1)}, u32[]{:S(2)}, u32[]{:S(2)}) %all-to-all-start) | async-done | bytes 294944 | tf_op jit(solution)/shard_map/all_to_all | solution.py:448
  56.9 5.0 %collective-permute-done.6 = bf16[2,10,4,32,128]{4,3,2,1,0:T(8,128)(2,1)} collective-permute-done((bf16[2,10,4,32,128]{4,3,2,1,0:T(8,128)(2,1)}, bf16[2,10,4,32,128]{4,3,2,1,0:T(8,128)(2,1)}, u32[]{:S(2)}, u32[]{:S(2)}) %collective-permute-start.6) | collective-permute-done | bytes 655392 | tf_op jit(solution)/shard_map/ppermute | solution.py:34
  63.3 2.7 %collective-permute-start.7 = (f32[4,32,128]{2,1,0:T(8,128)S(1)}, f32[4,32,128]{2,1,0:T(8,128)S(1)}, u32[]{:S(2)}, u32[]{:S(2)}) collective-permute-start(f32[4,32,128]{2,1,0:T(8,128)S(1)} %get-tuple-element.65), channel_id=1, source_target_pairs={{0,252},{1,253},{2,254},{3,255},{4,8},{5,9},{6,10},{7,11},{8,4},{9... | collective-permute-start | bytes 196616 | tf_op jit(solution)/shard_map/ppermute | solution.py:34
  67.2 3.0 %collective-permute-start.11 = (bf16[2,10,4,32,128]{4,3,2,1,0:T(8,128)(2,1)}, bf16[2,10,4,32,128]{4,3,2,1,0:T(8,128)(2,1)}, u32[]{:S(2)}, u32[]{:S(2)}) collective-permute-start(bf16[2,10,4,32,128]{4,3,2,1,0:T(8,128)(2,1)} %collective-permute-done.6), channel_id=1, source_target_pairs={{0,2},{1,3},{62,60},{63,61},{64,66},{65,67},{126,124},{127,125},{1... | collective-permute-start | bytes 1966088 | tf_op jit(solution)/shard_map/ppermute | solution.py:34
  70.2 9.6 %collective-permute-done.7 = f32[4,32,128]{2,1,0:T(8,128)S(1)} collective-permute-done((f32[4,32,128]{2,1,0:T(8,128)S(1)}, f32[4,32,128]{2,1,0:T(8,128)S(1)}, u32[]{:S(2)}, u32[]{:S(2)}) %collective-permute-start.7) | collective-permute-done | bytes 65568 | tf_op jit(solution)/shard_map/ppermute | solution.py:34
  83.5 2.4 %collective-permute-start.13 = (bf16[2,10,4,32,128]{4,3,2,1,0:T(8,128)(2,1)}, bf16[2,10,4,32,128]{4,3,2,1,0:T(8,128)(2,1)}, u32[]{:S(2)}, u32[]{:S(2)}) collective-permute-start(bf16[2,10,4,32,128]{4,3,2,1,0:T(8,128)(2,1)} %pad_maximum_fusion.4), channel_id=1, source_target_pairs={{0,252},{1,253},{62,66},{63,67},{64,60},{65,61},{126,130},{127,131... | collective-permute-start | bytes 1966088 | tf_op jit(solution)/shard_map/ppermute | solution.py:34
  85.9 4.2 %collective-permute-start.12 = (bf16[2,10,4,32,128]{4,3,2,1,0:T(8,128)(2,1)}, bf16[2,10,4,32,128]{4,3,2,1,0:T(8,128)(2,1)}, u32[]{:S(2)}, u32[]{:S(2)}) collective-permute-start(bf16[2,10,4,32,128]{4,3,2,1,0:T(8,128)(2,1)} %pad_maximum_fusion.4), channel_id=1, source_target_pairs={{0,254},{1,255},{4,8},{5,9},{6,10},{7,11},{8,4},{9,5},{10,6},{11,7... | collective-permute-start | bytes 1966088 | tf_op jit(solution)/shard_map/ppermute | solution.py:34
  90.3 7.0 %inner.1 = f32[4,12,32,128]{3,2,1,0:T(8,128)S(1)} custom-call(bf16[10,12,32,128]{3,2,1,0:T(8,128)(2,1)S(1)} %get-tuple-element.45.refs_0_.e0_ref, bf16[10,12,32,128]{3,2,1,0:T(8,128)(2,1)} %collective-permute-done.refs_1_.e1_ref, bf16[10,12,32,128]{3,2,1,0:T(8,128)(2,1)} %collective-permute-done.1.refs_2_.e2_ref, ...), custom_call_target="tpu_custom_call" | custom-call | flops 1 | bytes 1 | tf_op jit(solution)/shard_map/inner/pallas_call | solution.py:297
  97.2 9.9 %collective-permute-done.19 = f32[20,32,128]{2,1,0:T(8,128)} collective-permute-done((f32[20,32,128]{2,1,0:T(8,128)}, f32[20,32,128]{2,1,0:T(8,128)}, u32[]{:S(2)}, u32[]{:S(2)}) %collective-permute-start.19) | collective-permute-done | bytes 327712 | tf_op jit(solution)/shard_map/ppermute | solution.py:34
  108.9 4.7 %collective-permute-done.12 = bf16[2,10,4,32,128]{4,3,2,1,0:T(8,128)(2,1)} collective-permute-done((bf16[2,10,4,32,128]{4,3,2,1,0:T(8,128)(2,1)}, bf16[2,10,4,32,128]{4,3,2,1,0:T(8,128)(2,1)}, u32[]{:S(2)}, u32[]{:S(2)}) %collective-permute-start.12) | collective-permute-done | bytes 655392 | tf_op jit(solution)/shard_map/ppermute | solution.py:34
  115.7 5.5 %edges.1 = f32[4,8,32,128]{3,2,1,0:T(8,128)S(1)} custom-call(bf16[2,10,4,32,128]{4,3,2,1,0:T(8,128)(2,1)S(1)} %get-tuple-element.78.refs_0_, bf16[2,10,4,32,128]{4,3,2,1,0:T(8,128)(2,1)S(1)} %get-tuple-element.77.refs_1_, bf16[2,10,4,32,128]{4,3,2,1,0:T(8,128)(2,1)S(1)} %get-tuple-element.46.refs_2_, ...), custom_call_target="tpu_custom_call" | custom-call | flops 1 | bytes 1 | tf_op jit(solution)/shard_map/edges/pallas_call | solution.py:297
  121.2 3.8 %collective-permute-start.15 = (f32[2,8,32,128]{3,2,1,0:T(8,128)S(1)}, f32[2,8,32,128]{3,2,1,0:T(8,128)S(1)}, u32[]{:S(2)}, u32[]{:S(2)}) collective-permute-start(f32[2,8,32,128]{3,2,1,0:T(8,128)S(1)} %slice.127), channel_id=1, source_target_pairs={{0,1},{1,0},{2,3},{3,2},{4,5},{5,4},{6,7},{7,6},{8,9},{9,8},{10,11... | collective-permute-start | bytes 786440 | tf_op jit(solution)/shard_map/ppermute | solution.py:34
  128.5 4.3 %adjoint.3 = (f32[20,12,32,128]{3,2,1,0:T(8,128)}, f32[2,12,32,128]{3,2,1,0:T(8,128)S(1)}) custom-call(s32[1]{0:T(128)} %bitcast.10._core, bf16[10,12,32,128]{3,2,1,0:T(8,128)(2,1)S(1)} %get-tuple-element.45.refs_0_.e0_ref, bf16[10,12,32,128]{3,2,1,0:T(8,128)(2,1)} %collective-permute-done.refs_1_.e1_ref, ...), custom_call_target="tpu_custom_call" | custom-call | flops 1 | bytes 1 | tf_op jit(solution)/shard_map/adjoint/pallas_call | solution.py:355
  133.4 7.0 %adjoint.4 = (f32[20,12,32,128]{3,2,1,0:T(8,128)}, f32[4,12,32,128]{3,2,1,0:T(8,128)S(1)}) custom-call(s32[1]{0:T(128)} %bitcast.10._core, bf16[10,12,32,128]{3,2,1,0:T(8,128)(2,1)S(1)} %get-tuple-element.45.refs_0_.e0_ref, bf16[10,12,32,128]{3,2,1,0:T(8,128)(2,1)} %collective-permute-done.refs_1_.e1_ref, ...), custom_call_target="tpu_custom_call", output_to_operand_aliasing={{0}: (15, {})} | custom-call | flops 1 | bytes 1 | tf_op jit(solution)/shard_map/adjoint/pallas_call | solution.py:355
  141.4 4.8 %collective-permute-done.16 = f32[2,4,32,128]{3,2,1,0:T(8,128)S(1)} collective-permute-done((f32[2,4,32,128]{3,2,1,0:T(8,128)S(1)}, f32[2,4,32,128]{3,2,1,0:T(8,128)S(1)}, u32[]{:S(2)}, u32[]{:S(2)}) %collective-permute-start.16) | collective-permute-done | bytes 131104 | tf_op jit(solution)/shard_map/ppermute | solution.py:34
  146.2 7.0 %adjoint.5 = (f32[20,12,32,128]{3,2,1,0:T(8,128)}, f32[4,12,32,128]{3,2,1,0:T(8,128)S(1)}) custom-call(s32[1]{0:T(128)} %bitcast.10._core, bf16[10,12,32,128]{3,2,1,0:T(8,128)(2,1)S(1)} %get-tuple-element.45.refs_0_.e0_ref, bf16[10,12,32,128]{3,2,1,0:T(8,128)(2,1)} %collective-permute-done.refs_1_.e1_ref, ...), custom_call_target="tpu_custom_call", output_to_operand_aliasing={{0}: (15, {})} | custom-call | flops 1 | bytes 1 | tf_op jit(solution)/shard_map/adjoint/pallas_call | solution.py:355
  155.5 4.9 %collective-permute-done.18 = f32[12,32,128]{2,1,0:T(8,128)S(1)} collective-permute-done((f32[12,32,128]{2,1,0:T(8,128)S(1)}, f32[12,32,128]{2,1,0:T(8,128)S(1)}, u32[]{:S(2)}, u32[]{:S(2)}) %collective-permute-start.18) | collective-permute-done | bytes 196640 | tf_op jit(solution)/shard_map/ppermute | solution.py:34
  (97 shorter events, 34.1 us)
Async XLA Ops:
  1.4 18.6 %collective-permute-start.3 = (f32[4,128]{1,0:T(4,128)S(1)}, f32[4,128]{1,0:T(4,128)S(1)}, u32[]{:S(2)}, u32[]{:S(2)}) collective-permute-start(f32[4,128]{1,0:T(4,128)S(1)} %get-tuple-element.69), channel_id=1, source_target_pairs={{0,252},{1,253},{2,254},{3,255},{4,8},{5,9},{6,10},{7,11},{8,4},{9... | collective-permute-start | bytes 6152 | tf_op jit(solution)/shard_map/ppermute | solution.py:34
  12.8 7.2 %collective-permute-start.4 = (f32[4,128]{1,0:T(4,128)S(1)}, f32[4,128]{1,0:T(4,128)S(1)}, u32[]{:S(2)}, u32[]{:S(2)}) collective-permute-start(f32[4,128]{1,0:T(4,128)S(1)} %get-tuple-element.70), channel_id=1, source_target_pairs={{0,4},{1,5},{2,6},{3,7},{4,0},{5,1},{6,2},{7,3},{8,12},{9,13},{10,... | collective-permute-start | bytes 6152 | tf_op jit(solution)/shard_map/ppermute | solution.py:34
  14.5 5.6 %collective-permute-start = (bf16[10,12,32,128]{3,2,1,0:T(8,128)(2,1)S(1)}, bf16[10,12,32,128]{3,2,1,0:T(8,128)(2,1)}, u32[]{:S(2)}, u32[]{:S(2)}) collective-permute-start(bf16[10,12,32,128]{3,2,1,0:T(8,128)(2,1)S(1)} %get-tuple-element.44), channel_id=1, source_target_pairs={{0,1},{1,0},{2,3},{3,2},{4,5},{5,4},{6,7},{7,6},{8,9},{9,8},{10,11... | collective-permute-start | bytes 2949128 | tf_op jit(solution)/shard_map/ppermute | solution.py:34
  15.6 41.3 %collective-permute-start.1 = (bf16[10,12,32,128]{3,2,1,0:T(8,128)(2,1)S(1)}, bf16[10,12,32,128]{3,2,1,0:T(8,128)(2,1)}, u32[]{:S(2)}, u32[]{:S(2)}) collective-permute-start(bf16[10,12,32,128]{3,2,1,0:T(8,128)(2,1)S(1)} %get-tuple-element.45.refs_0_.e0_ref), channel_id=1, source_target_pairs={{0,2},{1,3},{2,0},{3,1},{4,6},{5,7},{6,4},{7,5},{8,10},{9,11},{10,... | collective-permute-start | bytes 2949128 | tf_op jit(solution)/shard_map/ppermute | solution.py:34
  31.3 48.5 %collective-permute-start.9 = (bf16[10,20,32,128]{3,2,1,0:T(8,128)(2,1)}, bf16[10,20,32,128]{3,2,1,0:T(8,128)(2,1)}, u32[]{:S(2)}, u32[]{:S(2)}) collective-permute-start(bf16[10,20,32,128]{3,2,1,0:T(8,128)(2,1)} %smooth.2), channel_id=1, source_target_pairs={{0,1},{1,0},{2,3},{3,2},{4,5},{5,4},{6,7},{7,6},{8,9},{9,8},{10,11... | collective-permute-start | bytes 4915208 | tf_op jit(solution)/shard_map/ppermute | solution.py:34
  31.7 25.2 %collective-permute-start.5 = (bf16[2,10,4,32,128]{4,3,2,1,0:T(8,128)(2,1)}, bf16[2,10,4,32,128]{4,3,2,1,0:T(8,128)(2,1)}, u32[]{:S(2)}, u32[]{:S(2)}) collective-permute-start(bf16[2,10,4,32,128]{4,3,2,1,0:T(8,128)(2,1)} %pad_maximum_fusion.1), channel_id=1, source_target_pairs={{0,4},{1,5},{2,6},{3,7},{4,0},{5,1},{6,2},{7,3},{8,12},{9,13},{10,... | collective-permute-start | bytes 1966088 | tf_op jit(solution)/shard_map/ppermute | solution.py:34
  33.4 28.5 %collective-permute-start.6 = (bf16[2,10,4,32,128]{4,3,2,1,0:T(8,128)(2,1)}, bf16[2,10,4,32,128]{4,3,2,1,0:T(8,128)(2,1)}, u32[]{:S(2)}, u32[]{:S(2)}) collective-permute-start(bf16[2,10,4,32,128]{4,3,2,1,0:T(8,128)(2,1)} %pad_maximum_fusion.2), channel_id=1, source_target_pairs={{0,254},{1,255},{4,8},{5,9},{6,10},{7,11},{8,4},{9,5},{10,6},{11,7... | collective-permute-start | bytes 1966088 | tf_op jit(solution)/shard_map/ppermute | solution.py:34
  36.2 20.7 %all-to-all-start = ((f32[64,1,1152]{2,1,0:T(1,128)}), f32[64,1,1152]{2,1,0:T(1,128)S(1)}, u32[]{:S(2)}, u32[]{:S(2)}) async-start(f32[64,1,1152]{2,1,0:T(1,128)} %bitcast.9), calls=%async_computation | async-start | bytes 589824 | tf_op jit(solution)/shard_map/all_to_all | solution.py:448
  42.3 38.3 %collective-permute-start.2 = (bf16[10,12,32,128]{3,2,1,0:T(8,128)(2,1)}, bf16[10,12,32,128]{3,2,1,0:T(8,128)(2,1)}, u32[]{:S(2)}, u32[]{:S(2)}) collective-permute-start(bf16[10,12,32,128]{3,2,1,0:T(8,128)(2,1)} %collective-permute-done.refs_1_.e1_ref), channel_id=1, source_target_pairs={{0,2},{1,3},{2,0},{3,1},{4,6},{5,7},{6,4},{7,5},{8,10},{9,11},{10,... | collective-permute-start | bytes 2949128 | tf_op jit(solution)/shard_map/ppermute | solution.py:34
  63.3 16.4 %collective-permute-start.7 = (f32[4,32,128]{2,1,0:T(8,128)S(1)}, f32[4,32,128]{2,1,0:T(8,128)S(1)}, u32[]{:S(2)}, u32[]{:S(2)}) collective-permute-start(f32[4,32,128]{2,1,0:T(8,128)S(1)} %get-tuple-element.65), channel_id=1, source_target_pairs={{0,252},{1,253},{2,254},{3,255},{4,8},{5,9},{6,10},{7,11},{8,4},{9... | collective-permute-start | bytes 196616 | tf_op jit(solution)/shard_map/ppermute | solution.py:34
  66.1 13.7 %collective-permute-start.8 = (f32[4,32,128]{2,1,0:T(8,128)S(1)}, f32[4,32,128]{2,1,0:T(8,128)S(1)}, u32[]{:S(2)}, u32[]{:S(2)}) collective-permute-start(f32[4,32,128]{2,1,0:T(8,128)S(1)} %get-tuple-element.66), channel_id=1, source_target_pairs={{0,4},{1,5},{2,6},{3,7},{4,0},{5,1},{6,2},{7,3},{8,12},{9,13},{10,... | collective-permute-start | bytes 196616 | tf_op jit(solution)/shard_map/ppermute | solution.py:34
  67.2 41.7 %collective-permute-start.11 = (bf16[2,10,4,32,128]{4,3,2,1,0:T(8,128)(2,1)}, bf16[2,10,4,32,128]{4,3,2,1,0:T(8,128)(2,1)}, u32[]{:S(2)}, u32[]{:S(2)}) collective-permute-start(bf16[2,10,4,32,128]{4,3,2,1,0:T(8,128)(2,1)} %collective-permute-done.6), channel_id=1, source_target_pairs={{0,2},{1,3},{62,60},{63,61},{64,66},{65,67},{126,124},{127,125},{1... | collective-permute-start | bytes 1966088 | tf_op jit(solution)/shard_map/ppermute | solution.py:34
  82.6 26.3 %collective-permute-start.14 = (bf16[2,10,4,32,128]{4,3,2,1,0:T(8,128)(2,1)}, bf16[2,10,4,32,128]{4,3,2,1,0:T(8,128)(2,1)}, u32[]{:S(2)}, u32[]{:S(2)}) collective-permute-start(bf16[2,10,4,32,128]{4,3,2,1,0:T(8,128)(2,1)} %pad_maximum_fusion.3), channel_id=1, source_target_pairs={{0,4},{1,5},{2,6},{3,7},{4,0},{5,1},{6,2},{7,3},{8,12},{9,13},{10,... | collective-permute-start | bytes 1966088 | tf_op jit(solution)/shard_map/ppermute | solution.py:34
  83.5 25.4 %collective-permute-start.13 = (bf16[2,10,4,32,128]{4,3,2,1,0:T(8,128)(2,1)}, bf16[2,10,4,32,128]{4,3,2,1,0:T(8,128)(2,1)}, u32[]{:S(2)}, u32[]{:S(2)}) collective-permute-start(bf16[2,10,4,32,128]{4,3,2,1,0:T(8,128)(2,1)} %pad_maximum_fusion.4), channel_id=1, source_target_pairs={{0,252},{1,253},{62,66},{63,67},{64,60},{65,61},{126,130},{127,131... | collective-permute-start | bytes 1966088 | tf_op jit(solution)/shard_map/ppermute | solution.py:34
  85.9 27.8 %collective-permute-start.12 = (bf16[2,10,4,32,128]{4,3,2,1,0:T(8,128)(2,1)}, bf16[2,10,4,32,128]{4,3,2,1,0:T(8,128)(2,1)}, u32[]{:S(2)}, u32[]{:S(2)}) collective-permute-start(bf16[2,10,4,32,128]{4,3,2,1,0:T(8,128)(2,1)} %pad_maximum_fusion.4), channel_id=1, source_target_pairs={{0,254},{1,255},{4,8},{5,9},{6,10},{7,11},{8,4},{9,5},{10,6},{11,7... | collective-permute-start | bytes 1966088 | tf_op jit(solution)/shard_map/ppermute | solution.py:34
  90.1 17.0 %collective-permute-start.19 = (f32[20,32,128]{2,1,0:T(8,128)}, f32[20,32,128]{2,1,0:T(8,128)}, u32[]{:S(2)}, u32[]{:S(2)}) collective-permute-start(f32[20,32,128]{2,1,0:T(8,128)} %get-tuple-element.62), channel_id=1, source_target_pairs={{0,2},{1,3},{2,0},{3,1},{4,6},{5,7},{6,4},{7,5},{8,10},{9,11},{10,... | collective-permute-start | bytes 983048 | tf_op jit(solution)/shard_map/ppermute | solution.py:34
  108.1 18.1 %collective-permute-start.20 = (f32[2,20,32,128]{3,2,1,0:T(8,128)S(1)}, f32[2,20,32,128]{3,2,1,0:T(8,128)S(1)}, u32[]{:S(2)}, u32[]{:S(2)}) collective-permute-start(f32[2,20,32,128]{3,2,1,0:T(8,128)S(1)} %pad_maximum_fusion.5), channel_id=1, source_target_pairs={{0,1},{1,0},{2,3},{3,2},{4,5},{5,4},{6,7},{7,6},{8,9},{9,8},{10,11... | collective-permute-start | bytes 1966088 | tf_op jit(solution)/shard_map/ppermute | solution.py:34
  125.1 8.3 %collective-permute-start.10 = (f32[2,12,32,128]{3,2,1,0:T(8,128)S(1)}, f32[2,12,32,128]{3,2,1,0:T(8,128)S(1)}, u32[]{:S(2)}, u32[]{:S(2)}) collective-permute-start(f32[2,12,32,128]{3,2,1,0:T(8,128)S(1)} %slice.124), channel_id=1, source_target_pairs={{0,1},{1,0},{2,3},{3,2},{4,5},{5,4},{6,7},{7,6},{8,9},{9,8},{10,11... | collective-permute-start | bytes 1179656 | tf_op jit(solution)/shard_map/ppermute | solution.py:34
  132.7 7.9 %collective-permute-start.21 = (f32[2,12,32,128]{3,2,1,0:T(8,128)S(1)}, f32[2,12,32,128]{3,2,1,0:T(8,128)S(1)}, u32[]{:S(2)}, u32[]{:S(2)}) collective-permute-start(f32[2,12,32,128]{3,2,1,0:T(8,128)S(1)} %get-tuple-element.33), channel_id=1, source_target_pairs={{0,1},{1,0},{2,3},{3,2},{4,5},{5,4},{6,7},{7,6},{8,9},{9,8},{10,11... | collective-permute-start | bytes 1179656 | tf_op jit(solution)/shard_map/ppermute | solution.py:34
  133.1 13.0 %collective-permute-start.16 = (f32[2,4,32,128]{3,2,1,0:T(8,128)S(1)}, f32[2,4,32,128]{3,2,1,0:T(8,128)S(1)}, u32[]{:S(2)}, u32[]{:S(2)}) collective-permute-start(f32[2,4,32,128]{3,2,1,0:T(8,128)S(1)} %get-tuple-element.63), channel_id=1, source_target_pairs={{0,252},{1,253},{2,254},{3,255},{4,8},{5,9},{6,10},{7,11},{8,4},{9... | collective-permute-start | bytes 393224 | tf_op jit(solution)/shard_map/ppermute | solution.py:34
  133.2 12.9 %collective-permute-start.17 = (f32[2,4,32,128]{3,2,1,0:T(8,128)S(1)}, f32[2,4,32,128]{3,2,1,0:T(8,128)S(1)}, u32[]{:S(2)}, u32[]{:S(2)}) collective-permute-start(f32[2,4,32,128]{3,2,1,0:T(8,128)S(1)} %get-tuple-element.64), channel_id=1, source_target_pairs={{0,4},{1,5},{2,6},{3,7},{4,0},{5,1},{6,2},{7,3},{8,12},{9,13},{10,... | collective-permute-start | bytes 393224 | tf_op jit(solution)/shard_map/ppermute | solution.py:34
  140.5 20.7 %collective-permute-start.23 = (f32[4,12,32,128]{3,2,1,0:T(8,128)S(1)}, f32[4,12,32,128]{3,2,1,0:T(8,128)S(1)}, u32[]{:S(2)}, u32[]{:S(2)}) collective-permute-start(f32[4,12,32,128]{3,2,1,0:T(8,128)S(1)} %get-tuple-element.38), channel_id=1, source_target_pairs={{0,1},{1,0},{2,3},{3,2},{4,5},{5,4},{6,7},{7,6},{8,9},{9,8},{10,11... | collective-permute-start | bytes 2359304 | tf_op jit(solution)/shard_map/ppermute | solution.py:34
  153.3 8.8 %collective-permute-start.22 = (f32[4,12,32,128]{3,2,1,0:T(8,128)S(1)}, f32[4,12,32,128]{3,2,1,0:T(8,128)S(1)}, u32[]{:S(2)}, u32[]{:S(2)}) collective-permute-start(f32[4,12,32,128]{3,2,1,0:T(8,128)S(1)} %get-tuple-element.37), channel_id=1, source_target_pairs={{0,1},{1,0},{2,3},{3,2},{4,5},{5,4},{6,7},{7,6},{8,9},{9,8},{10,11... | collective-permute-start | bytes 2359304 | tf_op jit(solution)/shard_map/ppermute | solution.py:34
  153.8 6.7 %collective-permute-start.18 = (f32[12,32,128]{2,1,0:T(8,128)S(1)}, f32[12,32,128]{2,1,0:T(8,128)S(1)}, u32[]{:S(2)}, u32[]{:S(2)}) collective-permute-start(f32[12,32,128]{2,1,0:T(8,128)S(1)} %slice_bitcast_fusion), channel_id=1, source_target_pairs={{0,2},{1,3},{2,0},{3,1},{4,6},{5,7},{6,4},{7,5},{8,10},{9,11},{10,... | collective-permute-start | bytes 589832 | tf_op jit(solution)/shard_map/ppermute | solution.py:34
  (11 other events, 43.4 us)

commit v4 on v3

--- a/solution.py
+++ b/solution.py
@@ -14,7 +14,7 @@
 
 
 def chunks_of(half):
-    sizes = [half - 2 * (2 * half // 5), 2 * half // 5, 2 * half // 5]
+    sizes = [half - 2 * half // 5, 2 * half // 5]
     out, at = [], 0
     for s in sizes:
         if s:
@@ -495,10 +495,7 @@
     returned.append(flip_core(r))
     inc = jnp.concatenate([inner[:, :W] + edge_low, inner[:, W : cols - W], inner[:, cols - W :] + edge_high], 1)
     inc = inc[0] + flip_chip(inc[1])
-    grad = finish_call(core_arg, plan[0][0], returned[0], control, grad)
-    grad, r = adjoint(2, grad)
-    returned.append(flip_core(r))
-    for n in (1, 2):
+    for n in (0, 1):
         grad = finish_call(core_arg, plan[n][0], returned[n], control, grad)
     return jnp.transpose(inc, (1, 0, 2)), jnp.transpose(grad, (0, 2, 1, 3))
 

time: 164 us -> 162 us (0.988)
  starting transfers between devices: 47.8 us -> 51.6 us
  waiting for transfers between devices: 42.5 us -> 39.4 us
  other arithmetic: 17 us -> 14.2 us
  Pallas kernels: 50.8 us -> 49.1 us
    ppermute x24 -> x23, starting transfers between devices: 41.7 us -> 45.5 us  [permute(): return lax.ppermute(x, ('tile', 'lev'), pairs)]
    ppermute x24 -> x23, waiting for transfers between devices: 39.9 us -> 36.8 us  [permute(): return lax.ppermute(x, ('tile', 'lev'), pairs)]
    another operation x2, other arithmetic: 2.04 us -> 0.18 us  [local(): g = jnp.stack([g_own, g_beside[0], g_far, g_beside[1]])]
    pallas_call x3 -> x2, Pallas kernels: 18.4 us -> 16.8 us  [adjoint_call(): pl.pallas_call(adjoint_kernel, grid_spec=pltpu.PrefetchScalarGridSpec(num...]
  transfers between devices with their start and end apart: 25 -> 24, of which waited for: 8 -> 7; matrix products, arithmetic and copies ran while one was open for 10% -> 9% of each run, Pallas kernels for 31% -> 30%
where the time goes in v4:
time: 162 us; the launch traced here: 160 us
  starting transfers between devices  51.6 us (32%)
  Pallas kernels  49.1 us (30%)
  waiting for transfers between devices  39.4 us (24%)
  other arithmetic  14.2 us (9%)
  local copies, waits for them, and re-layouts  4.82 us (3%)
    ppermute x23, starting transfers between devices, permute(): return lax.ppermute(x, ('tile', 'lev'), pairs)  45.5 us
    ppermute x23, waiting for transfers between devices, permute(): return lax.ppermute(x, ('tile', 'lev'), pairs)  36.8 us
    pallas_call x2, Pallas kernels, adjoint_call(): pl.pallas_call(adjoint_kernel, grid_spec=pltpu.PrefetchScalarGridSpec(num...  16.8 us
    pallas_call x2, Pallas kernels, smooth_call(): pl.pallas_call(smooth_kernel, grid_spec=pltpu.PrefetchScalarGridSpec(num_...  13.4 us
    pallas_call x2, Pallas kernels, forward_call(): pl.pallas_call(functools.partial(forward_kernel, edges), grid=(members,),...  12.5 us
    all_to_all x1, starting transfers between devices, local(): lax.all_to_all(message.reshape(rows, -1), 'tile', split_axis=0, concat_ax...  6.06 us
    another operation x6, other arithmetic, payloads(): jnp.stack([jnp.where(even, bottom(x), top(x)) for x in pair])  5.38 us
    unnamed x21, local copies, waits for them, and re-layouts  4.11 us
  transfers between devices with their start and end apart: 24, of which 7 were waited for; matrix products, arithmetic and copies ran while one was open for 9% of the time, Pallas kernels for 30%

profile of v4, /device:TPU:1, one launch (start us, length us, event | category | flops | bytes accessed | tf_op | source)
XLA Modules:
  0.0 160.3 jit_solution(10783999315956374714)
XLA Ops:
  1.4 11.5 %collective-permute-start.3 = (f32[4,128]{1,0:T(4,128)S(1)}, f32[4,128]{1,0:T(4,128)S(1)}, u32[]{:S(2)}, u32[]{:S(2)}) collective-permute-start(f32[4,128]{1,0:T(4,128)S(1)} %get-tuple-element.65), channel_id=1, source_target_pairs={{0,252},{1,253},{2,254},{3,255},{4,8},{5,9},{6,10},{7,11},{8,4},{9... | collective-permute-start | bytes 6152 | tf_op jit(solution)/shard_map/ppermute | solution.py:34
  24.2 7.1 %smooth.2 = bf16[10,20,32,128]{3,2,1,0:T(8,128)(2,1)} custom-call(s32[1]{0:T(128)} %bitcast.10._core, f32[20,12,32,128]{3,2,1,0:T(8,128)S(1)} %bitcast.47, f32[20,128]{1,0:T(8,128)S(1)} %pad_maximum_fusion.8.cx_ref.refs_6_, f32[20,128]{1,0:T(8,128)S(1)} %fusion.2.mid_ref.refs_7_, f32[2,128]{1,0:T(2,128)S(1)} %pad_maximum_fusion.9.cy_ref.refs_8_), custom_call_target="tpu_custom_call" | custom-call | flops 1 | bytes 1 | tf_op jit(solution)/shard_map/smooth/pallas_call | solution.py:141
  33.4 2.8 %collective-permute-start.6 = (bf16[2,10,4,32,128]{4,3,2,1,0:T(8,128)(2,1)}, bf16[2,10,4,32,128]{4,3,2,1,0:T(8,128)(2,1)}, u32[]{:S(2)}, u32[]{:S(2)}) collective-permute-start(bf16[2,10,4,32,128]{4,3,2,1,0:T(8,128)(2,1)} %pad_maximum_fusion.2), channel_id=1, source_target_pairs={{0,254},{1,255},{4,8},{5,9},{6,10},{7,11},{8,4},{9,5},{10,6},{11,7... | collective-permute-start | bytes 1966088 | tf_op jit(solution)/shard_map/ppermute | solution.py:34
  36.2 6.1 %all-to-all-start = ((f32[64,1,1152]{2,1,0:T(1,128)}), f32[64,1,1152]{2,1,0:T(1,128)S(1)}, u32[]{:S(2)}, u32[]{:S(2)}) async-start(f32[64,1,1152]{2,1,0:T(1,128)} %bitcast.9), calls=%async_computation | async-start | bytes 589824 | tf_op jit(solution)/shard_map/all_to_all | solution.py:448
  42.2 3.5 %collective-permute-start.2 = (bf16[10,12,32,128]{3,2,1,0:T(8,128)(2,1)}, bf16[10,12,32,128]{3,2,1,0:T(8,128)(2,1)}, u32[]{:S(2)}, u32[]{:S(2)}) collective-permute-start(bf16[10,12,32,128]{3,2,1,0:T(8,128)(2,1)} %collective-permute-done.refs_1_.e1_ref), channel_id=1, source_target_pairs={{0,2},{1,3},{2,0},{3,1},{4,6},{5,7},{6,4},{7,5},{8,10},{9,11},{10,... | collective-permute-start | bytes 2949128 | tf_op jit(solution)/shard_map/ppermute | solution.py:34
  45.8 2.1 %copy-done.1 = f32[20,32,12,128]{3,1,2,0:T(8,128)S(1)} copy-done((f32[20,32,12,128]{3,1,2,0:T(8,128)S(1)}, f32[20,32,12,128]{3,1,2,0:T(8,128)}, u32[]{:S(2)}) %copy-start.1) | copy-done | bytes 3932184
  47.9 6.3 %smooth.3.refs_4_.refs_5_ = bf16[10,20,32,128]{3,2,1,0:T(8,128)(2,1)S(1)} custom-call(s32[1]{0:T(128)} %bitcast.10._core, f32[20,12,32,128]{3,2,1,0:T(8,128)S(1)} %bitcast.48, f32[20,128]{1,0:T(8,128)S(1)} %pad_maximum_fusion.8.cx_ref.refs_6_, f32[20,128]{1,0:T(8,128)S(1)} %fusion.2.mid_ref.refs_7_, f32[2,128]{1,0:T(2,128)S(1)} %pad_maximum_fusion.9.cy_ref.refs_8_), custom_call_target="tpu_custom_call" | custom-call | flops 1 | bytes 1 | tf_op jit(solution)/shard_map/smooth/pallas_call | solution.py:141
  54.2 2.6 %all-to-all-done = f32[64,1,1152]{2,1,0:T(1,128)S(1)} async-done(((f32[64,1,1152]{2,1,0:T(1,128)}), f32[64,1,1152]{2,1,0:T(1,128)S(1)}, u32[]{:S(2)}, u32[]{:S(2)}) %all-to-all-start) | async-done | bytes 294944 | tf_op jit(solution)/shard_map/all_to_all | solution.py:448
  56.9 5.0 %collective-permute-done.6 = bf16[2,10,4,32,128]{4,3,2,1,0:T(8,128)(2,1)} collective-permute-done((bf16[2,10,4,32,128]{4,3,2,1,0:T(8,128)(2,1)}, bf16[2,10,4,32,128]{4,3,2,1,0:T(8,128)(2,1)}, u32[]{:S(2)}, u32[]{:S(2)}) %collective-permute-start.6) | collective-permute-done | bytes 655392 | tf_op jit(solution)/shard_map/ppermute | solution.py:34
  63.3 2.7 %collective-permute-start.7 = (f32[4,32,128]{2,1,0:T(8,128)S(1)}, f32[4,32,128]{2,1,0:T(8,128)S(1)}, u32[]{:S(2)}, u32[]{:S(2)}) collective-permute-start(f32[4,32,128]{2,1,0:T(8,128)S(1)} %get-tuple-element.61), channel_id=1, source_target_pairs={{0,252},{1,253},{2,254},{3,255},{4,8},{5,9},{6,10},{7,11},{8,4},{9... | collective-permute-start | bytes 196616 | tf_op jit(solution)/shard_map/ppermute | solution.py:34
  67.2 3.0 %collective-permute-start.11 = (bf16[2,10,4,32,128]{4,3,2,1,0:T(8,128)(2,1)}, bf16[2,10,4,32,128]{4,3,2,1,0:T(8,128)(2,1)}, u32[]{:S(2)}, u32[]{:S(2)}) collective-permute-start(bf16[2,10,4,32,128]{4,3,2,1,0:T(8,128)(2,1)} %collective-permute-done.6), channel_id=1, source_target_pairs={{0,2},{1,3},{62,60},{63,61},{64,66},{65,67},{126,124},{127,125},{1... | collective-permute-start | bytes 1966088 | tf_op jit(solution)/shard_map/ppermute | solution.py:34
  70.2 9.6 %collective-permute-done.7 = f32[4,32,128]{2,1,0:T(8,128)S(1)} collective-permute-done((f32[4,32,128]{2,1,0:T(8,128)S(1)}, f32[4,32,128]{2,1,0:T(8,128)S(1)}, u32[]{:S(2)}, u32[]{:S(2)}) %collective-permute-start.7) | collective-permute-done | bytes 65568 | tf_op jit(solution)/shard_map/ppermute | solution.py:34
  82.8 2.5 %collective-permute-start.13 = (bf16[2,10,4,32,128]{4,3,2,1,0:T(8,128)(2,1)}, bf16[2,10,4,32,128]{4,3,2,1,0:T(8,128)(2,1)}, u32[]{:S(2)}, u32[]{:S(2)}) collective-permute-start(bf16[2,10,4,32,128]{4,3,2,1,0:T(8,128)(2,1)} %pad_maximum_fusion.4), channel_id=1, source_target_pairs={{0,252},{1,253},{62,66},{63,67},{64,60},{65,61},{126,130},{127,131... | collective-permute-start | bytes 1966088 | tf_op jit(solution)/shard_map/ppermute | solution.py:34
  85.2 4.1 %collective-permute-start.12 = (bf16[2,10,4,32,128]{4,3,2,1,0:T(8,128)(2,1)}, bf16[2,10,4,32,128]{4,3,2,1,0:T(8,128)(2,1)}, u32[]{:S(2)}, u32[]{:S(2)}) collective-permute-start(bf16[2,10,4,32,128]{4,3,2,1,0:T(8,128)(2,1)} %pad_maximum_fusion.4), channel_id=1, source_target_pairs={{0,254},{1,255},{4,8},{5,9},{6,10},{7,11},{8,4},{9,5},{10,6},{11,7... | collective-permute-start | bytes 1966088 | tf_op jit(solution)/shard_map/ppermute | solution.py:34
  89.7 7.0 %inner.1 = f32[4,12,32,128]{3,2,1,0:T(8,128)S(1)} custom-call(bf16[10,12,32,128]{3,2,1,0:T(8,128)(2,1)S(1)} %get-tuple-element.41.refs_0_.e0_ref, bf16[10,12,32,128]{3,2,1,0:T(8,128)(2,1)} %collective-permute-done.refs_1_.e1_ref, bf16[10,12,32,128]{3,2,1,0:T(8,128)(2,1)} %collective-permute-done.1.refs_2_.e2_ref, ...), custom_call_target="tpu_custom_call" | custom-call | flops 1 | bytes 1 | tf_op jit(solution)/shard_map/inner/pallas_call | solution.py:297
  96.7 16.2 %collective-permute-done.12 = bf16[2,10,4,32,128]{4,3,2,1,0:T(8,128)(2,1)} collective-permute-done((bf16[2,10,4,32,128]{4,3,2,1,0:T(8,128)(2,1)}, bf16[2,10,4,32,128]{4,3,2,1,0:T(8,128)(2,1)}, u32[]{:S(2)}, u32[]{:S(2)}) %collective-permute-start.12) | collective-permute-done | bytes 655392 | tf_op jit(solution)/shard_map/ppermute | solution.py:34
  112.9 1.9 %broadcast_select_fusion.2 = (bf16[2,10,4,32,128]{4,3,2,1,0:T(8,128)(2,1)S(1)}, bf16[2,10,4,32,128]{4,3,2,1,0:T(8,128)(2,1)S(1)}, bf16[2,10,4,32,128]{4,3,2,1,0:T(8,128)(2,1)S(1)}, bf16[2,10,4,32,128]{4,3,2,1,0:T(8,128)(2,1)S(1)}) fusion(bf16[2,10,4,32,128]{4,3,2,1,0:T(8,128)(2,1)} %collective-permute-done.14, pred[]{:T(512)S(6)} %eq.27, ...), kind=kLoop, calls=%fused_computation.10 | loop fusion | flops 1966080 | bytes 6553603 | tf_op jit(solution)/shard_map/jit(_where)/select_n | solution.py:478
  115.0 5.5 %edges.1 = f32[4,8,32,128]{3,2,1,0:T(8,128)S(1)} custom-call(bf16[2,10,4,32,128]{4,3,2,1,0:T(8,128)(2,1)S(1)} %get-tuple-element.74.refs_0_, bf16[2,10,4,32,128]{4,3,2,1,0:T(8,128)(2,1)S(1)} %get-tuple-element.73.refs_1_, bf16[2,10,4,32,128]{4,3,2,1,0:T(8,128)(2,1)S(1)} %get-tuple-element.42.refs_2_, ...), custom_call_target="tpu_custom_call" | custom-call | flops 1 | bytes 1 | tf_op jit(solution)/shard_map/edges/pallas_call | solution.py:297
  120.5 3.8 %collective-permute-start.15 = (f32[2,8,32,128]{3,2,1,0:T(8,128)S(1)}, f32[2,8,32,128]{3,2,1,0:T(8,128)S(1)}, u32[]{:S(2)}, u32[]{:S(2)}) collective-permute-start(f32[2,8,32,128]{3,2,1,0:T(8,128)S(1)} %slice.127), channel_id=1, source_target_pairs={{0,1},{1,0},{2,3},{3,2},{4,5},{5,4},{6,7},{7,6},{8,9},{9,8},{10,11... | collective-permute-start | bytes 786440 | tf_op jit(solution)/shard_map/ppermute | solution.py:34
  126.7 1.9 %copy-done.2 = f32[20,32,12,128]{3,1,2,0:T(8,128)S(1)} copy-done((f32[20,32,12,128]{3,1,2,0:T(8,128)S(1)}, f32[20,32,12,128]{3,1,2,0:T(8,128)}, u32[]{:S(2)}) %copy-start.2) | copy-done | bytes 3932184
  128.7 9.7 %adjoint.2 = (f32[20,12,32,128]{3,2,1,0:T(8,128)}, f32[6,12,32,128]{3,2,1,0:T(8,128)S(1)}) custom-call(s32[1]{0:T(128)} %bitcast.10._core, bf16[10,12,32,128]{3,2,1,0:T(8,128)(2,1)S(1)} %get-tuple-element.41.refs_0_.e0_ref, bf16[10,12,32,128]{3,2,1,0:T(8,128)(2,1)} %collective-permute-done.refs_1_.e1_ref, ...), custom_call_target="tpu_custom_call" | custom-call | flops 1 | bytes 1 | tf_op jit(solution)/shard_map/adjoint/pallas_call | solution.py:355
  138.7 7.1 %adjoint.3 = (f32[20,12,32,128]{3,2,1,0:T(8,128)}, f32[4,12,32,128]{3,2,1,0:T(8,128)S(1)}) custom-call(s32[1]{0:T(128)} %bitcast.10._core, bf16[10,12,32,128]{3,2,1,0:T(8,128)(2,1)S(1)} %get-tuple-element.41.refs_0_.e0_ref, bf16[10,12,32,128]{3,2,1,0:T(8,128)(2,1)} %collective-permute-done.refs_1_.e1_ref, ...), custom_call_target="tpu_custom_call", output_to_operand_aliasing={{0}: (15, {})} | custom-call | flops 1 | bytes 1 | tf_op jit(solution)/shard_map/adjoint/pallas_call | solution.py:355
  146.2 6.1 %collective-permute-start.18 = (f32[12,32,128]{2,1,0:T(8,128)S(1)}, f32[12,32,128]{2,1,0:T(8,128)S(1)}, u32[]{:S(2)}, u32[]{:S(2)}) collective-permute-start(f32[12,32,128]{2,1,0:T(8,128)S(1)} %slice_bitcast_fusion), channel_id=1, source_target_pairs={{0,2},{1,3},{2,0},{3,1},{4,6},{5,7},{6,4},{7,5},{8,10},{9,11},{10,... | collective-permute-start | bytes 589832 | tf_op jit(solution)/shard_map/ppermute | solution.py:34
  152.2 4.8 %collective-permute-done.18 = f32[12,32,128]{2,1,0:T(8,128)S(1)} collective-permute-done((f32[12,32,128]{2,1,0:T(8,128)S(1)}, f32[12,32,128]{2,1,0:T(8,128)S(1)}, u32[]{:S(2)}, u32[]{:S(2)}) %collective-permute-start.18) | collective-permute-done | bytes 196640 | tf_op jit(solution)/shard_map/ppermute | solution.py:34
  (93 shorter events, 26.3 us)
Async XLA Ops:
  1.4 18.6 %collective-permute-start.3 = (f32[4,128]{1,0:T(4,128)S(1)}, f32[4,128]{1,0:T(4,128)S(1)}, u32[]{:S(2)}, u32[]{:S(2)}) collective-permute-start(f32[4,128]{1,0:T(4,128)S(1)} %get-tuple-element.65), channel_id=1, source_target_pairs={{0,252},{1,253},{2,254},{3,255},{4,8},{5,9},{6,10},{7,11},{8,4},{9... | collective-permute-start | bytes 6152 | tf_op jit(solution)/shard_map/ppermute | solution.py:34
  12.8 7.2 %collective-permute-start.4 = (f32[4,128]{1,0:T(4,128)S(1)}, f32[4,128]{1,0:T(4,128)S(1)}, u32[]{:S(2)}, u32[]{:S(2)}) collective-permute-start(f32[4,128]{1,0:T(4,128)S(1)} %get-tuple-element.66), channel_id=1, source_target_pairs={{0,4},{1,5},{2,6},{3,7},{4,0},{5,1},{6,2},{7,3},{8,12},{9,13},{10,... | collective-permute-start | bytes 6152 | tf_op jit(solution)/shard_map/ppermute | solution.py:34
  14.5 5.6 %collective-permute-start = (bf16[10,12,32,128]{3,2,1,0:T(8,128)(2,1)S(1)}, bf16[10,12,32,128]{3,2,1,0:T(8,128)(2,1)}, u32[]{:S(2)}, u32[]{:S(2)}) collective-permute-start(bf16[10,12,32,128]{3,2,1,0:T(8,128)(2,1)S(1)} %get-tuple-element.40), channel_id=1, source_target_pairs={{0,1},{1,0},{2,3},{3,2},{4,5},{5,4},{6,7},{7,6},{8,9},{9,8},{10,11... | collective-permute-start | bytes 2949128 | tf_op jit(solution)/shard_map/ppermute | solution.py:34
  15.6 41.3 %collective-permute-start.1 = (bf16[10,12,32,128]{3,2,1,0:T(8,128)(2,1)S(1)}, bf16[10,12,32,128]{3,2,1,0:T(8,128)(2,1)}, u32[]{:S(2)}, u32[]{:S(2)}) collective-permute-start(bf16[10,12,32,128]{3,2,1,0:T(8,128)(2,1)S(1)} %get-tuple-element.41.refs_0_.e0_ref), channel_id=1, source_target_pairs={{0,2},{1,3},{2,0},{3,1},{4,6},{5,7},{6,4},{7,5},{8,10},{9,11},{10,... | collective-permute-start | bytes 2949128 | tf_op jit(solution)/shard_map/ppermute | solution.py:34
  31.3 48.5 %collective-permute-start.9 = (bf16[10,20,32,128]{3,2,1,0:T(8,128)(2,1)}, bf16[10,20,32,128]{3,2,1,0:T(8,128)(2,1)}, u32[]{:S(2)}, u32[]{:S(2)}) collective-permute-start(bf16[10,20,32,128]{3,2,1,0:T(8,128)(2,1)} %smooth.2), channel_id=1, source_target_pairs={{0,1},{1,0},{2,3},{3,2},{4,5},{5,4},{6,7},{7,6},{8,9},{9,8},{10,11... | collective-permute-start | bytes 4915208 | tf_op jit(solution)/shard_map/ppermute | solution.py:34
  31.6 25.2 %collective-permute-start.5 = (bf16[2,10,4,32,128]{4,3,2,1,0:T(8,128)(2,1)}, bf16[2,10,4,32,128]{4,3,2,1,0:T(8,128)(2,1)}, u32[]{:S(2)}, u32[]{:S(2)}) collective-permute-start(bf16[2,10,4,32,128]{4,3,2,1,0:T(8,128)(2,1)} %pad_maximum_fusion.1), channel_id=1, source_target_pairs={{0,4},{1,5},{2,6},{3,7},{4,0},{5,1},{6,2},{7,3},{8,12},{9,13},{10,... | collective-permute-start | bytes 1966088 | tf_op jit(solution)/shard_map/ppermute | solution.py:34
  33.4 28.5 %collective-permute-start.6 = (bf16[2,10,4,32,128]{4,3,2,1,0:T(8,128)(2,1)}, bf16[2,10,4,32,128]{4,3,2,1,0:T(8,128)(2,1)}, u32[]{:S(2)}, u32[]{:S(2)}) collective-permute-start(bf16[2,10,4,32,128]{4,3,2,1,0:T(8,128)(2,1)} %pad_maximum_fusion.2), channel_id=1, source_target_pairs={{0,254},{1,255},{4,8},{5,9},{6,10},{7,11},{8,4},{9,5},{10,6},{11,7... | collective-permute-start | bytes 1966088 | tf_op jit(solution)/shard_map/ppermute | solution.py:34
  36.2 20.7 %all-to-all-start = ((f32[64,1,1152]{2,1,0:T(1,128)}), f32[64,1,1152]{2,1,0:T(1,128)S(1)}, u32[]{:S(2)}, u32[]{:S(2)}) async-start(f32[64,1,1152]{2,1,0:T(1,128)} %bitcast.9), calls=%async_computation | async-start | bytes 589824 | tf_op jit(solution)/shard_map/all_to_all | solution.py:448
  42.2 37.6 %collective-permute-start.2 = (bf16[10,12,32,128]{3,2,1,0:T(8,128)(2,1)}, bf16[10,12,32,128]{3,2,1,0:T(8,128)(2,1)}, u32[]{:S(2)}, u32[]{:S(2)}) collective-permute-start(bf16[10,12,32,128]{3,2,1,0:T(8,128)(2,1)} %collective-permute-done.refs_1_.e1_ref), channel_id=1, source_target_pairs={{0,2},{1,3},{2,0},{3,1},{4,6},{5,7},{6,4},{7,5},{8,10},{9,11},{10,... | collective-permute-start | bytes 2949128 | tf_op jit(solution)/shard_map/ppermute | solution.py:34
  63.3 16.4 %collective-permute-start.7 = (f32[4,32,128]{2,1,0:T(8,128)S(1)}, f32[4,32,128]{2,1,0:T(8,128)S(1)}, u32[]{:S(2)}, u32[]{:S(2)}) collective-permute-start(f32[4,32,128]{2,1,0:T(8,128)S(1)} %get-tuple-element.61), channel_id=1, source_target_pairs={{0,252},{1,253},{2,254},{3,255},{4,8},{5,9},{6,10},{7,11},{8,4},{9... | collective-permute-start | bytes 196616 | tf_op jit(solution)/shard_map/ppermute | solution.py:34
  66.0 13.7 %collective-permute-start.8 = (f32[4,32,128]{2,1,0:T(8,128)S(1)}, f32[4,32,128]{2,1,0:T(8,128)S(1)}, u32[]{:S(2)}, u32[]{:S(2)}) collective-permute-start(f32[4,32,128]{2,1,0:T(8,128)S(1)} %get-tuple-element.62), channel_id=1, source_target_pairs={{0,4},{1,5},{2,6},{3,7},{4,0},{5,1},{6,2},{7,3},{8,12},{9,13},{10,... | collective-permute-start | bytes 196616 | tf_op jit(solution)/shard_map/ppermute | solution.py:34
  67.2 29.5 %collective-permute-start.11 = (bf16[2,10,4,32,128]{4,3,2,1,0:T(8,128)(2,1)}, bf16[2,10,4,32,128]{4,3,2,1,0:T(8,128)(2,1)}, u32[]{:S(2)}, u32[]{:S(2)}) collective-permute-start(bf16[2,10,4,32,128]{4,3,2,1,0:T(8,128)(2,1)} %collective-permute-done.6), channel_id=1, source_target_pairs={{0,2},{1,3},{62,60},{63,61},{64,66},{65,67},{126,124},{127,125},{1... | collective-permute-start | bytes 1966088 | tf_op jit(solution)/shard_map/ppermute | solution.py:34
  81.9 14.8 %collective-permute-start.14 = (bf16[2,10,4,32,128]{4,3,2,1,0:T(8,128)(2,1)}, bf16[2,10,4,32,128]{4,3,2,1,0:T(8,128)(2,1)}, u32[]{:S(2)}, u32[]{:S(2)}) collective-permute-start(bf16[2,10,4,32,128]{4,3,2,1,0:T(8,128)(2,1)} %pad_maximum_fusion.3), channel_id=1, source_target_pairs={{0,4},{1,5},{2,6},{3,7},{4,0},{5,1},{6,2},{7,3},{8,12},{9,13},{10,... | collective-permute-start | bytes 1966088 | tf_op jit(solution)/shard_map/ppermute | solution.py:34
  82.8 13.9 %collective-permute-start.13 = (bf16[2,10,4,32,128]{4,3,2,1,0:T(8,128)(2,1)}, bf16[2,10,4,32,128]{4,3,2,1,0:T(8,128)(2,1)}, u32[]{:S(2)}, u32[]{:S(2)}) collective-permute-start(bf16[2,10,4,32,128]{4,3,2,1,0:T(8,128)(2,1)} %pad_maximum_fusion.4), channel_id=1, source_target_pairs={{0,252},{1,253},{62,66},{63,67},{64,60},{65,61},{126,130},{127,131... | collective-permute-start | bytes 1966088 | tf_op jit(solution)/shard_map/ppermute | solution.py:34
  85.2 27.7 %collective-permute-start.12 = (bf16[2,10,4,32,128]{4,3,2,1,0:T(8,128)(2,1)}, bf16[2,10,4,32,128]{4,3,2,1,0:T(8,128)(2,1)}, u32[]{:S(2)}, u32[]{:S(2)}) collective-permute-start(bf16[2,10,4,32,128]{4,3,2,1,0:T(8,128)(2,1)} %pad_maximum_fusion.4), channel_id=1, source_target_pairs={{0,254},{1,255},{4,8},{5,9},{6,10},{7,11},{8,4},{9,5},{10,6},{11,7... | collective-permute-start | bytes 1966088 | tf_op jit(solution)/shard_map/ppermute | solution.py:34
  89.4 34.9 %collective-permute-start.19 = (f32[20,32,128]{2,1,0:T(8,128)S(1)}, f32[20,32,128]{2,1,0:T(8,128)S(1)}, u32[]{:S(2)}, u32[]{:S(2)}) collective-permute-start(f32[20,32,128]{2,1,0:T(8,128)S(1)} %get-tuple-element.58), channel_id=1, source_target_pairs={{0,2},{1,3},{2,0},{3,1},{4,6},{5,7},{6,4},{7,5},{8,10},{9,11},{10,... | collective-permute-start | bytes 983048 | tf_op jit(solution)/shard_map/ppermute | solution.py:34
  120.5 5.0 %collective-permute-start.15 = (f32[2,8,32,128]{3,2,1,0:T(8,128)S(1)}, f32[2,8,32,128]{3,2,1,0:T(8,128)S(1)}, u32[]{:S(2)}, u32[]{:S(2)}) collective-permute-start(f32[2,8,32,128]{3,2,1,0:T(8,128)S(1)} %slice.127), channel_id=1, source_target_pairs={{0,1},{1,0},{2,3},{3,2},{4,5},{5,4},{6,7},{7,6},{8,9},{9,8},{10,11... | collective-permute-start | bytes 786440 | tf_op jit(solution)/shard_map/ppermute | solution.py:34
  124.4 2.2 %collective-permute-start.20 = (f32[2,20,32,128]{3,2,1,0:T(8,128)S(1)}, f32[2,20,32,128]{3,2,1,0:T(8,128)S(1)}, u32[]{:S(2)}, u32[]{:S(2)}) collective-permute-start(f32[2,20,32,128]{3,2,1,0:T(8,128)S(1)} %pad_maximum_fusion.5), channel_id=1, source_target_pairs={{0,1},{1,0},{2,3},{3,2},{4,5},{5,4},{6,7},{7,6},{8,9},{9,8},{10,11... | collective-permute-start | bytes 1966088 | tf_op jit(solution)/shard_map/ppermute | solution.py:34
  124.5 14.1 %collective-permute-start.10 = (f32[2,12,32,128]{3,2,1,0:T(8,128)S(1)}, f32[2,12,32,128]{3,2,1,0:T(8,128)S(1)}, u32[]{:S(2)}, u32[]{:S(2)}) collective-permute-start(f32[2,12,32,128]{3,2,1,0:T(8,128)S(1)} %slice.124), channel_id=1, source_target_pairs={{0,1},{1,0},{2,3},{3,2},{4,5},{5,4},{6,7},{7,6},{8,9},{9,8},{10,11... | collective-permute-start | bytes 1179656 | tf_op jit(solution)/shard_map/ppermute | solution.py:34
  125.5 20.5 %collective-permute-start.16 = (f32[2,4,32,128]{3,2,1,0:T(8,128)S(1)}, f32[2,4,32,128]{3,2,1,0:T(8,128)S(1)}, u32[]{:S(2)}, u32[]{:S(2)}) collective-permute-start(f32[2,4,32,128]{3,2,1,0:T(8,128)S(1)} %get-tuple-element.59), channel_id=1, source_target_pairs={{0,252},{1,253},{2,254},{3,255},{4,8},{5,9},{6,10},{7,11},{8,4},{9... | collective-permute-start | bytes 393224 | tf_op jit(solution)/shard_map/ppermute | solution.py:34
  125.6 20.4 %collective-permute-start.17 = (f32[2,4,32,128]{3,2,1,0:T(8,128)S(1)}, f32[2,4,32,128]{3,2,1,0:T(8,128)S(1)}, u32[]{:S(2)}, u32[]{:S(2)}) collective-permute-start(f32[2,4,32,128]{3,2,1,0:T(8,128)S(1)} %get-tuple-element.60), channel_id=1, source_target_pairs={{0,4},{1,5},{2,6},{3,7},{4,0},{5,1},{6,2},{7,3},{8,12},{9,13},{10,... | collective-permute-start | bytes 393224 | tf_op jit(solution)/shard_map/ppermute | solution.py:34
  138.4 19.4 %collective-permute-start.22 = (f32[6,12,32,128]{3,2,1,0:T(8,128)S(1)}, f32[6,12,32,128]{3,2,1,0:T(8,128)S(1)}, u32[]{:S(2)}, u32[]{:S(2)}) collective-permute-start(f32[6,12,32,128]{3,2,1,0:T(8,128)S(1)} %get-tuple-element.34), channel_id=1, source_target_pairs={{0,1},{1,0},{2,3},{3,2},{4,5},{5,4},{6,7},{7,6},{8,9},{9,8},{10,11... | collective-permute-start | bytes 3538952 | tf_op jit(solution)/shard_map/ppermute | solution.py:34
  145.8 13.6 %collective-permute-start.21 = (f32[4,12,32,128]{3,2,1,0:T(8,128)S(1)}, f32[4,12,32,128]{3,2,1,0:T(8,128)S(1)}, u32[]{:S(2)}, u32[]{:S(2)}) collective-permute-start(f32[4,12,32,128]{3,2,1,0:T(8,128)S(1)} %get-tuple-element.33), channel_id=1, source_target_pairs={{0,1},{1,0},{2,3},{3,2},{4,5},{5,4},{6,7},{7,6},{8,9},{9,8},{10,11... | collective-permute-start | bytes 2359304 | tf_op jit(solution)/shard_map/ppermute | solution.py:34
  146.2 10.9 %collective-permute-start.18 = (f32[12,32,128]{2,1,0:T(8,128)S(1)}, f32[12,32,128]{2,1,0:T(8,128)S(1)}, u32[]{:S(2)}, u32[]{:S(2)}) collective-permute-start(f32[12,32,128]{2,1,0:T(8,128)S(1)} %slice_bitcast_fusion), channel_id=1, source_target_pairs={{0,2},{1,3},{2,0},{3,1},{4,6},{5,7},{6,4},{7,5},{8,10},{9,11},{10,... | collective-permute-start | bytes 589832 | tf_op jit(solution)/shard_map/ppermute | solution.py:34
  (10 other events, 38.3 us)
